TPU v7x, 32 devices: a whole 2x2x4 slice. The times are simulated.
32 devices in a mesh: bx: 8 (over z, x), by: 2 (over y), cores: 2 (over core).
Axes of the slice: x: 2, y: 2, z: 4, core: 2. Of those that a mesh axis runs over, the one named last changes fastest.
Arguments:
- weights: float32 [16, 2, 2, 16, 16, 1024], P(('bx', 'cores'), 'by'), may hold values from -6 to 6
- speed_modes: float32 [4, 4], replicated, may hold values from -0.05 to 0.05
Outputs:
- radon_weights: float32 [16, 2, 2, 16, 16, 1024], P(('bx', 'cores'), 'by')
All inputs are finite; a program needn't handle non-finite values.
Results may differ from a plain program's by a relative error of at most 0.02.
Values sent between devices are 32-bit elements; how exact they have to be, the bound alone decides.
No kernel may reach another device: no remote copies, remote signals or barrier semaphores. Data moves between devices by JAX's collectives and lax.ppermute only.
A program may use at most 128 MiB of HBM per device.

v0:
```python
from functools import partial
import math

import jax
import jax.numpy as jnp
import numpy as np
from jax import lax
from jax.sharding import PartitionSpec as P

N = 8192
TGT = 32


def partner_2(value, axis, apart):
    mask = 2**apart
    pairs = [(source, source ^ mask) for source in range(lax.axis_size(axis))]
    return lax.ppermute(value, axis, pairs)


def cheb_nodes(degree):
    return np.cos(np.pi * (2 * np.arange(degree) + 1) / (2 * degree))


def lagrange_table(degree):
    points = cheb_nodes(degree)
    result = np.ones((degree, 2 * degree))
    for child_side in range(2):
        inside = (points + 2 * child_side - 1) / 2
        for node_row in range(degree):
            for node_other in range(degree):
                if node_other != node_row:
                    result[node_row, child_side * degree : (child_side + 1) * degree] *= (
                        inside - points[node_other]
                    ) / (points[node_row] - points[node_other])
    return result


def speed_of(speed_modes, target_one, target_two):
    mode_count = speed_modes.shape[0]
    frequencies = jnp.arange(mode_count).astype(jnp.float32) * math.pi
    along_one = jnp.cos(frequencies[:, None] * target_one[None, :])
    along_two = jnp.cos(frequencies[:, None] * target_two[None, :])
    blended = jnp.dot(
        speed_modes, along_two, preferred_element_type=jnp.float32, precision=lax.Precision.HIGHEST
    )
    return 1.0 + jnp.sum(blended * along_one, axis=0)


def rotation(target_one, target_two, speed_value, wave_one, wave_two):
    phase = (
        target_one * wave_one
        + target_two * wave_two
        + speed_value * jnp.sqrt(wave_one * wave_one + wave_two * wave_two)
    )
    phase = phase - jnp.floor(phase)
    angle = 2.0 * math.pi * phase
    return (jnp.cos(angle), jnp.sin(angle))


def node_phase(layout, speed_value, center, half_width, degree):
    target_one, target_two, merge_dim, centers, child_half, other_center, other_half = layout
    points = jnp.asarray(cheb_nodes(degree), jnp.float32)
    merged = center[None, :] + half_width * points[:, None]
    across = other_center[None, :] + other_half * points[:, None]
    if merge_dim == 0:
        return rotation(target_one, target_two, speed_value, merged[:, None, :], across[None, :, :])
    return rotation(target_one, target_two, speed_value, across[:, None, :], merged[None, :, :])


def merge_children(child_low, child_high, layout, speed_modes):
    target_one, target_two, merge_dim, centers, child_half, other_center, other_half = layout
    degree = child_low.shape[1]
    speed_value = speed_of(speed_modes, target_one, target_two)
    lagrange = jnp.asarray(lagrange_table(degree), jnp.float32)
    pieces = []
    for child, center in ((child_low, centers[0]), (child_high, centers[1])):
        cosine, sine_part = node_phase(layout, speed_value, center, child_half, degree)
        real_part = child[0] * cosine + child[1] * sine_part
        imag_part = child[1] * cosine - child[0] * sine_part
        pieces.append(jnp.stack([real_part, imag_part]))
    stacked = jnp.concatenate(pieces, axis=1 + merge_dim)
    if merge_dim == 0:
        blended = jnp.einsum("ij,rjks->riks", lagrange, stacked, precision=lax.Precision.HIGHEST)
    else:
        blended = jnp.einsum("kj,rijs->riks", lagrange, stacked, precision=lax.Precision.HIGHEST)
    cosine, sine_part = node_phase(layout, speed_value, centers[2], 2.0 * child_half, degree)
    return jnp.stack(
        [blended[0] * cosine - blended[1] * sine_part, blended[0] * sine_part + blended[1] * cosine]
    )


def reversed_bits(box_code, bit_count):
    result = jnp.zeros_like(box_code)
    for bit_place in range(bit_count):
        result = result + box_code // 2**bit_place % 2 * 2 ** (bit_count - 1 - bit_place)
    return result


def x_layout(level_index, box_code, targets, y_box, geometry):
    extent, side_count, src_x, src_y = geometry
    span_size = 2 ** (level_index + 1)
    row_index = targets // side_count * span_size + reversed_bits(box_code, level_index + 1)
    target_one = (row_index.astype(jnp.float32) + 0.5) / (side_count * span_size)
    target_two = ((targets % side_count).astype(jnp.float32) + 0.5) / side_count
    parent = (box_code // span_size).astype(jnp.float32)
    child_width = extent * 2**level_index / src_x
    low_center = -extent / 2 + (2.0 * parent + 0.5) * child_width
    high_center = low_center + child_width
    parent_center = -extent / 2 + (parent + 0.5) * (2.0 * child_width)
    other_center = jnp.zeros_like(target_one) + (
        -extent / 2 + (jnp.asarray(y_box).astype(jnp.float32) + 0.5) * (extent / src_y)
    )
    return (
        target_one,
        target_two,
        0,
        (low_center, high_center, parent_center),
        child_width / 2,
        other_center,
        extent / (2 * src_y),
    )


def y_layout(level_index, box_code, targets, x_code, x_bits, geometry):
    extent, side_count, src_x, src_y = geometry
    span_size = 2 ** (level_index + 1)
    col_index = targets % side_count * span_size + reversed_bits(box_code, level_index + 1)
    target_two = (col_index.astype(jnp.float32) + 0.5) / (side_count * span_size)
    row_index = targets // side_count * src_x + reversed_bits(x_code, x_bits)
    target_one = (row_index.astype(jnp.float32) + 0.5) / (side_count * src_x)
    parent = (box_code // span_size).astype(jnp.float32)
    child_width = extent * 2**level_index / src_y
    low_center = -extent / 2 + (2.0 * parent + 0.5) * child_width
    high_center = low_center + child_width
    parent_center = -extent / 2 + (parent + 0.5) * (2.0 * child_width)
    other_center = jnp.zeros_like(target_one)
    return (
        target_one,
        target_two,
        1,
        (low_center, high_center, parent_center),
        child_width / 2,
        other_center,
        extent / 2,
    )


def pair_level(current, partner, level_index, box_code, targets, layout_fn, speed_modes):
    own_bit = box_code // 2**level_index % 2
    child_low = jnp.where(own_bit == 0, current, partner)
    child_high = jnp.where(own_bit == 0, partner, current)
    box_codes = jnp.zeros_like(targets) + box_code
    return merge_children(
        child_low, child_high, layout_fn(level_index, box_codes, targets), speed_modes
    )


def on_device(weights, speed_modes):
    current = weights.reshape(weights.shape[2:])
    pair_count = current.shape[3]
    core_count = lax.axis_size("cores")
    src_x = lax.axis_size("bx") * core_count
    src_y = lax.axis_size("by")
    x_bits = src_x.bit_length() - 1
    y_bits = src_y.bit_length() - 1
    x_code = lax.axis_index("bx") * core_count + lax.axis_index("cores")
    y_box = lax.axis_index("by")
    geometry = (float(N), TGT, src_x, src_y)
    targets = jnp.arange(pair_count, dtype=jnp.int32)
    first_layout = partial(x_layout, y_box=y_box, geometry=geometry)
    second_layout = partial(y_layout, x_code=x_code, x_bits=x_bits, geometry=geometry)
    for level_index in range(x_bits):
        if level_index == 0:
            partner = partner_2(current, "cores", 0)
        else:
            partner = partner_2(current, "bx", level_index - 1)
        current = pair_level(
            current, partner, level_index, x_code, targets, first_layout, speed_modes
        )
    for level_index in range(y_bits):
        partner = partner_2(current, "by", level_index)
        current = pair_level(
            current, partner, level_index, y_box, targets, second_layout, speed_modes
        )
    return current.reshape(weights.shape)


def solution(mesh):
    return jax.shard_map(
        on_device,
        mesh=mesh,
        in_specs=(P(("bx", "cores"), "by", None, None, None, None), P()),
        out_specs=P(("bx", "cores"), "by", None, None, None, None),
        check_vma=False,
    )
```

profile of v0, /device:TPU:10, one launch (start us, length us, event | category | flops | bytes accessed | tf_op | source)
XLA Modules:
  0.0 344.5 jit_solution(14999793737579775875)
XLA Ops:
  0.0 4.3 %copy.37 = f32[1,1,2,16,16,1024]{5,3,4,2,1,0:T(8,128)} copy(f32[1,1,2,16,16,1024]{5,4,3,2,1,0:T(8,128)} %param.22) | data formatting | bytes 4194304 | tf_op args[0]
  5.3 3.5 %collective-permute-done = f32[2,16,16,1024]{3,1,2,0:T(8,128)} collective-permute-done((f32[2,16,16,1024]{3,1,2,0:T(8,128)}, f32[2,16,16,1024]{3,1,2,0:T(8,128)}, u32[]{:S(2)}, u32[]{:S(2)}) %collective-permute-start) | collective-permute-done | bytes 2097184 | tf_op jit(solution)/shard_map/ppermute | solution.py:17
  8.8 3.0 broadcast_select_fusion.1
  11.9 8.5 %multiply_add_fusion.14 = (f32[1,16,16,1024]{3,1,2,0:T(8,128)S(1)}, f32[1,16,16,1024]{3,1,2,0:T(8,128)S(1)}, f32[1,16,16,1024]{3,1,2,0:T(8,128)S(1)}, f32[1,16,16,1024]{3,1,2,0:T(8,128)S(1)}) fusion(f32[2,16,16,1024]{3,1,2,0:T(8,128)S(1)} %get-tuple-element.17, f32[16]{0:T(128)S(1)} %get-tuple-element.85, f32[16]{0:T(128)S(1)} %get-tuple-element.112, ...), kind=kLoop, calls=%fused_computation.137 | loop fusion | flops 6815744 | bytes 8589504 | tf_op jit(solution)/shard_map/add | solution.py:78
  20.4 2.5 fusion.43
  22.9 4.2 %multiply_subtract_fusion.12 = (f32[1,16,16,1024]{3,1,2,0:T(8,128)S(1)}, f32[1,16,16,1024]{3,1,2,0:T(8,128)S(1)}) fusion(f32[2,16,16,1024]{3,1,2,0:T(8,128)S(1)} %fusion.43, f32[16]{0:T(128)S(1)} %get-tuple-element.117, f32[16,1024]{1,0:T(8,128)S(1)} %get-tuple-element.72, f32[16]{0:T(128)S(1)} %get-tuple-element.85, f32[1024]{0:T(1024)S(1)} %broadcast_add_fusion.4, ...), kind=kLoop, calls=%fused_computation.129 | loop fusion | flops 3407872 | bytes 4329600 | tf_op jit(solution)/shard_map/sub | solution.py:88
  27.2 1.5 pad_maximum_fusion
  29.3 47.4 %collective-permute-done.1 = f32[2,16,16,1024]{3,1,2,0:T(8,128)} collective-permute-done((f32[2,16,16,1024]{3,1,2,0:T(8,128)}, f32[2,16,16,1024]{3,1,2,0:T(8,128)}, u32[]{:S(2)}, u32[]{:S(2)}) %collective-permute-start.1) | collective-permute-done | bytes 2097184 | tf_op jit(solution)/shard_map/ppermute | solution.py:17
  76.6 2.1 broadcast_select_fusion.3
  78.8 8.6 %multiply_add_fusion.11 = (f32[1,16,16,1024]{3,1,2,0:T(8,128)S(1)}, f32[1,16,16,1024]{3,1,2,0:T(8,128)S(1)}, f32[1,16,16,1024]{3,1,2,0:T(8,128)S(1)}, f32[1,16,16,1024]{3,1,2,0:T(8,128)S(1)}) fusion(f32[2,16,16,1024]{3,1,2,0:T(8,128)S(1)} %get-tuple-element.15, f32[16]{0:T(128)S(1)} %get-tuple-element.118, f32[1024]{0:T(1024)S(1)} %broadcast_add_fusion.3, ...), kind=kLoop, calls=%fused_computation.125 | loop fusion | flops 6815744 | bytes 8589504 | tf_op jit(solution)/shard_map/add | solution.py:78
  87.3 2.5 fusion.40
  89.8 4.2 %multiply_subtract_fusion.9 = (f32[1,16,16,1024]{3,1,2,0:T(8,128)S(1)}, f32[1,16,16,1024]{3,1,2,0:T(8,128)S(1)}) fusion(f32[2,16,16,1024]{3,1,2,0:T(8,128)S(1)} %fusion.40, f32[16]{0:T(128)S(1)} %get-tuple-element.94, f32[16,1024]{1,0:T(8,128)S(1)} %get-tuple-element.69, f32[1024]{0:T(1024)S(1)} %broadcast_add_fusion.3, f32[16]{0:T(128)S(1)} %get-tuple-element.85, ...), kind=kLoop, calls=%fused_computation.117 | loop fusion | flops 3407872 | bytes 4329600 | tf_op jit(solution)/shard_map/sub | solution.py:88
  94.1 1.5 pad_maximum_fusion.1
  96.1 46.6 %collective-permute-done.2 = f32[2,16,16,1024]{3,1,2,0:T(8,128)} collective-permute-done((f32[2,16,16,1024]{3,1,2,0:T(8,128)}, f32[2,16,16,1024]{3,1,2,0:T(8,128)}, u32[]{:S(2)}, u32[]{:S(2)}) %collective-permute-start.2) | collective-permute-done | bytes 2097184 | tf_op jit(solution)/shard_map/ppermute | solution.py:17
  142.7 2.1 broadcast_select_fusion.5
  144.8 8.8 %multiply_add_fusion.8 = (f32[1,16,16,1024]{3,1,2,0:T(8,128)S(1)}, f32[1,16,16,1024]{3,1,2,0:T(8,128)S(1)}, f32[1,16,16,1024]{3,1,2,0:T(8,128)S(1)}, f32[1,16,16,1024]{3,1,2,0:T(8,128)S(1)}) fusion(f32[2,16,16,1024]{3,1,2,0:T(8,128)S(1)} %get-tuple-element.13, f32[16]{0:T(128)S(1)} %get-tuple-element.93, f32[1024]{0:T(1024)S(1)} %broadcast_add_fusion.2, ...), kind=kLoop, calls=%fused_computation.113 | loop fusion | flops 6815744 | bytes 8589504 | tf_op jit(solution)/shard_map/add | solution.py:78
  153.6 2.5 fusion.37
  156.1 4.2 %multiply_subtract_fusion.6 = (f32[1,16,16,1024]{3,1,2,0:T(8,128)S(1)}, f32[1,16,16,1024]{3,1,2,0:T(8,128)S(1)}) fusion(f32[2,16,16,1024]{3,1,2,0:T(8,128)S(1)} %fusion.37, f32[16]{0:T(128)S(1)} %get-tuple-element.84, f32[16,1024]{1,0:T(8,128)S(1)} %get-tuple-element.66, f32[1024]{0:T(1024)S(1)} %broadcast_add_fusion.2, f32[16]{0:T(128)S(1)} %get-tuple-element.85, ...), kind=kLoop, calls=%fused_computation.105 | loop fusion | flops 3407872 | bytes 4329600 | tf_op jit(solution)/shard_map/sub | solution.py:88
  161.8 2.6 collective-permute-start.3
  164.5 88.5 %collective-permute-done.3 = f32[2,16,16,1024]{3,1,2,0:T(8,128)} collective-permute-done((f32[2,16,16,1024]{3,1,2,0:T(8,128)}, f32[2,16,16,1024]{3,1,2,0:T(8,128)}, u32[]{:S(2)}, u32[]{:S(2)}) %collective-permute-start.3) | collective-permute-done | bytes 2097184 | tf_op jit(solution)/shard_map/ppermute | solution.py:17
  253.0 2.1 broadcast_select_fusion.7
  255.1 8.5 %multiply_add_fusion.5 = (f32[1,16,16,1024]{3,1,2,0:T(8,128)S(1)}, f32[1,16,16,1024]{3,1,2,0:T(8,128)S(1)}, f32[1,16,16,1024]{3,1,2,0:T(8,128)S(1)}, f32[1,16,16,1024]{3,1,2,0:T(8,128)S(1)}) fusion(f32[2,16,16,1024]{3,1,2,0:T(8,128)S(1)} %get-tuple-element.11, f32[16]{0:T(128)S(1)} %get-tuple-element.83, f32[1024]{0:T(1024)S(1)} %broadcast_add_fusion.1, ...), kind=kLoop, calls=%fused_computation.101 | loop fusion | flops 6815744 | bytes 8589504 | tf_op jit(solution)/shard_map/add | solution.py:78
  263.6 2.5 fusion.34
  266.1 4.2 %multiply_subtract_fusion.3 = (f32[1,16,16,1024]{3,1,2,0:T(8,128)S(1)}, f32[1,16,16,1024]{3,1,2,0:T(8,128)S(1)}) fusion(f32[2,16,16,1024]{3,1,2,0:T(8,128)S(1)} %fusion.34, f32[16]{0:T(128)S(1)} %get-tuple-element.77, f32[16,1024]{1,0:T(8,128)S(1)} %get-tuple-element.64, f32[1024]{0:T(1024)S(1)} %broadcast_add_fusion.1, f32[16]{0:T(128)S(1)} %get-tuple-element.85, ...), kind=kLoop, calls=%fused_computation.93 | loop fusion | flops 3407872 | bytes 4329600 | tf_op jit(solution)/shard_map/sub | solution.py:88
  270.4 1.5 pad_maximum_fusion.3
  271.8 1.5 collective-permute-start.4
  273.9 45.8 %collective-permute-done.4 = f32[2,16,16,1024]{3,1,2,0:T(8,128)} collective-permute-done((f32[2,16,16,1024]{3,1,2,0:T(8,128)}, f32[2,16,16,1024]{3,1,2,0:T(8,128)}, u32[]{:S(2)}, u32[]{:S(2)}) %collective-permute-start.4) | collective-permute-done | bytes 2097184 | tf_op jit(solution)/shard_map/ppermute | solution.py:17
  319.7 2.1 broadcast_select_fusion.9
  321.9 8.7 %multiply_add_fusion.2 = (f32[1,16,16,1024]{3,1,2,0:T(8,128)S(1)}, f32[1,16,16,1024]{3,1,2,0:T(8,128)S(1)}, f32[1,16,16,1024]{3,1,2,0:T(8,128)S(1)}, f32[1,16,16,1024]{3,1,2,0:T(8,128)S(1)}) fusion(f32[2,16,16,1024]{3,1,2,0:T(8,128)S(1)} %get-tuple-element.9, f32[16]{0:T(128)S(1)} %get-tuple-element.81, f32[16]{0:T(128)S(1)} %copy-done.3, ...), kind=kLoop, calls=%fused_computation.89 | loop fusion | flops 6815744 | bytes 8589504 | tf_op jit(solution)/shard_map/add | solution.py:78
  331.1 4.9 %fusion.32 = f32[2,16,1024,16]{2,3,1,0:T(8,128)S(1)} fusion(f32[16,32,1,1]{1,0,3,2:T(8,128)S(1)} %copy-done.2, f32[2,16,32,1024]{3,1,2,0:T(8,128)S(1)} %maximum_maximum_fusion), kind=kOutput, calls=%fused_computation.33 | convolution fusion | flops 201326592 | bytes 6293504 | tf_op jit(solution)/shard_map/kj,rijs->riks/dot_general | solution.py:85
  337.2 4.2 %multiply_subtract_fusion = (f32[1,16,16,1024]{3,1,2,0:T(8,128)S(1)}, f32[1,16,16,1024]{3,1,2,0:T(8,128)S(1)}) fusion(f32[2,16,16,1024]{3,1,2,0:T(8,128)S(1)} %bitcast.38, f32[16]{0:T(128)S(1)} %get-tuple-element.76, f32[16,1024]{1,0:T(8,128)S(1)} %get-tuple-element.59, f32[16]{0:T(128)S(1)} %copy-done.3, f32[1024]{0:T(1024)S(1)} %broadcast_add_fusion, ...), kind=kLoop, calls=%fused_computation.81 | loop fusion | flops 3407872 | bytes 4329600 | tf_op jit(solution)/shard_map/sub | solution.py:88
  341.7 2.5 copy.26
  (46 shorter events, 6.2 us)
Async XLA Ops:
  0.0 4.4 %copy-start = (f32[4,4]{1,0:T(4,128)S(1)}, f32[4,4]{1,0:T(4,128)}, u32[]{:S(2)}) copy-start(f32[4,4]{1,0:T(4,128)} %param.23) | copy-start | bytes 196
  0.0 5.1 %copy-start.5 = (f32[16]{0:T(128)S(1)}, f32[16]{0:T(128)}, u32[]{:S(2)}) copy-start(f32[16]{0:T(128)} %constant.348) | copy-start | bytes 196
  0.0 5.1 %copy-start.6 = (f32[16]{0:T(128)S(1)}, f32[16]{0:T(128)}, u32[]{:S(2)}) copy-start(f32[16]{0:T(128)} %constant.349) | copy-start | bytes 196
  0.0 5.1 %copy-start.7 = (f32[16]{0:T(128)S(1)}, f32[16]{0:T(128)}, u32[]{:S(2)}) copy-start(f32[16]{0:T(128)} %constant.346) | copy-start | bytes 196
  0.0 5.1 %copy-start.8 = (f32[16]{0:T(128)S(1)}, f32[16]{0:T(128)}, u32[]{:S(2)}) copy-start(f32[16]{0:T(128)} %constant.347) | copy-start | bytes 196
  0.0 8.8 %copy-start.1 = (f32[1,1,2,16,16,1024]{5,4,3,2,1,0:T(8,128)S(1)}, f32[1,1,2,16,16,1024]{5,4,3,2,1,0:T(8,128)}, u32[]{:S(2)}) copy-start(f32[1,1,2,16,16,1024]{5,4,3,2,1,0:T(8,128)} %param.22) | copy-start | bytes 6291460
  4.3 4.5 %collective-permute-start = (f32[2,16,16,1024]{3,1,2,0:T(8,128)}, f32[2,16,16,1024]{3,1,2,0:T(8,128)}, u32[]{:S(2)}, u32[]{:S(2)}) collective-permute-start(f32[2,16,16,1024]{3,1,2,0:T(8,128)} %bitcast.37), channel_id=1, source_target_pairs={{0,1},{1,0},{2,3},{3,2},{4,5},{5,4},{6,7},{7,6},{8,9},{9,8},{10,11... | collective-permute-start | bytes 6291464 | tf_op jit(solution)/shard_map/ppermute | solution.py:17
  11.9 8.5 %copy-start.2 = (f32[16,32,1,1]{1,0,3,2:T(8,128)S(1)}, f32[16,32,1,1]{1,0,3,2:T(8,128)}, u32[]{:S(2)}) copy-start(f32[16,32,1,1]{1,0,3,2:T(8,128)} %constant.354) | copy-start | bytes 6148
  28.6 48.0 %collective-permute-start.1 = (f32[2,16,16,1024]{3,1,2,0:T(8,128)}, f32[2,16,16,1024]{3,1,2,0:T(8,128)}, u32[]{:S(2)}, u32[]{:S(2)}) collective-permute-start(f32[2,16,16,1024]{3,1,2,0:T(8,128)} %pad_maximum_fusion), channel_id=1, source_target_pairs={{0,4},{4,0},{8,12},{12,8},{16,20},{20,16},{24,28},{28,24},{1,5},{5... | collective-permute-start | bytes 6291464 | tf_op jit(solution)/shard_map/ppermute | solution.py:17
  95.5 47.2 %collective-permute-start.2 = (f32[2,16,16,1024]{3,1,2,0:T(8,128)}, f32[2,16,16,1024]{3,1,2,0:T(8,128)}, u32[]{:S(2)}, u32[]{:S(2)}) collective-permute-start(f32[2,16,16,1024]{3,1,2,0:T(8,128)} %pad_maximum_fusion.1), channel_id=1, source_target_pairs={{0,8},{4,12},{8,0},{12,4},{16,24},{20,28},{24,16},{28,20},{1,9},{5... | collective-permute-start | bytes 6291464 | tf_op jit(solution)/shard_map/ppermute | solution.py:17
  160.3 4.1 %copy-start.4 = (f32[16]{0:T(128)S(1)}, f32[16]{0:T(128)}, u32[]{:S(2)}) copy-start(f32[16]{0:T(128)} %constant.350) | copy-start | bytes 196
  161.8 91.2 %collective-permute-start.3 = (f32[2,16,16,1024]{3,1,2,0:T(8,128)}, f32[2,16,16,1024]{3,1,2,0:T(8,128)}, u32[]{:S(2)}, u32[]{:S(2)}) collective-permute-start(f32[2,16,16,1024]{3,1,2,0:T(8,128)} %pad_maximum_fusion.2), channel_id=1, source_target_pairs={{0,16},{4,20},{8,24},{12,28},{16,0},{20,4},{24,8},{28,12},{1,17},{... | collective-permute-start | bytes 6291464 | tf_op jit(solution)/shard_map/ppermute | solution.py:17
  271.8 47.9 %collective-permute-start.4 = (f32[2,16,16,1024]{3,1,2,0:T(8,128)}, f32[2,16,16,1024]{3,1,2,0:T(8,128)}, u32[]{:S(2)}, u32[]{:S(2)}) collective-permute-start(f32[2,16,16,1024]{3,1,2,0:T(8,128)} %pad_maximum_fusion.3), channel_id=1, source_target_pairs={{0,2},{2,0},{1,3},{3,1},{4,6},{6,4},{5,7},{7,5},{8,10},{10,8},{9,1... | collective-permute-start | bytes 6291464 | tf_op jit(solution)/shard_map/ppermute | solution.py:17
  273.9 48.0 %copy-start.3 = (f32[16]{0:T(128)S(1)}, f32[16]{0:T(128)}, u32[]{:S(2)}) copy-start(f32[16]{0:T(128)} %constant.353) | copy-start | bytes 196
where the time goes:
time: 350 us; the launch traced here: 344 us
  waiting for transfers between devices  232 us (66%)
  other arithmetic  83 us (24%)
  matrix products  15.9 us (5%)
  local copies, waits for them, and re-layouts  8.09 us (2%)
  starting transfers between devices  5.11 us (1%)
    ppermute x5, waiting for transfers between devices, partner_2(): return lax.ppermute(value, axis, pairs)  232 us
    add x5, other arithmetic, merge_children(): real_part = child[0] * cosine + child[1] * sine_part  43 us
    sub x5, other arithmetic, merge_children(): blended[0] * cosine - blended[1] * sine_part  21.2 us
    select_n x5, other arithmetic, pair_level(): child_low = jnp.where(own_bit == 0, current, partner)  11.6 us
    dot_general x4, matrix products, merge_children(): jnp.einsum('ij,rjks->riks', lagrange, stacked, precision=lax.Precision.HI...  9.99 us
  transfers between devices with their start and end apart: 5, of which 5 were waited for; matrix products, arithmetic and copies ran while one was open for 0% of the time, Pallas kernels for 0%

commit v1 on v0

--- a/solution.py
+++ b/solution.py
@@ -5,6 +5,8 @@
 import jax.numpy as jnp
 import numpy as np
 from jax import lax
+from jax.experimental import pallas as pl
+from jax.experimental.pallas import tpu as pltpu
 from jax.sharding import PartitionSpec as P
 
 N = 8192
@@ -185,11 +187,443 @@
     return current.reshape(weights.shape)
 
 
+SIN_HALF = (4.442879586386342, -7.3078180422392816, 3.597788667381583, -0.7912380409231197)
+COS_HALF = (
+    1.4142134965636117,
+    -6.978850988059019,
+    5.739461167077472,
+    -1.883562964211867,
+    0.3106981455985473,
+)
+CHUNKS = 2
+PIECES = 16
+LEVEL_ROWS = (0, 256, 384, 448, 480)
+VMEM_LIMIT = 48 * 2**20
+
+
+def node_tables():
+    points = cheb_nodes(16).astype(np.float32)
+    nodes = []
+    for level_index in range(5):
+        width = np.float32(N * 2**level_index / 16)
+        for box in range(16 >> level_index):
+            center = np.float32(-N / 2 + (box + 0.5) * width)
+            nodes.append(center + (width / 2) * points)
+    nodes = np.concatenate(nodes).astype(np.float32)
+    sub = np.arange(8)
+    lane = np.arange(128)
+    half = (sub // 4)[:, None] + 0 * lane[None, :]
+    second = (lane // 32 * 4)[None, :] + (sub % 4)[:, None]
+    wave_two = (-N / 2 + (half + 0.5) * (N / 2)).astype(np.float32) + np.float32(N / 4) * points[second]
+    wave_two = wave_two.astype(np.float32)
+    lengths = np.sqrt(nodes[:, None, None] * nodes[:, None, None] + wave_two * wave_two)
+    return nodes, wave_two, lengths.astype(np.float32)
+
+
+def final_tables():
+    points = cheb_nodes(16).astype(np.float32) * np.float32(N / 2)
+    lane = np.arange(128)
+    one = np.broadcast_to(points.reshape(2, 8, 1), (2, 8, 128)).astype(np.float32)
+    two = np.stack([np.broadcast_to(points[lane // 32 * 4 + a], (8, 128)) for a in range(4)])
+    two = two.astype(np.float32)
+    lengths = np.sqrt((one * one)[:, None] + (two * two)[None, :]).astype(np.float32)
+    return np.array(one), two, lengths
+
+
+def second_weights():
+    table = lagrange_table(16)
+    result = np.zeros((8, 4, 32, 4, 4, 32), np.float32)
+    same = np.eye(32, dtype=np.float32)
+    for half in range(2):
+        for a in range(4):
+            for b in range(4):
+                for out_a in range(4):
+                    for out_b in range(4):
+                        weight = table[4 * out_b + out_a, half * 16 + 4 * b + a]
+                        result[half * 4 + a, b, :, out_a, out_b, :] = np.float32(weight) * same
+    return result.reshape(8, 128, 512)
+
+
+def folded_table():
+    table = lagrange_table(16)[:, :16]
+    even = (table[:8] + table[::-1][:8]) / 2
+    odd = (table[:8] - table[::-1][:8]) / 2
+    return even, odd
+
+
+def turn(phase):
+    part = phase - jnp.round(phase)
+    square = part * part
+    sine = SIN_HALF[3]
+    for coefficient in SIN_HALF[2::-1]:
+        sine = sine * square + coefficient
+    sine = sine * part
+    cosine = COS_HALF[4]
+    for coefficient in COS_HALF[3::-1]:
+        cosine = cosine * square + coefficient
+    return 1.0 - sine * sine, sine * cosine
+
+
+def swap_lanes(values):
+    lane = lax.broadcasted_iota(jnp.int32, (8, 128), 1)
+    low = lane < 64
+    even = lane // 32 % 2 == 0
+    half = [None] * 4
+    for b in range(2):
+        half[b] = jnp.where(low, values[b], pltpu.roll(values[b + 2], 64, 1))
+        half[b + 2] = jnp.where(low, pltpu.roll(values[b], 64, 1), values[b + 2])
+    full = [None] * 4
+    for j in (0, 2):
+        full[j] = jnp.where(even, half[j], pltpu.roll(half[j + 1], 32, 1))
+        full[j + 1] = jnp.where(even, pltpu.roll(half[j], 96, 1), half[j + 1])
+    return full
+
+
+def pack_kernel(in_ref, out_ref):
+    upper = lax.broadcasted_iota(jnp.int32, (8, 128), 0) < 4
+    for t1 in range(16):
+        groups = [None] * 4
+        for high in range(2):
+            real = in_ref[0, t1, 8 * high : 8 * high + 8, :]
+            imag = in_ref[1, t1, 8 * high : 8 * high + 8, :]
+            groups[2 * high] = jnp.where(upper, real, pltpu.roll(imag, 4, 0))
+            groups[2 * high + 1] = jnp.where(upper, pltpu.roll(real, 4, 0), imag)
+        for j, tile in enumerate(swap_lanes(groups)):
+            out_ref[j, t1] = tile
+
+
+def pack(weights, chunk):
+    return pl.pallas_call(
+        pack_kernel,
+        grid=(4,),
+        in_specs=[pl.BlockSpec((2, 16, 16, 128), lambda i: (0, 0, 0, 4 * chunk + i))],
+        out_specs=pl.BlockSpec((4, 16, 8, 128), lambda i: (i, 0, 0, 0)),
+        out_shape=jax.ShapeDtypeStruct((PIECES, 16, 8, 128), jnp.float32),
+        cost_estimate=pl.CostEstimate(flops=10**6, bytes_accessed=2**21, transcendentals=0),
+        name="pack",
+    )(weights)
+
+
+def join_kernel(in_ref, out_ref):
+    upper = lax.broadcasted_iota(jnp.int32, (8, 128), 0) < 4
+
+    def step(box, carry):
+        for t1 in range(16):
+            low = in_ref[2 * box, t1]
+            high = in_ref[2 * box + 1, t1]
+            out_ref[box, 0, t1] = jnp.where(upper, low, pltpu.roll(high, 4, 0))
+            out_ref[box, 1, t1] = jnp.where(upper, pltpu.roll(low, 4, 0), high)
+        return carry
+
+    lax.fori_loop(0, 8, step, 0)
+
+
+def join(received):
+    return pl.pallas_call(
+        join_kernel,
+        in_specs=[pl.BlockSpec(memory_space=pltpu.VMEM)],
+        out_specs=pl.BlockSpec(memory_space=pltpu.VMEM),
+        out_shape=jax.ShapeDtypeStruct((8, 2, 16, 8, 128), jnp.float32),
+        compiler_params=pltpu.CompilerParams(vmem_limit_bytes=VMEM_LIMIT),
+        cost_estimate=pl.CostEstimate(flops=10**6, bytes_accessed=2**21, transcendentals=0),
+        name="join",
+    )(received)
+
+
+def levels_kernel(
+    chunk, ids, nodes, own, other, speeds, waves, lengths, last_one, last_two, last_lengths,
+    weights, out, boxes_a, boxes_b, sums, turned, mixed,
+):
+    even, odd = folded_table()
+    row = (chunk * PIECES + ids[0]).astype(jnp.float32)
+    core = ids[1]
+    core_float = core.astype(jnp.float32)
+    wave_two = waves[...]
+    lane = lax.broadcasted_iota(jnp.int32, (8, 128), 1)
+    along_two = ((lane % 32).astype(jnp.float32) + 0.5) * (1.0 / 32)
+    second_phase = along_two * wave_two
+
+    def first_point(level_index, low_code):
+        span = 2.0 ** (level_index + 1)
+        code = core_float * 2.0**level_index + low_code
+        return (row * span + code + 0.5) * (1.0 / (32 * span))
+
+    def speed_row(level_index, low_code):
+        return jnp.broadcast_to(speeds[pl.ds(2**level_index - 1 + low_code, 1), :], (8, 128))
+
+    def blend(copies, target, boxes):
+        for i_half in range(2):
+            totals = {}
+            for parity, table in ((0, even), (1, odd)):
+                for j in range(16):
+                    piece = sums[parity, j, :copies]
+                    for i in range(4 * i_half, 4 * i_half + 4):
+                        term = piece * float(table[i, j])
+                        key = (parity, i)
+                        totals[key] = term if j == 0 else totals[key] + term
+            for i in range(4 * i_half, 4 * i_half + 4):
+                plus = totals[0, i] + totals[1, i]
+                minus = totals[0, i] - totals[1, i]
+                for n, box in enumerate(boxes):
+                    for part in range(2):
+                        target[box, part, i] = plus[2 * n + part]
+                        target[box, part, 15 - i] = minus[2 * n + part]
+
+    sign = 1.0 - 2.0 * core_float
+
+    def first_level(box, carry):
+        point = first_point(0, 0.0)
+        speed = speed_row(0, 0)
+        for j in range(16):
+            own_node = jnp.where(core == 0, j, 15 - j)
+            pieces = []
+            for source, node, box_code in (
+                (own, own_node, 2 * box + core),
+                (other, 15 - own_node, 2 * box + 1 - core),
+            ):
+                entry = box_code * 16 + node
+                phase = (point * nodes[entry] + second_phase) + speed * lengths[entry]
+                cosine, sine = turn(phase)
+                real = source[box, 0, node]
+                imag = source[box, 1, node]
+                pieces.append((real * cosine + imag * sine, imag * cosine - real * sine))
+            for part in range(2):
+                sums[0, j, part] = pieces[0][part] + pieces[1][part]
+                sums[1, j, part] = (pieces[0][part] - pieces[1][part]) * sign
+        blend(2, boxes_a, [box])
+        return carry
+
+    lax.fori_loop(0, 8, first_level, 0)
+
+    def later_level(level_index, source, target):
+        low_bits = level_index - 1
+        stride = 2**low_bits
+
+        def group(index, carry):
+            parent = index // stride
+            low = index % stride
+            code = 0
+            for bit in range(low_bits):
+                code = code + low // 2**bit % 2 * 2 ** (low_bits - 1 - bit)
+            code = jnp.int32(0) + code
+            before = first_point(level_index - 1, code.astype(jnp.float32))
+            before_speed = speed_row(level_index - 1, code)
+            points = [first_point(level_index, (2 * code + b).astype(jnp.float32)) for b in range(2)]
+            point_speeds = [speed_row(level_index, 2 * code + b) for b in range(2)]
+            first_box = parent * (2 * stride) + low
+            for j in range(16):
+                pieces = []
+                for child in range(2):
+                    node = j if child == 0 else 15 - j
+                    entry = LEVEL_ROWS[level_index] + (2 * parent + child) * 16 + node
+                    length = lengths[entry]
+                    wave = nodes[entry]
+                    real = source[first_box + child * stride, 0, node]
+                    imag = source[first_box + child * stride, 1, node]
+                    old = (before * wave + second_phase) + before_speed * length
+                    for b in range(2):
+                        new = (points[b] * wave + second_phase) + point_speeds[b] * length
+                        cosine, sine = turn(new - old)
+                        pieces.append((real * cosine + imag * sine, imag * cosine - real * sine))
+                for b in range(2):
+                    for part in range(2):
+                        sums[0, j, 2 * b + part] = pieces[b][part] + pieces[2 + b][part]
+                        sums[1, j, 2 * b + part] = pieces[b][part] - pieces[2 + b][part]
+            blend(4, target, [first_box, first_box + stride])
+            return carry
+
+        lax.fori_loop(0, 4, group, 0)
+
+    later_level(1, boxes_a, boxes_b)
+    later_level(2, boxes_b, boxes_a)
+    later_level(3, boxes_a, boxes_b)
+
+    fine_two = [((lane % 32).astype(jnp.float32) * 2.0 + (e + 0.5)) * (1.0 / 64) for e in range(2)]
+    fine_phase = [fine_two[e] * wave_two for e in range(2)]
+
+    def reversed_code(box):
+        return box % 2 * 4 + box // 2 % 2 * 2 + box // 4
+
+    def fine_speed(code, e):
+        return jnp.broadcast_to(speeds[pl.ds(15 + 2 * code + e, 1), :], (8, 128))
+
+    def rotate_box(box, carry):
+        code = reversed_code(box)
+        point = first_point(3, code.astype(jnp.float32))
+        old_speed = speed_row(3, code)
+        new_speeds = [fine_speed(code, e) for e in range(2)]
+        for t1 in range(16):
+            entry = LEVEL_ROWS[4] + t1
+            length = lengths[entry]
+            across = point * nodes[entry]
+            real = boxes_b[box, 0, t1]
+            imag = boxes_b[box, 1, t1]
+            old = (across + second_phase) + old_speed * length
+            for e in range(2):
+                new = (across + fine_phase[e]) + new_speeds[e] * length
+                cosine, sine = turn(new - old)
+                first = pl.multiple_of((box * 32 + t1) * 8, 8)
+                turned[e, pl.ds(first, 8), :] = real * cosine + imag * sine
+                turned[e, pl.ds(first + 128, 8), :] = imag * cosine - real * sine
+        return carry
+
+    lax.fori_loop(0, 8, rotate_box, 0)
+
+    for e in range(2):
+        total = None
+        for j in range(8):
+            rows = turned[e, pl.ds(j, 256, stride=8), :]
+            term = jnp.dot(
+                rows, weights[j], preferred_element_type=jnp.float32, precision=lax.Precision.HIGHEST
+            )
+            total = term if total is None else total + term
+        mixed[e] = total
+
+    last_phase = [[fine_two[e] * last_two[a] for a in range(4)] for e in range(2)]
+
+    def finish_box(box, carry):
+        code = reversed_code(box)
+        point = first_point(3, code.astype(jnp.float32))
+        for e in range(2):
+            speed = fine_speed(code, e)
+            for high in range(2):
+                across = point * last_one[high]
+                first = pl.multiple_of(box * 32 + high * 8, 8)
+                for a in range(4):
+                    phase = (across + last_phase[e][a]) + speed * last_lengths[high, a]
+                    cosine, sine = turn(phase)
+                    real = mixed[e, pl.ds(first, 8), 128 * a : 128 * a + 128]
+                    imag = mixed[e, pl.ds(first + 16, 8), 128 * a : 128 * a + 128]
+                    out[2 * box + e, high * 4 + a] = real * cosine - imag * sine
+                    out[2 * box + e, 8 + high * 4 + a] = real * sine + imag * cosine
+        return carry
+
+    lax.fori_loop(0, 8, finish_box, 0)
+
+
+def levels(chunk, ids, own, other, speeds):
+    nodes, waves, lengths = node_tables()
+    last_one, last_two, last_lengths = final_tables()
+    in_vmem = pl.BlockSpec(memory_space=pltpu.VMEM)
+    in_smem = pl.BlockSpec(memory_space=pltpu.SMEM)
+    return pl.pallas_call(
+        partial(levels_kernel, chunk),
+        in_specs=[in_smem, in_smem] + [in_vmem] * 9,
+        out_specs=in_vmem,
+        out_shape=jax.ShapeDtypeStruct((PIECES, 16, 8, 128), jnp.float32),
+        scratch_shapes=[
+            pltpu.VMEM((8, 2, 16, 8, 128), jnp.float32),
+            pltpu.VMEM((8, 2, 16, 8, 128), jnp.float32),
+            pltpu.VMEM((2, 16, 4, 8, 128), jnp.float32),
+            pltpu.VMEM((2, 2048, 128), jnp.float32),
+            pltpu.VMEM((2, 256, 512), jnp.float32),
+        ],
+        compiler_params=pltpu.CompilerParams(vmem_limit_bytes=VMEM_LIMIT),
+        cost_estimate=pl.CostEstimate(flops=10**8, bytes_accessed=2**23, transcendentals=0),
+        name="levels",
+    )(
+        ids, jnp.asarray(nodes), own, other, speeds, jnp.asarray(waves), jnp.asarray(lengths),
+        jnp.asarray(last_one), jnp.asarray(last_two), jnp.asarray(last_lengths),
+        jnp.asarray(second_weights()),
+    )
+
+
+def unpack_kernel(*refs):
+    in_ref, out_ref, rows = refs[0], refs[-2], refs[-1]
+    for part in range(2):
+        for high in range(2):
+            for a in range(4):
+                tiles = [in_ref[j, part * 8 + high * 4 + a] for j in range(4)]
+                for b, tile in enumerate(swap_lanes(tiles)):
+                    t2 = 4 * b + a
+                    rows[part * 2 + high, 8 * t2 : 8 * t2 + 8, :] = tile
+            for t1 in range(8):
+                out_ref[part, high * 8 + t1] = rows[part * 2 + high, pl.ds(t1, 16, stride=8), :]
+
+
+def unpack(received, chunk, earlier):
+    operands = [received]
+    in_specs = [pl.BlockSpec((4, 16, 8, 128), lambda i: (i, 0, 0, 0))]
+    aliases = {}
+    if earlier is not None:
+        operands.append(earlier)
+        in_specs.append(pl.BlockSpec(memory_space=pl.ANY))
+        aliases = {1: 0}
+    return pl.pallas_call(
+        unpack_kernel,
+        grid=(4,),
+        in_specs=in_specs,
+        out_specs=pl.BlockSpec((2, 16, 16, 128), lambda i: (0, 0, 0, 4 * chunk + i)),
+        out_shape=jax.ShapeDtypeStruct((2, 16, 16, 1024), jnp.float32),
+        scratch_shapes=[pltpu.VMEM((4, 128, 128), jnp.float32)],
+        input_output_aliases=aliases,
+        cost_estimate=pl.CostEstimate(flops=10**6, bytes_accessed=2**21, transcendentals=0),
+        name="unpack",
+    )(*operands)
+
+
+def speed_tables(speed_modes, core):
+    numerators, spans = [], []
+    for level_index in range(4):
+        for code in range(2**level_index):
+            numerators.append(core * 2**level_index + code)
+            spans.append(2 ** (level_index + 1))
+    for code in range(8):
+        for e in range(2):
+            numerators.append(core * 8 + code)
+            spans.append(16)
+    codes = jnp.stack(numerators).astype(jnp.float32)
+    spans = jnp.asarray(np.array(spans), jnp.float32)
+    me = lax.axis_index("bx") * 2 + lax.axis_index("by")
+    rows = (jnp.arange(CHUNKS) * PIECES + me).astype(jnp.float32)
+    target_one = (rows[:, None] * spans + codes + 0.5) / (TGT * spans)
+    columns = jnp.arange(32).astype(jnp.float32)
+    coarse = jnp.broadcast_to((columns + 0.5) / TGT, (15, 32))
+    fine = jnp.stack([(2 * columns + e + 0.5) / (2 * TGT) for e in range(2)])
+    target_two = jnp.concatenate([coarse, jnp.tile(fine, (8, 1))])
+    target_one = jnp.broadcast_to(target_one[:, :, None], (CHUNKS, 31, 32))
+    target_two = jnp.broadcast_to(target_two[None], (CHUNKS, 31, 32))
+    speed = speed_of(speed_modes, target_one.reshape(-1), target_two.reshape(-1))
+    return jnp.tile(speed.reshape(CHUNKS, 31, 32), (1, 1, 4))
+
+
+def on_device_dealt(weights, speed_modes):
+    local = weights.reshape(weights.shape[2:])
+    core = lax.axis_index("cores")
+    me = lax.axis_index("bx") * 2 + lax.axis_index("by")
+    ids = jnp.stack([me, core]).astype(jnp.int32)
+    speeds = speed_tables(speed_modes, core)
+    received = []
+    for chunk in range(CHUNKS):
+        received.append(deal(pack(local, chunk)))
+    results = []
+    for chunk in range(CHUNKS):
+        own = join(received[chunk])
+        other = partner_2(own, "cores", 0)
+        results.append(deal(levels(chunk, ids, own, other, speeds[chunk])))
+    out = None
+    for chunk in range(CHUNKS):
+        out = unpack(results[chunk], chunk, out)
+    return out.reshape(weights.shape)
+
+
+def deal(pieces):
+    return lax.all_to_all(pieces, ("bx", "by"), 0, 0, tiled=True)
+
+
 def solution(mesh):
-    return jax.shard_map(
-        on_device,
-        mesh=mesh,
-        in_specs=(P(("bx", "cores"), "by", None, None, None, None), P()),
-        out_specs=P(("bx", "cores"), "by", None, None, None, None),
-        check_vma=False,
-    )
+    sizes = dict(mesh.shape)
+    spec = P(("bx", "cores"), "by", None, None, None, None)
+    dealt = (sizes["bx"], sizes["by"], sizes["cores"]) == (8, 2, 2)
+
+    def whole(weights, speed_modes):
+        fits = dealt and weights.shape[2:] == (2, 16, 16, 1024)
+        return jax.shard_map(
+            on_device_dealt if fits else on_device,
+            mesh=mesh,
+            in_specs=(spec, P()),
+            out_specs=spec,
+            check_vma=False,
+        )(weights, speed_modes)
+
+    return whole

time: 350 us -> 138 us (0.39); the launches traced: 344 us -> 137 us
  waiting for transfers between devices: 232 us -> 49.5 us
  other arithmetic: 83 us -> 0.2 us
  Pallas kernels: 0 us -> 58 us
  starting transfers between devices: 5.11 us -> 24.4 us
  matrix products: 15.9 us -> 0.6 us
  local copies, waits for them, and re-layouts: 8.09 us -> 3.88 us
    ppermute x5 -> x2, waiting for transfers between devices: 232 us -> 4.06 us  [partner_2(): return lax.ppermute(value, axis, pairs)]
    pallas_call x0 -> x8, Pallas kernels: none -> 58 us  [the longest x2 41.1 us: levels(): pl.pallas_call(partial(levels_kernel, chunk), in_specs=[in_smem, in_smem]...]
    all_to_all x0 -> x4, waiting for transfers between devices: none -> 45.4 us  [deal(): return lax.all_to_all(pieces, ('bx', 'by'), 0, 0, tiled=True)]
    add x8 -> x0, other arithmetic: 43.1 us -> none  [the longest x5 43 us: merge_children(): real_part = child[0] * cosine + child[1] * sine_part]
    all_to_all x0 -> x4, starting transfers between devices: none -> 24.3 us  [deal(): return lax.all_to_all(pieces, ('bx', 'by'), 0, 0, tiled=True)]
    sub x5 -> x0, other arithmetic: 21.2 us -> none  [merge_children(): blended[0] * cosine - blended[1] * sine_part]
    dot_general x5 -> x0, matrix products: 14.9 us -> none  [the longest x4 9.99 us: merge_children(): jnp.einsum('ij,rjks->riks', lagrange, stacked, precision=lax.Precision.HI...]
    select_n x5 -> x0, other arithmetic: 11.6 us -> none  [pair_level(): child_low = jnp.where(own_bit == 0, current, partner)]
  transfers between devices with their start and end apart: 5 -> 6, of which waited for: 5 -> 5; matrix products, arithmetic and copies ran while one was open for 0% -> 1% of each run, Pallas kernels for 0% -> 37%
where the time goes in v1:
time: 138 us; the launch traced here: 137 us
  Pallas kernels  58 us (42%)
  waiting for transfers between devices  49.5 us (36%)
  starting transfers between devices  24.4 us (18%)
  local copies, waits for them, and re-layouts  3.88 us (3%)
    all_to_all x4, waiting for transfers between devices, deal(): return lax.all_to_all(pieces, ('bx', 'by'), 0, 0, tiled=True)  45.4 us
    pallas_call x2, Pallas kernels, levels(): pl.pallas_call(partial(levels_kernel, chunk), in_specs=[in_smem, in_smem]...  41.1 us
    all_to_all x4, starting transfers between devices, deal(): return lax.all_to_all(pieces, ('bx', 'by'), 0, 0, tiled=True)  24.3 us
    pallas_call x2, Pallas kernels, unpack(): pl.pallas_call(unpack_kernel, grid=(4,), in_specs=in_specs, out_specs=pl....  7.75 us
    pallas_call x2, Pallas kernels, pack(): pl.pallas_call(pack_kernel, grid=(4,), in_specs=[pl.BlockSpec((2, 16, 16,...  7.72 us
    ppermute x2, waiting for transfers between devices, partner_2(): return lax.ppermute(value, axis, pairs)  4.06 us
    unnamed x26, local copies, waits for them, and re-layouts  3.25 us
  transfers between devices with their start and end apart: 6, of which 5 were waited for; matrix products, arithmetic and copies ran while one was open for 1% of the time, Pallas kernels for 37%

profile of v1, /device:TPU:10, one launch (start us, length us, event | category | flops | bytes accessed | tf_op | source)
XLA Modules:
  0.0 136.8 jit_solution(14584647717399793180)
XLA Ops:
  0.0 3.9 %pack.3 = f32[16,16,8,128]{3,2,1,0:T(8,128)} custom-call(f32[2,16,16,1024]{3,2,1,0:T(8,128)} %bitcast.30), custom_call_target="tpu_custom_call" | custom-call | flops 1000000 | bytes 2097152 | tf_op jit(solution)/shard_map/pack/pallas_call | solution.py:296
  3.9 7.2 %all-to-all-start.2 = ((f32[16,16,8,128]{3,2,1,0:T(8,128)}), f32[16,16,8,128]{3,2,1,0:T(8,128)S(1)}, u32[]{:S(2)}, u32[]{:S(2)}) async-start(f32[16,16,8,128]{3,2,1,0:T(8,128)} %pack.3), calls=%async_computation.2 | async-start | bytes 2097152 | tf_op jit(solution)/shard_map/all_to_all | solution.py:611
  11.1 3.9 %pack.2 = f32[16,16,8,128]{3,2,1,0:T(8,128)} custom-call(f32[2,16,16,1024]{3,2,1,0:T(8,128)} %bitcast.31), custom_call_target="tpu_custom_call" | custom-call | flops 1000000 | bytes 2097152 | tf_op jit(solution)/shard_map/pack/pallas_call | solution.py:296
  15.0 22.0 %all-to-all-done.2.in_ref = f32[16,16,8,128]{3,2,1,0:T(8,128)S(1)} async-done(((f32[16,16,8,128]{3,2,1,0:T(8,128)}), f32[16,16,8,128]{3,2,1,0:T(8,128)S(1)}, u32[]{:S(2)}, u32[]{:S(2)}) %all-to-all-start.2) | async-done | bytes 1048608 | tf_op jit(solution)/shard_map/all_to_all | solution.py:611
  37.0 4.4 %all-to-all-start = ((f32[16,16,8,128]{3,2,1,0:T(8,128)}), f32[16,16,8,128]{3,2,1,0:T(8,128)}, u32[]{:S(2)}, u32[]{:S(2)}) async-start(f32[16,16,8,128]{3,2,1,0:T(8,128)} %pack.2), calls=%async_computation | async-start | bytes 2097152 | tf_op jit(solution)/shard_map/all_to_all | solution.py:611
  41.4 1.2 copy-done.4
  42.6 0.1 join.3.own
  42.8 0.1 collective-permute-start.1
  42.9 0.1 stack.94
  43.0 0.1 mul.130
  43.1 0.1 add_multiply_fusion
  43.2 0.1 broadcast_in_dim.8
  43.2 0.1 mul.141
  43.3 0.6 fusion.1
  43.9 0.1 add.152
  44.0 0.1 tile.26.speeds
  44.1 0.1 pad_add_fusion.ids
  44.2 1.4 %collective-permute-done.1.other = f32[8,2,16,8,128]{4,3,2,1,0:T(8,128)} collective-permute-done((f32[8,2,16,8,128]{4,3,2,1,0:T(8,128)S(1)}, f32[8,2,16,8,128]{4,3,2,1,0:T(8,128)}, u32[]{:S(2)}, u32[]{:S(2)}) %collective-permute-start.1) | collective-permute-done | bytes 1048608 | tf_op jit(solution)/shard_map/ppermute | solution.py:19
  45.7 20.0 %levels.3 = f32[16,16,8,128]{3,2,1,0:T(8,128)S(1)} custom-call(s32[2]{0:T(128)S(1)} %pad_add_fusion.ids, f32[496]{0:T(512)S(1)} %copy-done.9, f32[8,2,16,8,128]{4,3,2,1,0:T(8,128)S(1)} %join.3.own, f32[8,2,16,8,128]{4,3,2,1,0:T(8,128)} %collective-permute-done.1.other, f32[31,128]{1,0:T(8,128)S(1)} %tile.26.speeds, f32[8,128]{1,0:T(8,128)S(1)} %copy-done.8, ...), custom_call_target="tpu_custom_call" | custom-call | flops 100000000 | bytes 8388608 | tf_op jit(solution)/shard_map/levels/pallas_call | solution.py:509
  65.7 1.0 copy-done.2
  66.7 6.9 %all-to-all-start.3 = ((f32[16,16,8,128]{3,2,1,0:T(8,128)}), f32[16,16,8,128]{3,2,1,0:T(8,128)}, u32[]{:S(2)}, u32[]{:S(2)}) async-start(f32[16,16,8,128]{3,2,1,0:T(8,128)} %copy-done.2), calls=%async_computation.3 | async-start | bytes 2097152 | tf_op jit(solution)/shard_map/all_to_all | solution.py:611
  73.6 1.3 join.2.own
  74.9 0.1 collective-permute-start
  75.0 0.1 tile.24.speeds
  75.1 2.7 %collective-permute-done.other = f32[8,2,16,8,128]{4,3,2,1,0:T(8,128)} collective-permute-done((f32[8,2,16,8,128]{4,3,2,1,0:T(8,128)S(1)}, f32[8,2,16,8,128]{4,3,2,1,0:T(8,128)}, u32[]{:S(2)}, u32[]{:S(2)}) %collective-permute-start) | collective-permute-done | bytes 1048608 | tf_op jit(solution)/shard_map/ppermute | solution.py:19
  77.8 21.0 %levels.2 = f32[16,16,8,128]{3,2,1,0:T(8,128)} custom-call(s32[2]{0:T(128)S(1)} %pad_add_fusion.ids, f32[496]{0:T(512)S(1)} %copy-done.9, f32[8,2,16,8,128]{4,3,2,1,0:T(8,128)S(1)} %join.2.own, f32[8,2,16,8,128]{4,3,2,1,0:T(8,128)} %collective-permute-done.other, f32[31,128]{1,0:T(8,128)S(1)} %tile.24.speeds, f32[8,128]{1,0:T(8,128)S(1)} %copy-done.8, ...), custom_call_target="tpu_custom_call" | custom-call | flops 100000000 | bytes 8388608 | tf_op jit(solution)/shard_map/levels/pallas_call | solution.py:509
  98.8 1.1 all-to-all-done.3.refs_0_
  99.9 5.8 %all-to-all-start.1 = ((f32[16,16,8,128]{3,2,1,0:T(8,128)}), f32[16,16,8,128]{3,2,1,0:T(8,128)S(1)}, u32[]{:S(2)}, u32[]{:S(2)}) async-start(f32[16,16,8,128]{3,2,1,0:T(8,128)} %levels.2), calls=%async_computation.1 | async-start | bytes 2097152 | tf_op jit(solution)/shard_map/all_to_all | solution.py:611
  105.7 3.9 %unpack.2.refs_1_ = f32[2,16,16,1024]{3,2,1,0:T(8,128)} custom-call(f32[16,16,8,128]{3,2,1,0:T(8,128)} %all-to-all-done.3.refs_0_), custom_call_target="tpu_custom_call" | custom-call | flops 1000000 | bytes 2097152 | tf_op jit(solution)/shard_map/unpack/pallas_call | solution.py:552
  109.6 22.3 %all-to-all-done.1.refs_0_ = f32[16,16,8,128]{3,2,1,0:T(8,128)S(1)} async-done(((f32[16,16,8,128]{3,2,1,0:T(8,128)}), f32[16,16,8,128]{3,2,1,0:T(8,128)S(1)}, u32[]{:S(2)}, u32[]{:S(2)}) %all-to-all-start.1) | async-done | bytes 1048608 | tf_op jit(solution)/shard_map/all_to_all | solution.py:611
  132.0 1.0 copy-done.10
  133.0 3.9 %unpack.3 = f32[2,16,16,1024]{3,2,1,0:T(8,128)} custom-call(f32[16,16,8,128]{3,2,1,0:T(8,128)} %copy-done.10, f32[2,16,16,1024]{3,2,1,0:T(8,128)} %unpack.2.refs_1_), custom_call_target="tpu_custom_call", output_to_operand_aliasing={{}: (1, {})} | custom-call | flops 1000000 | bytes 2097152 | tf_op jit(solution)/shard_map/unpack/pallas_call | solution.py:552
  (38 shorter events, 0.2 us)
Async XLA Ops:
  0.0 43.3 %copy-start = (f32[4,4]{1,0:T(4,128)S(1)}, f32[4,4]{1,0:T(4,128)}, u32[]{:S(2)}) copy-start(f32[4,4]{1,0:T(4,128)} %param.18) | copy-start | bytes 196
  3.9 33.1 %all-to-all-start.2 = ((f32[16,16,8,128]{3,2,1,0:T(8,128)}), f32[16,16,8,128]{3,2,1,0:T(8,128)S(1)}, u32[]{:S(2)}, u32[]{:S(2)}) async-start(f32[16,16,8,128]{3,2,1,0:T(8,128)} %pack.3), calls=%async_computation.2 | async-start | bytes 2097152 | tf_op jit(solution)/shard_map/all_to_all | solution.py:611
  14.9 28.1 %copy-start.11 = (f32[31]{0:T(128)S(1)}, f32[31]{0:T(128)}, u32[]{:S(2)}) copy-start(f32[31]{0:T(128)} %constant.79) | copy-start | bytes 376
  14.9 28.1 %copy-start.12 = (f32[31]{0:T(128)S(1)}, f32[31]{0:T(128)}, u32[]{:S(2)}) copy-start(f32[31]{0:T(128)} %constant.69.clone) | copy-start | bytes 376
  14.9 30.7 %copy-start.1 = (f32[496,8,128]{2,1,0:T(8,128)S(1)}, f32[496,8,128]{2,1,0:T(8,128)}, u32[]{:S(2)}) copy-start(f32[496,8,128]{2,1,0:T(8,128)} %constant.72.clone.lengths) | copy-start | bytes 6094852
  14.9 30.7 %copy-start.5 = (f32[2,4,8,128]{3,2,1,0:T(8,128)S(1)}, f32[2,4,8,128]{3,2,1,0:T(8,128)}, u32[]{:S(2)}) copy-start(f32[2,4,8,128]{3,2,1,0:T(8,128)} %constant.75.clone.last_lengths) | copy-start | bytes 98308
  14.9 30.7 %copy-start.6 = (f32[4,8,128]{2,1,0:T(8,128)S(1)}, f32[4,8,128]{2,1,0:T(8,128)}, u32[]{:S(2)}) copy-start(f32[4,8,128]{2,1,0:T(8,128)} %constant.74.clone.last_two) | copy-start | bytes 49156
  14.9 30.7 %copy-start.7 = (f32[2,8,128]{2,1,0:T(8,128)S(1)}, f32[2,8,128]{2,1,0:T(8,128)}, u32[]{:S(2)}) copy-start(f32[2,8,128]{2,1,0:T(8,128)} %constant.73.clone.last_one) | copy-start | bytes 24580
  15.0 30.7 %copy-start.8 = (f32[8,128]{1,0:T(8,128)S(1)}, f32[8,128]{1,0:T(8,128)}, u32[]{:S(2)}) copy-start(f32[8,128]{1,0:T(8,128)} %constant.71.clone.waves) | copy-start | bytes 12292
  15.0 30.7 %copy-start.9 = (f32[496]{0:T(512)S(1)}, f32[496]{0:T(512)}, u32[]{:S(2)}) copy-start(f32[496]{0:T(512)} %constant.70.clone.nodes) | copy-start | bytes 5956
  37.0 4.4 %copy-start.3 = (f32[16,16,8,128]{3,2,1,0:T(8,128)}, f32[16,16,8,128]{3,2,1,0:T(8,128)S(1)}, u32[]{:S(2)}) copy-start(f32[16,16,8,128]{3,2,1,0:T(8,128)S(1)} %all-to-all-done.2.in_ref) | copy-start | bytes 3145732
  37.0 29.7 %all-to-all-start = ((f32[16,16,8,128]{3,2,1,0:T(8,128)}), f32[16,16,8,128]{3,2,1,0:T(8,128)}, u32[]{:S(2)}, u32[]{:S(2)}) async-start(f32[16,16,8,128]{3,2,1,0:T(8,128)} %pack.2), calls=%async_computation | async-start | bytes 2097152 | tf_op jit(solution)/shard_map/all_to_all | solution.py:611
  41.4 1.2 copy-start.4
  42.8 2.9 %collective-permute-start.1 = (f32[8,2,16,8,128]{4,3,2,1,0:T(8,128)S(1)}, f32[8,2,16,8,128]{4,3,2,1,0:T(8,128)}, u32[]{:S(2)}, u32[]{:S(2)}) collective-permute-start(f32[8,2,16,8,128]{4,3,2,1,0:T(8,128)S(1)} %join.3.own), channel_id=1, source_target_pairs={{0,1},{1,0},{2,3},{3,2},{4,5},{5,4},{6,7},{7,6},{8,9},{9,8},{10,11... | collective-permute-start | bytes 3145736 | tf_op jit(solution)/shard_map/ppermute | solution.py:19
  65.7 1.0 copy-start.2
  66.7 33.2 %all-to-all-start.3 = ((f32[16,16,8,128]{3,2,1,0:T(8,128)}), f32[16,16,8,128]{3,2,1,0:T(8,128)}, u32[]{:S(2)}, u32[]{:S(2)}) async-start(f32[16,16,8,128]{3,2,1,0:T(8,128)} %copy-done.2), calls=%async_computation.3 | async-start | bytes 2097152 | tf_op jit(solution)/shard_map/all_to_all | solution.py:611
  74.9 2.9 %collective-permute-start = (f32[8,2,16,8,128]{4,3,2,1,0:T(8,128)S(1)}, f32[8,2,16,8,128]{4,3,2,1,0:T(8,128)}, u32[]{:S(2)}, u32[]{:S(2)}) collective-permute-start(f32[8,2,16,8,128]{4,3,2,1,0:T(8,128)S(1)} %join.2.own), channel_id=1, source_target_pairs={{0,1},{1,0},{2,3},{3,2},{4,5},{5,4},{6,7},{7,6},{8,9},{9,8},{10,11... | collective-permute-start | bytes 3145736 | tf_op jit(solution)/shard_map/ppermute | solution.py:19
  99.9 32.0 %all-to-all-start.1 = ((f32[16,16,8,128]{3,2,1,0:T(8,128)}), f32[16,16,8,128]{3,2,1,0:T(8,128)S(1)}, u32[]{:S(2)}, u32[]{:S(2)}) async-start(f32[16,16,8,128]{3,2,1,0:T(8,128)} %levels.2), calls=%async_computation.1 | async-start | bytes 2097152 | tf_op jit(solution)/shard_map/all_to_all | solution.py:611
  132.0 1.0 copy-start.10

commit v2 on v1

--- a/solution.py
+++ b/solution.py
@@ -279,61 +279,83 @@
     return full
 
 
-def pack_kernel(in_ref, out_ref):
+def pack_kernel(chunk, ids, in_ref, *refs):
+    outs, tiles = refs[:PIECES], refs[-1]
+    me = ids[0]
     upper = lax.broadcasted_iota(jnp.int32, (8, 128), 0) < 4
-    for t1 in range(16):
-        groups = [None] * 4
-        for high in range(2):
-            real = in_ref[0, t1, 8 * high : 8 * high + 8, :]
-            imag = in_ref[1, t1, 8 * high : 8 * high + 8, :]
-            groups[2 * high] = jnp.where(upper, real, pltpu.roll(imag, 4, 0))
-            groups[2 * high + 1] = jnp.where(upper, pltpu.roll(real, 4, 0), imag)
-        for j, tile in enumerate(swap_lanes(groups)):
-            out_ref[j, t1] = tile
-
-
-def pack(weights, chunk):
+    for turn_of in range(4):
+        group = turn_of ^ (me // 4)
+        lanes = pl.ds(pl.multiple_of(group * 128, 128), 128)
+
+        def step(t1, carry):
+            groups = [None] * 4
+            for high in range(2):
+                real = in_ref[0, t1, 8 * high : 8 * high + 8, lanes]
+                imag = in_ref[1, t1, 8 * high : 8 * high + 8, lanes]
+                groups[2 * high] = jnp.where(upper, real, pltpu.roll(imag, 4, 0))
+                groups[2 * high + 1] = jnp.where(upper, pltpu.roll(real, 4, 0), imag)
+            for j, tile in enumerate(swap_lanes(groups)):
+                tiles[j, t1] = tile
+            return carry
+
+        lax.fori_loop(0, 16, step, 0, unroll=True)
+        for j in range(4):
+            outs[4 * turn_of + j][...] = tiles[j ^ (me % 4)]
+
+
+def pack(weights, ids, chunk):
+    piece = jax.ShapeDtypeStruct((16, 8, 128), jnp.float32)
     return pl.pallas_call(
-        pack_kernel,
-        grid=(4,),
-        in_specs=[pl.BlockSpec((2, 16, 16, 128), lambda i: (0, 0, 0, 4 * chunk + i))],
-        out_specs=pl.BlockSpec((4, 16, 8, 128), lambda i: (i, 0, 0, 0)),
-        out_shape=jax.ShapeDtypeStruct((PIECES, 16, 8, 128), jnp.float32),
+        partial(pack_kernel, chunk),
+        grid=(1,),
+        in_specs=[
+            pl.BlockSpec(memory_space=pltpu.SMEM),
+            pl.BlockSpec((2, 16, 16, 512), lambda i: (0, 0, 0, chunk)),
+        ],
+        out_specs=[pl.BlockSpec((16, 8, 128), lambda i: (0, 0, 0))] * PIECES,
+        out_shape=[piece] * PIECES,
+        scratch_shapes=[pltpu.VMEM((4, 16, 8, 128), jnp.float32)],
+        compiler_params=pltpu.CompilerParams(vmem_limit_bytes=VMEM_LIMIT),
         cost_estimate=pl.CostEstimate(flops=10**6, bytes_accessed=2**21, transcendentals=0),
         name="pack",
-    )(weights)
-
-
-def join_kernel(in_ref, out_ref):
+    )(ids, weights)
+
+
+def join_kernel(ids, *refs):
+    pieces, out_ref = refs[:PIECES], refs[-1]
+    me = ids[0]
     upper = lax.broadcasted_iota(jnp.int32, (8, 128), 0) < 4
-
-    def step(box, carry):
+    by = me % 2
+    is_low = jnp.broadcast_to(by, (8, 128)) == 0
+    for pair in range(8):
+        box = pair ^ (me // 2)
         for t1 in range(16):
-            low = in_ref[2 * box, t1]
-            high = in_ref[2 * box + 1, t1]
+            mine = pieces[2 * pair][t1]
+            partner = pieces[2 * pair + 1][t1]
+            low = jnp.where(is_low, mine, partner)
+            high = jnp.where(is_low, partner, mine)
             out_ref[box, 0, t1] = jnp.where(upper, low, pltpu.roll(high, 4, 0))
             out_ref[box, 1, t1] = jnp.where(upper, pltpu.roll(low, 4, 0), high)
-        return carry
-
-    lax.fori_loop(0, 8, step, 0)
-
-
-def join(received):
+
+
+def join(ids, received):
     return pl.pallas_call(
         join_kernel,
-        in_specs=[pl.BlockSpec(memory_space=pltpu.VMEM)],
+        in_specs=[pl.BlockSpec(memory_space=pltpu.SMEM)]
+        + [pl.BlockSpec(memory_space=pltpu.VMEM)] * PIECES,
         out_specs=pl.BlockSpec(memory_space=pltpu.VMEM),
         out_shape=jax.ShapeDtypeStruct((8, 2, 16, 8, 128), jnp.float32),
         compiler_params=pltpu.CompilerParams(vmem_limit_bytes=VMEM_LIMIT),
         cost_estimate=pl.CostEstimate(flops=10**6, bytes_accessed=2**21, transcendentals=0),
         name="join",
-    )(received)
+    )(ids, *received)
 
 
 def levels_kernel(
     chunk, ids, nodes, own, other, speeds, waves, lengths, last_one, last_two, last_lengths,
-    weights, out, boxes_a, boxes_b, sums, turned, mixed,
+    weights, *refs,
 ):
+    outs, (boxes_a, boxes_b, sums, turned, mixed, last_phase) = refs[:PIECES], refs[PIECES:]
     even, odd = folded_table()
     row = (chunk * PIECES + ids[0]).astype(jnp.float32)
     core = ids[1]
@@ -479,26 +501,30 @@
             total = term if total is None else total + term
         mixed[e] = total
 
-    last_phase = [[fine_two[e] * last_two[a] for a in range(4)] for e in range(2)]
-
-    def finish_box(box, carry):
+    for e in range(2):
+        for a in range(4):
+            last_phase[e, a] = fine_two[e] * last_two[a]
+
+    def finish_box(mask):
+        target = mask ^ ids[0]
+        box, e = target // 2, target % 2
+        out = outs[mask]
         code = reversed_code(box)
         point = first_point(3, code.astype(jnp.float32))
-        for e in range(2):
-            speed = fine_speed(code, e)
-            for high in range(2):
-                across = point * last_one[high]
-                first = pl.multiple_of(box * 32 + high * 8, 8)
-                for a in range(4):
-                    phase = (across + last_phase[e][a]) + speed * last_lengths[high, a]
-                    cosine, sine = turn(phase)
-                    real = mixed[e, pl.ds(first, 8), 128 * a : 128 * a + 128]
-                    imag = mixed[e, pl.ds(first + 16, 8), 128 * a : 128 * a + 128]
-                    out[2 * box + e, high * 4 + a] = real * cosine - imag * sine
-                    out[2 * box + e, 8 + high * 4 + a] = real * sine + imag * cosine
-        return carry
-
-    lax.fori_loop(0, 8, finish_box, 0)
+        speed = fine_speed(code, e)
+        for high in range(2):
+            across = point * last_one[high]
+            first = pl.multiple_of(box * 32 + high * 8, 8)
+            for a in range(4):
+                phase = (across + last_phase[e, a]) + speed * last_lengths[high, a]
+                cosine, sine = turn(phase)
+                real = mixed[e, pl.ds(first, 8), 128 * a : 128 * a + 128]
+                imag = mixed[e, pl.ds(first + 16, 8), 128 * a : 128 * a + 128]
+                out[high * 4 + a] = real * cosine - imag * sine
+                out[8 + high * 4 + a] = real * sine + imag * cosine
+
+    for mask in range(PIECES):
+        finish_box(mask)
 
 
 def levels(chunk, ids, own, other, speeds):
@@ -509,14 +535,15 @@
     return pl.pallas_call(
         partial(levels_kernel, chunk),
         in_specs=[in_smem, in_smem] + [in_vmem] * 9,
-        out_specs=in_vmem,
-        out_shape=jax.ShapeDtypeStruct((PIECES, 16, 8, 128), jnp.float32),
+        out_specs=[in_vmem] * PIECES,
+        out_shape=[jax.ShapeDtypeStruct((16, 8, 128), jnp.float32)] * PIECES,
         scratch_shapes=[
             pltpu.VMEM((8, 2, 16, 8, 128), jnp.float32),
             pltpu.VMEM((8, 2, 16, 8, 128), jnp.float32),
             pltpu.VMEM((2, 16, 4, 8, 128), jnp.float32),
             pltpu.VMEM((2, 2048, 128), jnp.float32),
             pltpu.VMEM((2, 256, 512), jnp.float32),
+            pltpu.VMEM((2, 4, 8, 128), jnp.float32),
         ],
         compiler_params=pltpu.CompilerParams(vmem_limit_bytes=VMEM_LIMIT),
         cost_estimate=pl.CostEstimate(flops=10**8, bytes_accessed=2**23, transcendentals=0),
@@ -528,35 +555,47 @@
     )
 
 
-def unpack_kernel(*refs):
-    in_ref, out_ref, rows = refs[0], refs[-2], refs[-1]
-    for part in range(2):
-        for high in range(2):
-            for a in range(4):
-                tiles = [in_ref[j, part * 8 + high * 4 + a] for j in range(4)]
-                for b, tile in enumerate(swap_lanes(tiles)):
-                    t2 = 4 * b + a
-                    rows[part * 2 + high, 8 * t2 : 8 * t2 + 8, :] = tile
-            for t1 in range(8):
-                out_ref[part, high * 8 + t1] = rows[part * 2 + high, pl.ds(t1, 16, stride=8), :]
-
-
-def unpack(received, chunk, earlier):
-    operands = [received]
-    in_specs = [pl.BlockSpec((4, 16, 8, 128), lambda i: (i, 0, 0, 0))]
+def unpack_kernel(ids, *refs):
+    pieces, out_ref, tiles, rows = refs[:PIECES], refs[-3], refs[-2], refs[-1]
+    me = ids[0]
+    for turn_of in range(4):
+        group = turn_of ^ (me // 4)
+        lanes = pl.ds(pl.multiple_of(group * 128, 128), 128)
+        for j in range(4):
+            tiles[j ^ (me % 4)] = pieces[4 * turn_of + j][...]
+        for part in range(2):
+            for high in range(2):
+                block = part * 2 + high
+                for a in range(4):
+                    values = [tiles[j, part * 8 + high * 4 + a] for j in range(4)]
+                    for b, tile in enumerate(swap_lanes(values)):
+                        t2 = 4 * b + a
+                        rows[block, 8 * t2 : 8 * t2 + 8, :] = tile
+                for t1 in range(8):
+                    out_ref[part, high * 8 + t1, :, lanes] = rows[block, pl.ds(t1, 16, stride=8), :]
+
+
+def unpack(ids, received, chunk, earlier):
+    operands = [ids, *received]
+    in_specs = [pl.BlockSpec(memory_space=pltpu.SMEM)]
+    in_specs += [pl.BlockSpec((16, 8, 128), lambda i: (0, 0, 0))] * PIECES
     aliases = {}
     if earlier is not None:
         operands.append(earlier)
         in_specs.append(pl.BlockSpec(memory_space=pl.ANY))
-        aliases = {1: 0}
+        aliases = {len(operands) - 1: 0}
     return pl.pallas_call(
         unpack_kernel,
-        grid=(4,),
+        grid=(1,),
         in_specs=in_specs,
-        out_specs=pl.BlockSpec((2, 16, 16, 128), lambda i: (0, 0, 0, 4 * chunk + i)),
+        out_specs=pl.BlockSpec((2, 16, 16, 512), lambda i: (0, 0, 0, chunk)),
         out_shape=jax.ShapeDtypeStruct((2, 16, 16, 1024), jnp.float32),
-        scratch_shapes=[pltpu.VMEM((4, 128, 128), jnp.float32)],
+        scratch_shapes=[
+            pltpu.VMEM((4, 16, 8, 128), jnp.float32),
+            pltpu.VMEM((4, 128, 128), jnp.float32),
+        ],
         input_output_aliases=aliases,
+        compiler_params=pltpu.CompilerParams(vmem_limit_bytes=VMEM_LIMIT),
         cost_estimate=pl.CostEstimate(flops=10**6, bytes_accessed=2**21, transcendentals=0),
         name="unpack",
     )(*operands)
@@ -595,20 +634,24 @@
     speeds = speed_tables(speed_modes, core)
     received = []
     for chunk in range(CHUNKS):
-        received.append(deal(pack(local, chunk)))
+        received.append(deal(pack(local, ids, chunk)))
     results = []
     for chunk in range(CHUNKS):
-        own = join(received[chunk])
+        own = join(ids, received[chunk])
         other = partner_2(own, "cores", 0)
         results.append(deal(levels(chunk, ids, own, other, speeds[chunk])))
     out = None
     for chunk in range(CHUNKS):
-        out = unpack(results[chunk], chunk, out)
+        out = unpack(ids, results[chunk], chunk, out)
     return out.reshape(weights.shape)
 
 
 def deal(pieces):
-    return lax.all_to_all(pieces, ("bx", "by"), 0, 0, tiled=True)
+    moved = [pieces[0]]
+    for mask in range(1, PIECES):
+        pairs = [(source, source ^ mask) for source in range(PIECES)]
+        moved.append(lax.ppermute(pieces[mask], ("bx", "by"), pairs))
+    return moved
 
 
 def solution(mesh):

time: 138 us -> 190 us (1.38)
  starting transfers between devices: 24.4 us -> 97.4 us
  waiting for transfers between devices: 49.5 us -> 18.2 us
  Pallas kernels: 58 us -> 62.7 us
  local copies, waits for them, and re-layouts: 3.88 us -> 8.2 us
    ppermute x0 -> x60, starting transfers between devices: none -> 97.3 us  [deal(): moved.append(lax.ppermute(pieces[mask], ('bx', 'by'), pairs))]
    all_to_all x4 -> x0, waiting for transfers between devices: 45.4 us -> none  [deal(): return lax.all_to_all(pieces, ('bx', 'by'), 0, 0, tiled=True)]
    all_to_all x4 -> x0, starting transfers between devices: 24.3 us -> none  [deal(): return lax.all_to_all(pieces, ('bx', 'by'), 0, 0, tiled=True)]
    ppermute x0 -> x60, waiting for transfers between devices: none -> 18.2 us  [deal(): moved.append(lax.ppermute(pieces[mask], ('bx', 'by'), pairs))]
    pallas_call x6, Pallas kernels: 16.9 us -> 21.6 us  [the longest x2 10.9 us: unpack(): pl.pallas_call(unpack_kernel, grid=(1,), in_specs=in_specs, out_specs=pl....]
    ppermute x2, waiting for transfers between devices: 4.06 us -> 0.01 us  [partner_2(): return lax.ppermute(value, axis, pairs)]
    unnamed x26 -> x44, local copies, waits for them, and re-layouts: 3.25 us -> 6.12 us
  transfers between devices with their start and end apart: 6 -> 62, of which waited for: 5 -> 12; matrix products, arithmetic and copies ran while one was open for 1% -> 1% of each run, Pallas kernels for 37% -> 28%
where the time goes in v2:
time: 190 us; the launch traced here: 188 us
  starting transfers between devices  97.4 us (51%)
  Pallas kernels  62.7 us (33%)
  waiting for transfers between devices  18.2 us (10%)
  local copies, waits for them, and re-layouts  8.2 us (4%)
    ppermute x60, starting transfers between devices, deal(): moved.append(lax.ppermute(pieces[mask], ('bx', 'by'), pairs))  97.3 us
    pallas_call x2, Pallas kernels, levels(): pl.pallas_call(partial(levels_kernel, chunk), in_specs=[in_smem, in_smem]...  41.1 us
    ppermute x60, waiting for transfers between devices, deal(): moved.append(lax.ppermute(pieces[mask], ('bx', 'by'), pairs))  18.2 us
    pallas_call x2, Pallas kernels, unpack(): pl.pallas_call(unpack_kernel, grid=(1,), in_specs=in_specs, out_specs=pl....  10.9 us
    pallas_call x2, Pallas kernels, pack(): pl.pallas_call(partial(pack_kernel, chunk), grid=(1,), in_specs=[pl.Block...  8.42 us
    unnamed x44, local copies, waits for them, and re-layouts  6.12 us
  transfers between devices with their start and end apart: 62, of which 12 were waited for; matrix products, arithmetic and copies ran while one was open for 1% of the time, Pallas kernels for 28%

profile of v2, /device:TPU:10, one launch (start us, length us, event | category | flops | bytes accessed | tf_op | source)
XLA Modules:
  0.0 187.7 jit_solution(10124070774105620312)
XLA Ops:
  1.7 4.2 %pack.3 = (f32[16,8,128]{2,1,0:T(8,128)S(1)}, f32[16,8,128]{2,1,0:T(8,128)S(1)}, f32[16,8,128]{2,1,0:T(8,128)S(1)}, f32[16,8,128]{2,1,0:T(8,128)S(1)}, f32[16,8,...) custom-call(s32[2]{0:T(128)S(1)} %pad_add_fusion.ids, ...), custom_call_target="tpu_custom_call" | custom-call | flops 1000000 | bytes 2097152 | tf_op jit(solution)/shard_map/pack/pallas_call | solution.py:308
  9.9 2.5 %collective-permute-start.35 = (f32[16,8,128]{2,1,0:T(8,128)S(1)}, f32[16,8,128]{2,1,0:T(8,128)S(1)}, u32[]{:S(2)}, u32[]{:S(2)}) collective-permute-start(f32[16,8,128]{2,1,0:T(8,128)S(1)} %get-tuple-element.106), channel_id=1, source_target_pairs={{0,10},{2,8},{4,14},{6,12},{8,2},{10,0},{12,6},{14,4},{16,26},{18,... | collective-permute-start | bytes 196616 | tf_op jit(solution)/shard_map/ppermute | solution.py:653
  12.8 2.4 %collective-permute-start.37 = (f32[16,8,128]{2,1,0:T(8,128)S(1)}, f32[16,8,128]{2,1,0:T(8,128)S(1)}, u32[]{:S(2)}, u32[]{:S(2)}) collective-permute-start(f32[16,8,128]{2,1,0:T(8,128)S(1)} %get-tuple-element.108), channel_id=1, source_target_pairs={{0,14},{2,12},{4,10},{6,8},{8,6},{10,4},{12,2},{14,0},{16,30},{18,... | collective-permute-start | bytes 196616 | tf_op jit(solution)/shard_map/ppermute | solution.py:653
  15.3 2.6 %collective-permute-start.38 = (f32[16,8,128]{2,1,0:T(8,128)S(1)}, f32[16,8,128]{2,1,0:T(8,128)S(1)}, u32[]{:S(2)}, u32[]{:S(2)}) collective-permute-start(f32[16,8,128]{2,1,0:T(8,128)S(1)} %get-tuple-element.109), channel_id=1, source_target_pairs={{0,16},{2,18},{4,20},{6,22},{8,24},{10,26},{12,28},{14,30},{16,0},... | collective-permute-start | bytes 196616 | tf_op jit(solution)/shard_map/ppermute | solution.py:653
  19.2 2.6 %collective-permute-start.40 = (f32[16,8,128]{2,1,0:T(8,128)S(1)}, f32[16,8,128]{2,1,0:T(8,128)S(1)}, u32[]{:S(2)}, u32[]{:S(2)}) collective-permute-start(f32[16,8,128]{2,1,0:T(8,128)S(1)} %get-tuple-element.111), channel_id=1, source_target_pairs={{0,20},{2,22},{4,16},{6,18},{8,28},{10,30},{12,24},{14,26},{16,4},... | collective-permute-start | bytes 196616 | tf_op jit(solution)/shard_map/ppermute | solution.py:653
  21.8 4.2 %pack.2 = (f32[16,8,128]{2,1,0:T(8,128)S(1)}, f32[16,8,128]{2,1,0:T(8,128)S(1)}, f32[16,8,128]{2,1,0:T(8,128)S(1)}, f32[16,8,128]{2,1,0:T(8,128)S(1)}, f32[16,8,...) custom-call(s32[2]{0:T(128)S(1)} %pad_add_fusion.ids, ...), custom_call_target="tpu_custom_call" | custom-call | flops 1000000 | bytes 2097152 | tf_op jit(solution)/shard_map/pack/pallas_call | solution.py:308
  32.9 2.5 %collective-permute-start.6 = (f32[16,8,128]{2,1,0:T(8,128)S(1)}, f32[16,8,128]{2,1,0:T(8,128)S(1)}, u32[]{:S(2)}, u32[]{:S(2)}) collective-permute-start(f32[16,8,128]{2,1,0:T(8,128)S(1)} %get-tuple-element.76), channel_id=1, source_target_pairs={{0,14},{2,12},{4,10},{6,8},{8,6},{10,4},{12,2},{14,0},{16,30},{18,... | collective-permute-start | bytes 196616 | tf_op jit(solution)/shard_map/ppermute | solution.py:653
  35.8 2.5 %collective-permute-start.8 = (f32[16,8,128]{2,1,0:T(8,128)S(1)}, f32[16,8,128]{2,1,0:T(8,128)S(1)}, u32[]{:S(2)}, u32[]{:S(2)}) collective-permute-start(f32[16,8,128]{2,1,0:T(8,128)S(1)} %get-tuple-element.78), channel_id=1, source_target_pairs={{0,18},{2,16},{4,22},{6,20},{8,26},{10,24},{12,30},{14,28},{16,2},... | collective-permute-start | bytes 196616 | tf_op jit(solution)/shard_map/ppermute | solution.py:653
  39.6 3.6 %collective-permute-start.10 = (f32[16,8,128]{2,1,0:T(8,128)S(1)}, f32[16,8,128]{2,1,0:T(8,128)S(1)}, u32[]{:S(2)}, u32[]{:S(2)}) collective-permute-start(f32[16,8,128]{2,1,0:T(8,128)S(1)} %get-tuple-element.80), channel_id=1, source_target_pairs={{0,22},{2,20},{4,18},{6,16},{8,30},{10,28},{12,26},{14,24},{16,6},... | collective-permute-start | bytes 196616 | tf_op jit(solution)/shard_map/ppermute | solution.py:653
  43.1 2.0 %collective-permute-start.12 = (f32[16,8,128]{2,1,0:T(8,128)S(1)}, f32[16,8,128]{2,1,0:T(8,128)S(1)}, u32[]{:S(2)}, u32[]{:S(2)}) collective-permute-start(f32[16,8,128]{2,1,0:T(8,128)S(1)} %get-tuple-element.82), channel_id=1, source_target_pairs={{0,26},{2,24},{4,30},{6,28},{8,18},{10,16},{12,22},{14,20},{16,10}... | collective-permute-start | bytes 196616 | tf_op jit(solution)/shard_map/ppermute | solution.py:653
  46.2 3.3 %collective-permute-done.9.refs_10_ = f32[16,8,128]{2,1,0:T(8,128)S(1)} collective-permute-done((f32[16,8,128]{2,1,0:T(8,128)S(1)}, f32[16,8,128]{2,1,0:T(8,128)S(1)}, u32[]{:S(2)}, u32[]{:S(2)}) %collective-permute-start.9) | collective-permute-done | bytes 65568 | tf_op jit(solution)/shard_map/ppermute | solution.py:653
  49.5 3.7 %collective-permute-start.14 = (f32[16,8,128]{2,1,0:T(8,128)S(1)}, f32[16,8,128]{2,1,0:T(8,128)S(1)}, u32[]{:S(2)}, u32[]{:S(2)}) collective-permute-start(f32[16,8,128]{2,1,0:T(8,128)S(1)} %get-tuple-element.84), channel_id=1, source_target_pairs={{0,30},{2,28},{4,26},{6,24},{8,22},{10,20},{12,18},{14,16},{16,14}... | collective-permute-start | bytes 196616 | tf_op jit(solution)/shard_map/ppermute | solution.py:653
  53.3 4.3 %collective-permute-start.41 = (f32[16,8,128]{2,1,0:T(8,128)S(1)}, f32[16,8,128]{2,1,0:T(8,128)S(1)}, u32[]{:S(2)}, u32[]{:S(2)}) collective-permute-start(f32[16,8,128]{2,1,0:T(8,128)S(1)} %get-tuple-element.112), channel_id=1, source_target_pairs={{0,22},{2,20},{4,18},{6,16},{8,30},{10,28},{12,26},{14,24},{16,6},... | collective-permute-start | bytes 196616 | tf_op jit(solution)/shard_map/ppermute | solution.py:653
  57.6 2.1 %collective-permute-start.42 = (f32[16,8,128]{2,1,0:T(8,128)S(1)}, f32[16,8,128]{2,1,0:T(8,128)S(1)}, u32[]{:S(2)}, u32[]{:S(2)}) collective-permute-start(f32[16,8,128]{2,1,0:T(8,128)S(1)} %get-tuple-element.113), channel_id=1, source_target_pairs={{0,24},{2,26},{4,28},{6,30},{8,16},{10,18},{12,20},{14,22},{16,8},... | collective-permute-start | bytes 196616 | tf_op jit(solution)/shard_map/ppermute | solution.py:653
  62.8 2.1 %collective-permute-done.14.refs_15_ = f32[16,8,128]{2,1,0:T(8,128)S(1)} collective-permute-done((f32[16,8,128]{2,1,0:T(8,128)S(1)}, f32[16,8,128]{2,1,0:T(8,128)S(1)}, u32[]{:S(2)}, u32[]{:S(2)}) %collective-permute-start.14) | collective-permute-done | bytes 65568 | tf_op jit(solution)/shard_map/ppermute | solution.py:653
  69.4 2.3 %collective-permute-done.45.refs_15_ = f32[16,8,128]{2,1,0:T(8,128)S(1)} collective-permute-done((f32[16,8,128]{2,1,0:T(8,128)S(1)}, f32[16,8,128]{2,1,0:T(8,128)S(1)}, u32[]{:S(2)}, u32[]{:S(2)}) %collective-permute-start.45) | collective-permute-done | bytes 65568 | tf_op jit(solution)/shard_map/ppermute | solution.py:653
  73.8 21.0 %levels.2 = (f32[16,8,128]{2,1,0:T(8,128)S(1)}, f32[16,8,128]{2,1,0:T(8,128)S(1)}, f32[16,8,128]{2,1,0:T(8,128)S(1)}, f32[16,8,128]{2,1,0:T(8,128)S(1)}, f32[16,...) custom-call(s32[2]{0:T(128)S(1)} %pad_add_fusion.ids, ...), custom_call_target="tpu_custom_call" | custom-call | flops 100000000 | bytes 8388608 | tf_op jit(solution)/shard_map/levels/pallas_call | solution.py:535
  101.4 2.2 %collective-permute-start.20 = (f32[16,8,128]{2,1,0:T(8,128)S(1)}, f32[16,8,128]{2,1,0:T(8,128)S(1)}, u32[]{:S(2)}, u32[]{:S(2)}) collective-permute-start(f32[16,8,128]{2,1,0:T(8,128)S(1)} %get-tuple-element.90), channel_id=1, source_target_pairs={{0,10},{2,8},{4,14},{6,12},{8,2},{10,0},{12,6},{14,4},{16,26},{18,... | collective-permute-start | bytes 196616 | tf_op jit(solution)/shard_map/ppermute | solution.py:653
  104.8 2.5 %collective-permute-start.22 = (f32[16,8,128]{2,1,0:T(8,128)}, f32[16,8,128]{2,1,0:T(8,128)}, u32[]{:S(2)}, u32[]{:S(2)}) collective-permute-start(f32[16,8,128]{2,1,0:T(8,128)} %get-tuple-element.92), channel_id=1, source_target_pairs={{0,14},{2,12},{4,10},{6,8},{8,6},{10,4},{12,2},{14,0},{16,30},{18,... | collective-permute-start | bytes 196616 | tf_op jit(solution)/shard_map/ppermute | solution.py:653
  108.1 2.3 %collective-permute-start.24 = (f32[16,8,128]{2,1,0:T(8,128)}, f32[16,8,128]{2,1,0:T(8,128)}, u32[]{:S(2)}, u32[]{:S(2)}) collective-permute-start(f32[16,8,128]{2,1,0:T(8,128)} %get-tuple-element.94), channel_id=1, source_target_pairs={{0,18},{2,16},{4,22},{6,20},{8,26},{10,24},{12,30},{14,28},{16,2},... | collective-permute-start | bytes 196616 | tf_op jit(solution)/shard_map/ppermute | solution.py:653
  114.7 20.1 %levels.3 = (f32[16,8,128]{2,1,0:T(8,128)S(1)}, f32[16,8,128]{2,1,0:T(8,128)S(1)}, f32[16,8,128]{2,1,0:T(8,128)S(1)}, f32[16,8,128]{2,1,0:T(8,128)S(1)}, f32[16,...) custom-call(s32[2]{0:T(128)S(1)} %pad_add_fusion.ids, ...), custom_call_target="tpu_custom_call" | custom-call | flops 100000000 | bytes 8388608 | tf_op jit(solution)/shard_map/levels/pallas_call | solution.py:535
  135.3 1.8 collective-permute-start.48
  140.3 2.8 %collective-permute-start.52 = (f32[16,8,128]{2,1,0:T(8,128)S(1)}, f32[16,8,128]{2,1,0:T(8,128)S(1)}, u32[]{:S(2)}, u32[]{:S(2)}) collective-permute-start(f32[16,8,128]{2,1,0:T(8,128)S(1)} %get-tuple-element.123), channel_id=1, source_target_pairs={{0,12},{2,14},{4,8},{6,10},{8,4},{10,6},{12,0},{14,2},{16,28},{18,... | collective-permute-start | bytes 196616 | tf_op jit(solution)/shard_map/ppermute | solution.py:653
  144.3 1.9 %collective-permute-start.54 = (f32[16,8,128]{2,1,0:T(8,128)S(1)}, f32[16,8,128]{2,1,0:T(8,128)S(1)}, u32[]{:S(2)}, u32[]{:S(2)}) collective-permute-start(f32[16,8,128]{2,1,0:T(8,128)S(1)} %get-tuple-element.125), channel_id=1, source_target_pairs={{0,16},{2,18},{4,20},{6,22},{8,24},{10,26},{12,28},{14,30},{16,0},... | collective-permute-start | bytes 196616 | tf_op jit(solution)/shard_map/ppermute | solution.py:653
  147.0 3.4 %collective-permute-start.56 = (f32[16,8,128]{2,1,0:T(8,128)S(1)}, f32[16,8,128]{2,1,0:T(8,128)S(1)}, u32[]{:S(2)}, u32[]{:S(2)}) collective-permute-start(f32[16,8,128]{2,1,0:T(8,128)S(1)} %get-tuple-element.127), channel_id=1, source_target_pairs={{0,20},{2,22},{4,16},{6,18},{8,28},{10,30},{12,24},{14,26},{16,4},... | collective-permute-start | bytes 196616 | tf_op jit(solution)/shard_map/ppermute | solution.py:653
  154.2 3.5 %collective-permute-start.60 = (f32[16,8,128]{2,1,0:T(8,128)S(1)}, f32[16,8,128]{2,1,0:T(8,128)S(1)}, u32[]{:S(2)}, u32[]{:S(2)}) collective-permute-start(f32[16,8,128]{2,1,0:T(8,128)S(1)} %get-tuple-element.131), channel_id=1, source_target_pairs={{0,28},{2,30},{4,24},{6,26},{8,20},{10,22},{12,16},{14,18},{16,12}... | collective-permute-start | bytes 196616 | tf_op jit(solution)/shard_map/ppermute | solution.py:653
  157.8 3.4 %collective-permute-done.56.refs_10_ = f32[16,8,128]{2,1,0:T(8,128)S(1)} collective-permute-done((f32[16,8,128]{2,1,0:T(8,128)S(1)}, f32[16,8,128]{2,1,0:T(8,128)S(1)}, u32[]{:S(2)}, u32[]{:S(2)}) %collective-permute-start.56) | collective-permute-done | bytes 65568 | tf_op jit(solution)/shard_map/ppermute | solution.py:653
  161.1 2.1 %collective-permute-start.61 = (f32[16,8,128]{2,1,0:T(8,128)S(1)}, f32[16,8,128]{2,1,0:T(8,128)S(1)}, u32[]{:S(2)}, u32[]{:S(2)}) collective-permute-start(f32[16,8,128]{2,1,0:T(8,128)S(1)} %get-tuple-element.132), channel_id=1, source_target_pairs={{0,30},{2,28},{4,26},{6,24},{8,22},{10,20},{12,18},{14,16},{16,14}... | collective-permute-start | bytes 196616 | tf_op jit(solution)/shard_map/ppermute | solution.py:653
  164.0 5.5 %collective-permute-start.26 = (f32[16,8,128]{2,1,0:T(8,128)S(1)}, f32[16,8,128]{2,1,0:T(8,128)S(1)}, u32[]{:S(2)}, u32[]{:S(2)}) collective-permute-start(f32[16,8,128]{2,1,0:T(8,128)S(1)} %copy-done.19), channel_id=1, source_target_pairs={{0,22},{2,20},{4,18},{6,16},{8,30},{10,28},{12,26},{14,24},{16,6},... | collective-permute-start | bytes 196616 | tf_op jit(solution)/shard_map/ppermute | solution.py:653
  171.7 2.0 %collective-permute-done.60.refs_14_ = f32[16,8,128]{2,1,0:T(8,128)S(1)} collective-permute-done((f32[16,8,128]{2,1,0:T(8,128)S(1)}, f32[16,8,128]{2,1,0:T(8,128)S(1)}, u32[]{:S(2)}, u32[]{:S(2)}) %collective-permute-start.60) | collective-permute-done | bytes 65568 | tf_op jit(solution)/shard_map/ppermute | solution.py:653
  176.8 5.2 %unpack.2.refs_16_ = f32[2,16,16,1024]{3,2,1,0:T(8,128)} custom-call(s32[2]{0:T(128)S(1)} %pad_add_fusion.ids, f32[16,8,128]{2,1,0:T(8,128)S(1)} %get-tuple-element.117.refs_0_, f32[16,8,128]{2,1,0:T(8,128)S(1)} %collective-permute-done.47.refs_1_, f32[16,8,128]{2,1,0:T(8,128)S(1)} %collective-permute-done.48.refs_2_, ...), custom_call_target="tpu_custom_call" | custom-call | flops 1000000 | bytes 2097152 | tf_op jit(solution)/shard_map/unpack/pallas_call | solution.py:587
  182.1 5.7 %unpack.3 = f32[2,16,16,1024]{3,2,1,0:T(8,128)} custom-call(s32[2]{0:T(128)S(1)} %pad_add_fusion.ids, f32[16,8,128]{2,1,0:T(8,128)S(1)} %get-tuple-element.85.refs_0_, f32[16,8,128]{2,1,0:T(8,128)S(1)} %collective-permute-done.16.refs_1_, f32[16,8,128]{2,1,0:T(8,128)S(1)} %collective-permute-done.17.refs_2_, ...), custom_call_target="tpu_custom_call", output_to_operand_aliasing={{}: (17, {})} | custom-call | flops 1000000 | bytes 2097152 | tf_op jit(solution)/shard_map/unpack/pallas_call | solution.py:587
  (168 shorter events, 54.8 us)
Async XLA Ops:
  9.9 9.3 %collective-permute-start.35 = (f32[16,8,128]{2,1,0:T(8,128)S(1)}, f32[16,8,128]{2,1,0:T(8,128)S(1)}, u32[]{:S(2)}, u32[]{:S(2)}) collective-permute-start(f32[16,8,128]{2,1,0:T(8,128)S(1)} %get-tuple-element.106), channel_id=1, source_target_pairs={{0,10},{2,8},{4,14},{6,12},{8,2},{10,0},{12,6},{14,4},{16,26},{18,... | collective-permute-start | bytes 196616 | tf_op jit(solution)/shard_map/ppermute | solution.py:653
  12.4 13.5 %collective-permute-start.36 = (f32[16,8,128]{2,1,0:T(8,128)S(1)}, f32[16,8,128]{2,1,0:T(8,128)S(1)}, u32[]{:S(2)}, u32[]{:S(2)}) collective-permute-start(f32[16,8,128]{2,1,0:T(8,128)S(1)} %get-tuple-element.107), channel_id=1, source_target_pairs={{0,12},{2,14},{4,8},{6,10},{8,4},{10,6},{12,0},{14,2},{16,28},{18,... | collective-permute-start | bytes 196616 | tf_op jit(solution)/shard_map/ppermute | solution.py:653
  12.8 13.7 %collective-permute-start.37 = (f32[16,8,128]{2,1,0:T(8,128)S(1)}, f32[16,8,128]{2,1,0:T(8,128)S(1)}, u32[]{:S(2)}, u32[]{:S(2)}) collective-permute-start(f32[16,8,128]{2,1,0:T(8,128)S(1)} %get-tuple-element.108), channel_id=1, source_target_pairs={{0,14},{2,12},{4,10},{6,8},{8,6},{10,4},{12,2},{14,0},{16,30},{18,... | collective-permute-start | bytes 196616 | tf_op jit(solution)/shard_map/ppermute | solution.py:653
  15.3 12.7 %collective-permute-start.38 = (f32[16,8,128]{2,1,0:T(8,128)S(1)}, f32[16,8,128]{2,1,0:T(8,128)S(1)}, u32[]{:S(2)}, u32[]{:S(2)}) collective-permute-start(f32[16,8,128]{2,1,0:T(8,128)S(1)} %get-tuple-element.109), channel_id=1, source_target_pairs={{0,16},{2,18},{4,20},{6,22},{8,24},{10,26},{12,28},{14,30},{16,0},... | collective-permute-start | bytes 196616 | tf_op jit(solution)/shard_map/ppermute | solution.py:653
  17.9 11.6 %collective-permute-start.39 = (f32[16,8,128]{2,1,0:T(8,128)S(1)}, f32[16,8,128]{2,1,0:T(8,128)S(1)}, u32[]{:S(2)}, u32[]{:S(2)}) collective-permute-start(f32[16,8,128]{2,1,0:T(8,128)S(1)} %get-tuple-element.110), channel_id=1, source_target_pairs={{0,18},{2,16},{4,22},{6,20},{8,26},{10,24},{12,30},{14,28},{16,2},... | collective-permute-start | bytes 196616 | tf_op jit(solution)/shard_map/ppermute | solution.py:653
  19.2 10.8 %collective-permute-start.40 = (f32[16,8,128]{2,1,0:T(8,128)S(1)}, f32[16,8,128]{2,1,0:T(8,128)S(1)}, u32[]{:S(2)}, u32[]{:S(2)}) collective-permute-start(f32[16,8,128]{2,1,0:T(8,128)S(1)} %get-tuple-element.111), channel_id=1, source_target_pairs={{0,20},{2,22},{4,16},{6,18},{8,28},{10,30},{12,24},{14,26},{16,4},... | collective-permute-start | bytes 196616 | tf_op jit(solution)/shard_map/ppermute | solution.py:653
  32.9 10.2 %collective-permute-start.6 = (f32[16,8,128]{2,1,0:T(8,128)S(1)}, f32[16,8,128]{2,1,0:T(8,128)S(1)}, u32[]{:S(2)}, u32[]{:S(2)}) collective-permute-start(f32[16,8,128]{2,1,0:T(8,128)S(1)} %get-tuple-element.76), channel_id=1, source_target_pairs={{0,14},{2,12},{4,10},{6,8},{8,6},{10,4},{12,2},{14,0},{16,30},{18,... | collective-permute-start | bytes 196616 | tf_op jit(solution)/shard_map/ppermute | solution.py:653
  35.8 9.4 %collective-permute-start.8 = (f32[16,8,128]{2,1,0:T(8,128)S(1)}, f32[16,8,128]{2,1,0:T(8,128)S(1)}, u32[]{:S(2)}, u32[]{:S(2)}) collective-permute-start(f32[16,8,128]{2,1,0:T(8,128)S(1)} %get-tuple-element.78), channel_id=1, source_target_pairs={{0,18},{2,16},{4,22},{6,20},{8,26},{10,24},{12,30},{14,28},{16,2},... | collective-permute-start | bytes 196616 | tf_op jit(solution)/shard_map/ppermute | solution.py:653
  38.3 11.2 %collective-permute-start.9 = (f32[16,8,128]{2,1,0:T(8,128)S(1)}, f32[16,8,128]{2,1,0:T(8,128)S(1)}, u32[]{:S(2)}, u32[]{:S(2)}) collective-permute-start(f32[16,8,128]{2,1,0:T(8,128)S(1)} %get-tuple-element.79), channel_id=1, source_target_pairs={{0,20},{2,22},{4,16},{6,18},{8,28},{10,30},{12,24},{14,26},{16,4},... | collective-permute-start | bytes 196616 | tf_op jit(solution)/shard_map/ppermute | solution.py:653
  39.6 13.7 %collective-permute-start.10 = (f32[16,8,128]{2,1,0:T(8,128)S(1)}, f32[16,8,128]{2,1,0:T(8,128)S(1)}, u32[]{:S(2)}, u32[]{:S(2)}) collective-permute-start(f32[16,8,128]{2,1,0:T(8,128)S(1)} %get-tuple-element.80), channel_id=1, source_target_pairs={{0,22},{2,20},{4,18},{6,16},{8,30},{10,28},{12,26},{14,24},{16,6},... | collective-permute-start | bytes 196616 | tf_op jit(solution)/shard_map/ppermute | solution.py:653
  43.1 14.4 %collective-permute-start.11 = (f32[16,8,128]{2,1,0:T(8,128)S(1)}, f32[16,8,128]{2,1,0:T(8,128)S(1)}, u32[]{:S(2)}, u32[]{:S(2)}) collective-permute-start(f32[16,8,128]{2,1,0:T(8,128)S(1)} %get-tuple-element.81), channel_id=1, source_target_pairs={{0,24},{2,26},{4,28},{6,30},{8,16},{10,18},{12,20},{14,22},{16,8},... | collective-permute-start | bytes 196616 | tf_op jit(solution)/shard_map/ppermute | solution.py:653
  43.1 17.7 %collective-permute-start.12 = (f32[16,8,128]{2,1,0:T(8,128)S(1)}, f32[16,8,128]{2,1,0:T(8,128)S(1)}, u32[]{:S(2)}, u32[]{:S(2)}) collective-permute-start(f32[16,8,128]{2,1,0:T(8,128)S(1)} %get-tuple-element.82), channel_id=1, source_target_pairs={{0,26},{2,24},{4,30},{6,28},{8,18},{10,16},{12,22},{14,20},{16,10}... | collective-permute-start | bytes 196616 | tf_op jit(solution)/shard_map/ppermute | solution.py:653
  45.1 16.6 %collective-permute-start.13 = (f32[16,8,128]{2,1,0:T(8,128)S(1)}, f32[16,8,128]{2,1,0:T(8,128)S(1)}, u32[]{:S(2)}, u32[]{:S(2)}) collective-permute-start(f32[16,8,128]{2,1,0:T(8,128)S(1)} %get-tuple-element.83), channel_id=1, source_target_pairs={{0,28},{2,30},{4,24},{6,26},{8,20},{10,22},{12,16},{14,18},{16,12}... | collective-permute-start | bytes 196616 | tf_op jit(solution)/shard_map/ppermute | solution.py:653
  49.5 15.4 %collective-permute-start.14 = (f32[16,8,128]{2,1,0:T(8,128)S(1)}, f32[16,8,128]{2,1,0:T(8,128)S(1)}, u32[]{:S(2)}, u32[]{:S(2)}) collective-permute-start(f32[16,8,128]{2,1,0:T(8,128)S(1)} %get-tuple-element.84), channel_id=1, source_target_pairs={{0,30},{2,28},{4,26},{6,24},{8,22},{10,20},{12,18},{14,16},{16,14}... | collective-permute-start | bytes 196616 | tf_op jit(solution)/shard_map/ppermute | solution.py:653
  53.3 15.0 %collective-permute-start.41 = (f32[16,8,128]{2,1,0:T(8,128)S(1)}, f32[16,8,128]{2,1,0:T(8,128)S(1)}, u32[]{:S(2)}, u32[]{:S(2)}) collective-permute-start(f32[16,8,128]{2,1,0:T(8,128)S(1)} %get-tuple-element.112), channel_id=1, source_target_pairs={{0,22},{2,20},{4,18},{6,16},{8,30},{10,28},{12,26},{14,24},{16,6},... | collective-permute-start | bytes 196616 | tf_op jit(solution)/shard_map/ppermute | solution.py:653
  57.6 10.6 %collective-permute-start.42 = (f32[16,8,128]{2,1,0:T(8,128)S(1)}, f32[16,8,128]{2,1,0:T(8,128)S(1)}, u32[]{:S(2)}, u32[]{:S(2)}) collective-permute-start(f32[16,8,128]{2,1,0:T(8,128)S(1)} %get-tuple-element.113), channel_id=1, source_target_pairs={{0,24},{2,26},{4,28},{6,30},{8,16},{10,18},{12,20},{14,22},{16,8},... | collective-permute-start | bytes 196616 | tf_op jit(solution)/shard_map/ppermute | solution.py:653
  72.3 29.1 %collective-permute-start.46 = (f32[8,2,16,8,128]{4,3,2,1,0:T(8,128)S(1)}, f32[8,2,16,8,128]{4,3,2,1,0:T(8,128)}, u32[]{:S(2)}, u32[]{:S(2)}) collective-permute-start(f32[8,2,16,8,128]{4,3,2,1,0:T(8,128)S(1)} %join.3.own), channel_id=1, source_target_pairs={{0,1},{1,0},{2,3},{3,2},{4,5},{5,4},{6,7},{7,6},{8,9},{9,8},{10,11... | collective-permute-start | bytes 3145736 | tf_op jit(solution)/shard_map/ppermute | solution.py:19
  103.6 31.2 %collective-permute-start.21 = (f32[16,8,128]{2,1,0:T(8,128)}, f32[16,8,128]{2,1,0:T(8,128)}, u32[]{:S(2)}, u32[]{:S(2)}) collective-permute-start(f32[16,8,128]{2,1,0:T(8,128)} %get-tuple-element.91), channel_id=1, source_target_pairs={{0,12},{2,14},{4,8},{6,10},{8,4},{10,6},{12,0},{14,2},{16,28},{18,... | collective-permute-start | bytes 196616 | tf_op jit(solution)/shard_map/ppermute | solution.py:653
  104.8 30.5 %collective-permute-start.22 = (f32[16,8,128]{2,1,0:T(8,128)}, f32[16,8,128]{2,1,0:T(8,128)}, u32[]{:S(2)}, u32[]{:S(2)}) collective-permute-start(f32[16,8,128]{2,1,0:T(8,128)} %get-tuple-element.92), channel_id=1, source_target_pairs={{0,14},{2,12},{4,10},{6,8},{8,6},{10,4},{12,2},{14,0},{16,30},{18,... | collective-permute-start | bytes 196616 | tf_op jit(solution)/shard_map/ppermute | solution.py:653
  107.3 29.8 %collective-permute-start.23 = (f32[16,8,128]{2,1,0:T(8,128)}, f32[16,8,128]{2,1,0:T(8,128)}, u32[]{:S(2)}, u32[]{:S(2)}) collective-permute-start(f32[16,8,128]{2,1,0:T(8,128)} %get-tuple-element.93), channel_id=1, source_target_pairs={{0,16},{2,18},{4,20},{6,22},{8,24},{10,26},{12,28},{14,30},{16,0},... | collective-permute-start | bytes 196616 | tf_op jit(solution)/shard_map/ppermute | solution.py:653
  108.1 30.4 %collective-permute-start.24 = (f32[16,8,128]{2,1,0:T(8,128)}, f32[16,8,128]{2,1,0:T(8,128)}, u32[]{:S(2)}, u32[]{:S(2)}) collective-permute-start(f32[16,8,128]{2,1,0:T(8,128)} %get-tuple-element.94), channel_id=1, source_target_pairs={{0,18},{2,16},{4,22},{6,20},{8,26},{10,24},{12,30},{14,28},{16,2},... | collective-permute-start | bytes 196616 | tf_op jit(solution)/shard_map/ppermute | solution.py:653
  110.4 29.7 %collective-permute-start.25 = (f32[16,8,128]{2,1,0:T(8,128)}, f32[16,8,128]{2,1,0:T(8,128)}, u32[]{:S(2)}, u32[]{:S(2)}) collective-permute-start(f32[16,8,128]{2,1,0:T(8,128)} %get-tuple-element.95), channel_id=1, source_target_pairs={{0,20},{2,22},{4,16},{6,18},{8,28},{10,30},{12,24},{14,26},{16,4},... | collective-permute-start | bytes 196616 | tf_op jit(solution)/shard_map/ppermute | solution.py:653
  140.3 10.2 %collective-permute-start.52 = (f32[16,8,128]{2,1,0:T(8,128)S(1)}, f32[16,8,128]{2,1,0:T(8,128)S(1)}, u32[]{:S(2)}, u32[]{:S(2)}) collective-permute-start(f32[16,8,128]{2,1,0:T(8,128)S(1)} %get-tuple-element.123), channel_id=1, source_target_pairs={{0,12},{2,14},{4,8},{6,10},{8,4},{10,6},{12,0},{14,2},{16,28},{18,... | collective-permute-start | bytes 196616 | tf_op jit(solution)/shard_map/ppermute | solution.py:653
  147.0 14.1 %collective-permute-start.56 = (f32[16,8,128]{2,1,0:T(8,128)S(1)}, f32[16,8,128]{2,1,0:T(8,128)S(1)}, u32[]{:S(2)}, u32[]{:S(2)}) collective-permute-start(f32[16,8,128]{2,1,0:T(8,128)S(1)} %get-tuple-element.127), channel_id=1, source_target_pairs={{0,20},{2,22},{4,16},{6,18},{8,28},{10,30},{12,24},{14,26},{16,4},... | collective-permute-start | bytes 196616 | tf_op jit(solution)/shard_map/ppermute | solution.py:653
  150.4 13.5 %collective-permute-start.57 = (f32[16,8,128]{2,1,0:T(8,128)S(1)}, f32[16,8,128]{2,1,0:T(8,128)S(1)}, u32[]{:S(2)}, u32[]{:S(2)}) collective-permute-start(f32[16,8,128]{2,1,0:T(8,128)S(1)} %get-tuple-element.128), channel_id=1, source_target_pairs={{0,22},{2,20},{4,18},{6,16},{8,30},{10,28},{12,26},{14,24},{16,6},... | collective-permute-start | bytes 196616 | tf_op jit(solution)/shard_map/ppermute | solution.py:653
  152.0 17.5 %collective-permute-start.58 = (f32[16,8,128]{2,1,0:T(8,128)S(1)}, f32[16,8,128]{2,1,0:T(8,128)S(1)}, u32[]{:S(2)}, u32[]{:S(2)}) collective-permute-start(f32[16,8,128]{2,1,0:T(8,128)S(1)} %get-tuple-element.129), channel_id=1, source_target_pairs={{0,24},{2,26},{4,28},{6,30},{8,16},{10,18},{12,20},{14,22},{16,8},... | collective-permute-start | bytes 196616 | tf_op jit(solution)/shard_map/ppermute | solution.py:653
  153.2 17.3 %collective-permute-start.59 = (f32[16,8,128]{2,1,0:T(8,128)S(1)}, f32[16,8,128]{2,1,0:T(8,128)S(1)}, u32[]{:S(2)}, u32[]{:S(2)}) collective-permute-start(f32[16,8,128]{2,1,0:T(8,128)S(1)} %get-tuple-element.130), channel_id=1, source_target_pairs={{0,26},{2,24},{4,30},{6,28},{8,18},{10,16},{12,22},{14,20},{16,10}... | collective-permute-start | bytes 196616 | tf_op jit(solution)/shard_map/ppermute | solution.py:653
  154.2 19.4 %collective-permute-start.60 = (f32[16,8,128]{2,1,0:T(8,128)S(1)}, f32[16,8,128]{2,1,0:T(8,128)S(1)}, u32[]{:S(2)}, u32[]{:S(2)}) collective-permute-start(f32[16,8,128]{2,1,0:T(8,128)S(1)} %get-tuple-element.131), channel_id=1, source_target_pairs={{0,28},{2,30},{4,24},{6,26},{8,20},{10,22},{12,16},{14,18},{16,12}... | collective-permute-start | bytes 196616 | tf_op jit(solution)/shard_map/ppermute | solution.py:653
  161.1 14.0 %collective-permute-start.61 = (f32[16,8,128]{2,1,0:T(8,128)S(1)}, f32[16,8,128]{2,1,0:T(8,128)S(1)}, u32[]{:S(2)}, u32[]{:S(2)}) collective-permute-start(f32[16,8,128]{2,1,0:T(8,128)S(1)} %get-tuple-element.132), channel_id=1, source_target_pairs={{0,30},{2,28},{4,26},{6,24},{8,22},{10,20},{12,18},{14,16},{16,14}... | collective-permute-start | bytes 196616 | tf_op jit(solution)/shard_map/ppermute | solution.py:653
  164.0 18.1 %collective-permute-start.26 = (f32[16,8,128]{2,1,0:T(8,128)S(1)}, f32[16,8,128]{2,1,0:T(8,128)S(1)}, u32[]{:S(2)}, u32[]{:S(2)}) collective-permute-start(f32[16,8,128]{2,1,0:T(8,128)S(1)} %copy-done.19), channel_id=1, source_target_pairs={{0,22},{2,20},{4,18},{6,16},{8,30},{10,28},{12,26},{14,24},{16,6},... | collective-permute-start | bytes 196616 | tf_op jit(solution)/shard_map/ppermute | solution.py:653
  169.5 12.6 %collective-permute-start.27 = (f32[16,8,128]{2,1,0:T(8,128)S(1)}, f32[16,8,128]{2,1,0:T(8,128)S(1)}, u32[]{:S(2)}, u32[]{:S(2)}) collective-permute-start(f32[16,8,128]{2,1,0:T(8,128)S(1)} %copy-done.17), channel_id=1, source_target_pairs={{0,24},{2,26},{4,28},{6,30},{8,16},{10,18},{12,20},{14,22},{16,8},... | collective-permute-start | bytes 196616 | tf_op jit(solution)/shard_map/ppermute | solution.py:653
  170.5 11.6 %collective-permute-start.28 = (f32[16,8,128]{2,1,0:T(8,128)S(1)}, f32[16,8,128]{2,1,0:T(8,128)S(1)}, u32[]{:S(2)}, u32[]{:S(2)}) collective-permute-start(f32[16,8,128]{2,1,0:T(8,128)S(1)} %copy-done.15), channel_id=1, source_target_pairs={{0,26},{2,24},{4,30},{6,28},{8,18},{10,16},{12,22},{14,20},{16,10}... | collective-permute-start | bytes 196616 | tf_op jit(solution)/shard_map/ppermute | solution.py:653
  (52 other events, 630.6 us)

commit v3 on v1

--- a/solution.py
+++ b/solution.py
@@ -3,6 +3,7 @@
 
 import jax
 import jax.numpy as jnp
+import ml_dtypes
 import numpy as np
 from jax import lax
 from jax.experimental import pallas as pl
@@ -230,6 +231,18 @@
     return np.array(one), two, lengths
 
 
+def in_two_parts(table):
+    high = table.astype(ml_dtypes.bfloat16)
+    low = (table - high.astype(np.float32)).astype(ml_dtypes.bfloat16)
+    return high, low
+
+
+def first_weights():
+    table = lagrange_table(16).astype(np.float32)
+    high, low = in_two_parts(np.kron(table, np.eye(8, dtype=np.float32)))
+    return np.concatenate([high, low])
+
+
 def second_weights():
     table = lagrange_table(16)
     result = np.zeros((8, 4, 32, 4, 4, 32), np.float32)
@@ -241,14 +254,7 @@
                     for out_b in range(4):
                         weight = table[4 * out_b + out_a, half * 16 + 4 * b + a]
                         result[half * 4 + a, b, :, out_a, out_b, :] = np.float32(weight) * same
-    return result.reshape(8, 128, 512)
-
-
-def folded_table():
-    table = lagrange_table(16)[:, :16]
-    even = (table[:8] + table[::-1][:8]) / 2
-    odd = (table[:8] - table[::-1][:8]) / 2
-    return even, odd
+    return np.stack(in_two_parts(result.reshape(4, 256, 512)))
 
 
 def turn(phase):
@@ -279,17 +285,21 @@
     return full
 
 
-def pack_kernel(in_ref, out_ref):
+def pack_rows(in_ref, lanes, tiles):
     upper = lax.broadcasted_iota(jnp.int32, (8, 128), 0) < 4
     for t1 in range(16):
         groups = [None] * 4
         for high in range(2):
-            real = in_ref[0, t1, 8 * high : 8 * high + 8, :]
-            imag = in_ref[1, t1, 8 * high : 8 * high + 8, :]
+            real = in_ref[0, t1, 8 * high : 8 * high + 8, lanes]
+            imag = in_ref[1, t1, 8 * high : 8 * high + 8, lanes]
             groups[2 * high] = jnp.where(upper, real, pltpu.roll(imag, 4, 0))
             groups[2 * high + 1] = jnp.where(upper, pltpu.roll(real, 4, 0), imag)
         for j, tile in enumerate(swap_lanes(groups)):
-            out_ref[j, t1] = tile
+            tiles[j, t1] = tile
+
+
+def pack_kernel(in_ref, out_ref):
+    pack_rows(in_ref, slice(None), out_ref)
 
 
 def pack(weights, chunk):
@@ -304,37 +314,121 @@
     )(weights)
 
 
+def pack_masks_kernel(ids, in_ref, *refs):
+    outs, tiles = refs[:4], refs[4]
+    me = ids[0]
+
+    def step(mz, carry):
+        group = mz ^ (me // 4)
+        pack_rows(in_ref, pl.ds(pl.multiple_of(group * 128, 128), 128), tiles)
+        for mxy in range(4):
+            outs[mxy][mz] = tiles[mxy ^ (me % 4)]
+        return carry
+
+    lax.fori_loop(0, 4, step, 0)
+
+
+BUNDLE = (4, 16, 8, 128)
+
+
+def pack_masks(weights, ids, chunk):
+    return pl.pallas_call(
+        pack_masks_kernel,
+        grid=(1,),
+        in_specs=[
+            pl.BlockSpec(memory_space=pltpu.SMEM),
+            pl.BlockSpec((2, 16, 16, 512), lambda i: (0, 0, 0, chunk)),
+        ],
+        out_specs=[pl.BlockSpec(BUNDLE, lambda i: (0, 0, 0, 0))] * 4,
+        out_shape=[jax.ShapeDtypeStruct(BUNDLE, jnp.float32)] * 4,
+        scratch_shapes=[pltpu.VMEM(BUNDLE, jnp.float32)],
+        compiler_params=pltpu.CompilerParams(vmem_limit_bytes=VMEM_LIMIT),
+        cost_estimate=pl.CostEstimate(flops=10**6, bytes_accessed=2**21, transcendentals=0),
+        name="pack_masks",
+    )(ids, weights)
+
+
+def regroup_kernel(*refs):
+    for first in range(4):
+        for second in range(4):
+            refs[4 + second][first] = refs[first][second]
+
+
+def regroup(bundles):
+    in_vmem = pl.BlockSpec(memory_space=pltpu.VMEM)
+    return pl.pallas_call(
+        regroup_kernel,
+        in_specs=[in_vmem] * 4,
+        out_specs=[in_vmem] * 4,
+        out_shape=[jax.ShapeDtypeStruct(BUNDLE, jnp.float32)] * 4,
+        compiler_params=pltpu.CompilerParams(vmem_limit_bytes=VMEM_LIMIT),
+        cost_estimate=pl.CostEstimate(flops=10**5, bytes_accessed=2**21, transcendentals=0),
+        name="regroup",
+    )(*bundles)
+
+
+def exchange(bundles, unit):
+    moved = [bundles[0]]
+    for mask in range(1, 4):
+        pairs = [(source, source ^ (mask * unit)) for source in range(PIECES)]
+        moved.append(lax.ppermute(bundles[mask], ("bx", "by"), pairs))
+    return moved
+
+
+def merge_halves(out_ref, box, t1, low, high):
+    upper = lax.broadcasted_iota(jnp.int32, (8, 128), 0) < 4
+    out_ref[box, 0, t1] = jnp.where(upper, low, pltpu.roll(high, 4, 0))
+    out_ref[box, 1, t1] = jnp.where(upper, pltpu.roll(low, 4, 0), high)
+
+
 def join_kernel(in_ref, out_ref):
-    upper = lax.broadcasted_iota(jnp.int32, (8, 128), 0) < 4
-
     def step(box, carry):
         for t1 in range(16):
-            low = in_ref[2 * box, t1]
-            high = in_ref[2 * box + 1, t1]
-            out_ref[box, 0, t1] = jnp.where(upper, low, pltpu.roll(high, 4, 0))
-            out_ref[box, 1, t1] = jnp.where(upper, pltpu.roll(low, 4, 0), high)
+            merge_halves(out_ref, box, t1, in_ref[2 * box, t1], in_ref[2 * box + 1, t1])
         return carry
 
     lax.fori_loop(0, 8, step, 0)
 
 
-def join(received):
+def join_masks_kernel(ids, *refs):
+    bundles, out_ref = refs[:4], refs[4]
+    me = ids[0]
+    is_low = jnp.broadcast_to(me % 2, (8, 128)) == 0
+    for mz in range(4):
+        for mx in range(2):
+            box = (2 * mz + mx) ^ (me // 2)
+            for t1 in range(16):
+                mine = bundles[mz][2 * mx, t1]
+                partner = bundles[mz][2 * mx + 1, t1]
+                low = jnp.where(is_low, mine, partner)
+                high = jnp.where(is_low, partner, mine)
+                merge_halves(out_ref, box, t1, low, high)
+
+
+def join(received, ids=None):
+    in_vmem = pl.BlockSpec(memory_space=pltpu.VMEM)
+    if ids is None:
+        kernel, operands, in_specs = join_kernel, [received], [in_vmem]
+    else:
+        kernel, operands = join_masks_kernel, [ids, *received]
+        in_specs = [pl.BlockSpec(memory_space=pltpu.SMEM)] + [in_vmem] * 4
     return pl.pallas_call(
-        join_kernel,
-        in_specs=[pl.BlockSpec(memory_space=pltpu.VMEM)],
-        out_specs=pl.BlockSpec(memory_space=pltpu.VMEM),
+        kernel,
+        in_specs=in_specs,
+        out_specs=in_vmem,
         out_shape=jax.ShapeDtypeStruct((8, 2, 16, 8, 128), jnp.float32),
         compiler_params=pltpu.CompilerParams(vmem_limit_bytes=VMEM_LIMIT),
         cost_estimate=pl.CostEstimate(flops=10**6, bytes_accessed=2**21, transcendentals=0),
         name="join",
-    )(received)
+    )(*operands)
 
 
 def levels_kernel(
-    chunk, ids, nodes, own, other, speeds, waves, lengths, last_one, last_two, last_lengths,
-    weights, out, boxes_a, boxes_b, sums, turned, mixed,
+    chunk, by_masks, ids, nodes, own, other, speeds, waves, lengths, last_one, last_two,
+    last_lengths, first_table, second_table, *refs,
 ):
-    even, odd = folded_table()
+    outs = refs[:4] if by_masks else refs[0]
+    boxes_a, boxes_b, sums, turned, mixed, last_phase = refs[-6:]
     row = (chunk * PIECES + ids[0]).astype(jnp.float32)
     core = ids[1]
     core_float = core.astype(jnp.float32)
@@ -351,92 +445,75 @@
     def speed_row(level_index, low_code):
         return jnp.broadcast_to(speeds[pl.ds(2**level_index - 1 + low_code, 1), :], (8, 128))
 
-    def blend(copies, target, boxes):
-        for i_half in range(2):
-            totals = {}
-            for parity, table in ((0, even), (1, odd)):
-                for j in range(16):
-                    piece = sums[parity, j, :copies]
-                    for i in range(4 * i_half, 4 * i_half + 4):
-                        term = piece * float(table[i, j])
-                        key = (parity, i)
-                        totals[key] = term if j == 0 else totals[key] + term
-            for i in range(4 * i_half, 4 * i_half + 4):
-                plus = totals[0, i] + totals[1, i]
-                minus = totals[0, i] - totals[1, i]
-                for n, box in enumerate(boxes):
-                    for part in range(2):
-                        target[box, part, i] = plus[2 * n + part]
-                        target[box, part, 15 - i] = minus[2 * n + part]
-
-    sign = 1.0 - 2.0 * core_float
-
-    def first_level(box, carry):
+    def blend(slot, target, boxes):
+        rows = sums[slot].astype(jnp.bfloat16)
+        both = jnp.dot(first_table[...], rows, preferred_element_type=jnp.float32)
+        total = both[:128] + both[128:]
+        for n, box in enumerate(boxes):
+            for part in range(2):
+                column = 128 * (2 * n + part)
+                target[box, part] = total[:, column : column + 128].reshape(16, 8, 128)
+
+    def put(slot, first_row, column, real, imag):
+        sums[slot, pl.ds(first_row, 8), 256 * column : 256 * column + 128] = real
+        sums[slot, pl.ds(first_row, 8), 256 * column + 128 : 256 * column + 256] = imag
+
+    def first_level(pair, slot):
         point = first_point(0, 0.0)
         speed = speed_row(0, 0)
-        for j in range(16):
-            own_node = jnp.where(core == 0, j, 15 - j)
-            pieces = []
-            for source, node, box_code in (
-                (own, own_node, 2 * box + core),
-                (other, 15 - own_node, 2 * box + 1 - core),
-            ):
-                entry = box_code * 16 + node
-                phase = (point * nodes[entry] + second_phase) + speed * lengths[entry]
-                cosine, sine = turn(phase)
-                real = source[box, 0, node]
-                imag = source[box, 1, node]
-                pieces.append((real * cosine + imag * sine, imag * cosine - real * sine))
-            for part in range(2):
-                sums[0, j, part] = pieces[0][part] + pieces[1][part]
-                sums[1, j, part] = (pieces[0][part] - pieces[1][part]) * sign
-        blend(2, boxes_a, [box])
-        return carry
-
-    lax.fori_loop(0, 8, first_level, 0)
-
-    def later_level(level_index, source, target):
+        for n in range(2):
+            box = 2 * pair + n
+            for source, child in ((own, core), (other, 1 - core)):
+                for t1 in range(16):
+                    entry = (2 * box + child) * 16 + t1
+                    phase = (point * nodes[entry] + second_phase) + speed * lengths[entry]
+                    cosine, sine = turn(phase)
+                    real = source[box, 0, t1]
+                    imag = source[box, 1, t1]
+                    first_row = pl.multiple_of(child * 128 + 8 * t1, 8)
+                    put(slot, first_row, n, real * cosine + imag * sine, imag * cosine - real * sine)
+        blend(slot, boxes_a, [2 * pair, 2 * pair + 1])
+
+    def later_level(level_index, source, target, index, slot):
         low_bits = level_index - 1
         stride = 2**low_bits
-
-        def group(index, carry):
-            parent = index // stride
-            low = index % stride
-            code = 0
-            for bit in range(low_bits):
-                code = code + low // 2**bit % 2 * 2 ** (low_bits - 1 - bit)
-            code = jnp.int32(0) + code
-            before = first_point(level_index - 1, code.astype(jnp.float32))
-            before_speed = speed_row(level_index - 1, code)
-            points = [first_point(level_index, (2 * code + b).astype(jnp.float32)) for b in range(2)]
-            point_speeds = [speed_row(level_index, 2 * code + b) for b in range(2)]
-            first_box = parent * (2 * stride) + low
-            for j in range(16):
-                pieces = []
-                for child in range(2):
-                    node = j if child == 0 else 15 - j
-                    entry = LEVEL_ROWS[level_index] + (2 * parent + child) * 16 + node
-                    length = lengths[entry]
-                    wave = nodes[entry]
-                    real = source[first_box + child * stride, 0, node]
-                    imag = source[first_box + child * stride, 1, node]
-                    old = (before * wave + second_phase) + before_speed * length
-                    for b in range(2):
-                        new = (points[b] * wave + second_phase) + point_speeds[b] * length
-                        cosine, sine = turn(new - old)
-                        pieces.append((real * cosine + imag * sine, imag * cosine - real * sine))
+        parent = index // stride
+        low = index % stride
+        code = jnp.int32(0)
+        for bit in range(low_bits):
+            code = code + low // 2**bit % 2 * 2 ** (low_bits - 1 - bit)
+        before = first_point(level_index - 1, code.astype(jnp.float32))
+        before_speed = speed_row(level_index - 1, code)
+        points = [first_point(level_index, (2 * code + b).astype(jnp.float32)) for b in range(2)]
+        point_speeds = [speed_row(level_index, 2 * code + b) for b in range(2)]
+        first_box = parent * (2 * stride) + low
+        for child in range(2):
+            for t1 in range(16):
+                entry = LEVEL_ROWS[level_index] + (2 * parent + child) * 16 + t1
+                length = lengths[entry]
+                wave = nodes[entry]
+                real = source[first_box + child * stride, 0, t1]
+                imag = source[first_box + child * stride, 1, t1]
+                old = (before * wave + second_phase) + before_speed * length
                 for b in range(2):
-                    for part in range(2):
-                        sums[0, j, 2 * b + part] = pieces[b][part] + pieces[2 + b][part]
-                        sums[1, j, 2 * b + part] = pieces[b][part] - pieces[2 + b][part]
-            blend(4, target, [first_box, first_box + stride])
+                    new = (points[b] * wave + second_phase) + point_speeds[b] * length
+                    cosine, sine = turn(new - old)
+                    first_row = child * 128 + 8 * t1
+                    put(slot, first_row, b, real * cosine + imag * sine, imag * cosine - real * sine)
+        blend(slot, target, [first_box, first_box + stride])
+
+    def in_pairs(one):
+        def step(half, carry):
+            for slot in range(2):
+                one(2 * half + slot, slot)
             return carry
 
-        lax.fori_loop(0, 4, group, 0)
-
-    later_level(1, boxes_a, boxes_b)
-    later_level(2, boxes_b, boxes_a)
-    later_level(3, boxes_a, boxes_b)
+        lax.fori_loop(0, 2, step, 0)
+
+    in_pairs(first_level)
+    in_pairs(partial(later_level, 1, boxes_a, boxes_b))
+    in_pairs(partial(later_level, 2, boxes_b, boxes_a))
+    in_pairs(partial(later_level, 3, boxes_a, boxes_b))
 
     fine_two = [((lane % 32).astype(jnp.float32) * 2.0 + (e + 0.5)) * (1.0 / 64) for e in range(2)]
     fine_phase = [fine_two[e] * wave_two for e in range(2)]
@@ -462,101 +539,143 @@
             for e in range(2):
                 new = (across + fine_phase[e]) + new_speeds[e] * length
                 cosine, sine = turn(new - old)
-                first = pl.multiple_of((box * 32 + t1) * 8, 8)
-                turned[e, pl.ds(first, 8), :] = real * cosine + imag * sine
-                turned[e, pl.ds(first + 128, 8), :] = imag * cosine - real * sine
+                first = pl.multiple_of((e * 256 + box * 32 + t1) * 8, 8)
+                turned[pl.ds(first, 8), :] = real * cosine + imag * sine
+                turned[pl.ds(first + 128, 8), :] = imag * cosine - real * sine
         return carry
 
     lax.fori_loop(0, 8, rotate_box, 0)
 
     for e in range(2):
-        total = None
-        for j in range(8):
-            rows = turned[e, pl.ds(j, 256, stride=8), :]
-            term = jnp.dot(
-                rows, weights[j], preferred_element_type=jnp.float32, precision=lax.Precision.HIGHEST
-            )
+        for a in range(4):
+            last_phase[e, a] = fine_two[e] * last_two[a]
+
+    total = None
+    for j in range(4):
+        rows = jnp.concatenate(
+            [turned[pl.ds(2 * j + k, 512, stride=8), :] for k in range(2)], axis=1
+        ).astype(jnp.bfloat16)
+        for part in range(2):
+            term = jnp.dot(rows, second_table[part, j], preferred_element_type=jnp.float32)
             total = term if total is None else total + term
-        mixed[e] = total
-
-    last_phase = [[fine_two[e] * last_two[a] for a in range(4)] for e in range(2)]
-
-    def finish_box(box, carry):
+    mixed[...] = total
+
+    def finish_box(target, out):
+        box, e = target // 2, target % 2
         code = reversed_code(box)
         point = first_point(3, code.astype(jnp.float32))
-        for e in range(2):
-            speed = fine_speed(code, e)
-            for high in range(2):
-                across = point * last_one[high]
-                first = pl.multiple_of(box * 32 + high * 8, 8)
-                for a in range(4):
-                    phase = (across + last_phase[e][a]) + speed * last_lengths[high, a]
-                    cosine, sine = turn(phase)
-                    real = mixed[e, pl.ds(first, 8), 128 * a : 128 * a + 128]
-                    imag = mixed[e, pl.ds(first + 16, 8), 128 * a : 128 * a + 128]
-                    out[2 * box + e, high * 4 + a] = real * cosine - imag * sine
-                    out[2 * box + e, 8 + high * 4 + a] = real * sine + imag * cosine
+        speed = fine_speed(code, e)
+        for high in range(2):
+            across = point * last_one[high]
+            first = pl.multiple_of(e * 256 + box * 32 + high * 8, 8)
+            for a in range(4):
+                phase = (across + last_phase[e, a]) + speed * last_lengths[high, a]
+                cosine, sine = turn(phase)
+                real = mixed[pl.ds(first, 8), 128 * a : 128 * a + 128]
+                imag = mixed[pl.ds(first + 16, 8), 128 * a : 128 * a + 128]
+                out[high * 4 + a] = real * cosine - imag * sine
+                out[8 + high * 4 + a] = real * sine + imag * cosine
+
+    def finish_row(major, carry):
+        for minor in range(4):
+            if by_masks:
+                finish_box((4 * minor + major) ^ ids[0], outs[minor].at[major])
+            else:
+                finish_box(4 * major + minor, outs.at[4 * major + minor])
         return carry
 
-    lax.fori_loop(0, 8, finish_box, 0)
-
-
-def levels(chunk, ids, own, other, speeds):
+    lax.fori_loop(0, 4, finish_row, 0)
+
+
+def levels(chunk, by_masks, ids, own, other, speeds):
     nodes, waves, lengths = node_tables()
     last_one, last_two, last_lengths = final_tables()
+    tables = (waves, lengths, last_one, last_two, last_lengths, first_weights(), second_weights())
     in_vmem = pl.BlockSpec(memory_space=pltpu.VMEM)
     in_smem = pl.BlockSpec(memory_space=pltpu.SMEM)
+    if by_masks:
+        out_shape = [jax.ShapeDtypeStruct(BUNDLE, jnp.float32)] * 4
+        out_specs = [in_vmem] * 4
+    else:
+        out_shape = jax.ShapeDtypeStruct((PIECES, 16, 8, 128), jnp.float32)
+        out_specs = in_vmem
     return pl.pallas_call(
-        partial(levels_kernel, chunk),
-        in_specs=[in_smem, in_smem] + [in_vmem] * 9,
-        out_specs=in_vmem,
-        out_shape=jax.ShapeDtypeStruct((PIECES, 16, 8, 128), jnp.float32),
+        partial(levels_kernel, chunk, by_masks),
+        in_specs=[in_smem, in_smem] + [in_vmem] * 10,
+        out_specs=out_specs,
+        out_shape=out_shape,
         scratch_shapes=[
             pltpu.VMEM((8, 2, 16, 8, 128), jnp.float32),
             pltpu.VMEM((8, 2, 16, 8, 128), jnp.float32),
-            pltpu.VMEM((2, 16, 4, 8, 128), jnp.float32),
-            pltpu.VMEM((2, 2048, 128), jnp.float32),
             pltpu.VMEM((2, 256, 512), jnp.float32),
+            pltpu.VMEM((4096, 128), jnp.float32),
+            pltpu.VMEM((512, 512), jnp.float32),
+            pltpu.VMEM((2, 4, 8, 128), jnp.float32),
         ],
         compiler_params=pltpu.CompilerParams(vmem_limit_bytes=VMEM_LIMIT),
         cost_estimate=pl.CostEstimate(flops=10**8, bytes_accessed=2**23, transcendentals=0),
         name="levels",
-    )(
-        ids, jnp.asarray(nodes), own, other, speeds, jnp.asarray(waves), jnp.asarray(lengths),
-        jnp.asarray(last_one), jnp.asarray(last_two), jnp.asarray(last_lengths),
-        jnp.asarray(second_weights()),
-    )
-
-
-def unpack_kernel(*refs):
-    in_ref, out_ref, rows = refs[0], refs[-2], refs[-1]
+    )(ids, jnp.asarray(nodes), own, other, speeds, *[jnp.asarray(table) for table in tables])
+
+
+def unpack_rows(tiles, rows, out_ref, lanes):
     for part in range(2):
         for high in range(2):
+            block = part * 2 + high
             for a in range(4):
-                tiles = [in_ref[j, part * 8 + high * 4 + a] for j in range(4)]
-                for b, tile in enumerate(swap_lanes(tiles)):
+                values = [tiles[j, part * 8 + high * 4 + a] for j in range(4)]
+                for b, tile in enumerate(swap_lanes(values)):
                     t2 = 4 * b + a
-                    rows[part * 2 + high, 8 * t2 : 8 * t2 + 8, :] = tile
+                    rows[block, 8 * t2 : 8 * t2 + 8, :] = tile
             for t1 in range(8):
-                out_ref[part, high * 8 + t1] = rows[part * 2 + high, pl.ds(t1, 16, stride=8), :]
-
-
-def unpack(received, chunk, earlier):
-    operands = [received]
-    in_specs = [pl.BlockSpec((4, 16, 8, 128), lambda i: (i, 0, 0, 0))]
+                out_ref[part, high * 8 + t1, :, lanes] = rows[block, pl.ds(t1, 16, stride=8), :]
+
+
+def unpack_kernel(*refs):
+    unpack_rows(refs[0], refs[-1], refs[-2], slice(None))
+
+
+def unpack_masks_kernel(ids, *refs):
+    bundles, out_ref, tiles, rows = refs[:4], refs[-3], refs[-2], refs[-1]
+    me = ids[0]
+
+    def step(mz, carry):
+        group = mz ^ (me // 4)
+        for mxy in range(4):
+            tiles[mxy ^ (me % 4)] = bundles[mxy][mz]
+        unpack_rows(tiles, rows, out_ref, pl.ds(pl.multiple_of(group * 128, 128), 128))
+        return carry
+
+    lax.fori_loop(0, 4, step, 0)
+
+
+def unpack(received, chunk, earlier, ids=None):
+    rows = pltpu.VMEM((4, 128, 128), jnp.float32)
+    if ids is None:
+        kernel, operands, grid = unpack_kernel, [received], (4,)
+        in_specs = [pl.BlockSpec((4, 16, 8, 128), lambda i: (i, 0, 0, 0))]
+        out_spec = pl.BlockSpec((2, 16, 16, 128), lambda i: (0, 0, 0, 4 * chunk + i))
+        scratch = [rows]
+    else:
+        kernel, operands, grid = unpack_masks_kernel, [ids, *received], (1,)
+        in_specs = [pl.BlockSpec(memory_space=pltpu.SMEM)]
+        in_specs += [pl.BlockSpec(BUNDLE, lambda i: (0, 0, 0, 0))] * 4
+        out_spec = pl.BlockSpec((2, 16, 16, 512), lambda i: (0, 0, 0, chunk))
+        scratch = [pltpu.VMEM(BUNDLE, jnp.float32), rows]
     aliases = {}
     if earlier is not None:
+        aliases = {len(operands): 0}
         operands.append(earlier)
         in_specs.append(pl.BlockSpec(memory_space=pl.ANY))
-        aliases = {1: 0}
     return pl.pallas_call(
-        unpack_kernel,
-        grid=(4,),
+        kernel,
+        grid=grid,
         in_specs=in_specs,
-        out_specs=pl.BlockSpec((2, 16, 16, 128), lambda i: (0, 0, 0, 4 * chunk + i)),
+        out_specs=out_spec,
         out_shape=jax.ShapeDtypeStruct((2, 16, 16, 1024), jnp.float32),
-        scratch_shapes=[pltpu.VMEM((4, 128, 128), jnp.float32)],
+        scratch_shapes=scratch,
         input_output_aliases=aliases,
+        compiler_params=pltpu.CompilerParams(vmem_limit_bytes=VMEM_LIMIT),
         cost_estimate=pl.CostEstimate(flops=10**6, bytes_accessed=2**21, transcendentals=0),
         name="unpack",
     )(*operands)
@@ -593,17 +712,22 @@
     me = lax.axis_index("bx") * 2 + lax.axis_index("by")
     ids = jnp.stack([me, core]).astype(jnp.int32)
     speeds = speed_tables(speed_modes, core)
-    received = []
-    for chunk in range(CHUNKS):
-        received.append(deal(pack(local, chunk)))
-    results = []
-    for chunk in range(CHUNKS):
-        own = join(received[chunk])
-        other = partner_2(own, "cores", 0)
-        results.append(deal(levels(chunk, ids, own, other, speeds[chunk])))
-    out = None
-    for chunk in range(CHUNKS):
-        out = unpack(results[chunk], chunk, out)
+
+    first = deal(pack(local, 0))
+    near = exchange(pack_masks(local, ids, 1), 1)
+    second = exchange(regroup(near), 4)
+
+    own = join(first)
+    result = levels(0, True, ids, own, partner_2(own, "cores", 0), speeds[0])
+    far = exchange(result, 4)
+    back_first = exchange(regroup(far), 1)
+
+    own = join(second, ids)
+    result = levels(1, False, ids, own, partner_2(own, "cores", 0), speeds[1])
+    back_second = deal(result)
+
+    out = unpack(back_first, 0, None, ids)
+    out = unpack(back_second, 1, out)
     return out.reshape(weights.shape)
 
 

time: 138 us -> 152 us (1.10)
  waiting for transfers between devices: 49.5 us -> 81.3 us
  Pallas kernels: 58 us -> 37.5 us
  starting transfers between devices: 24.4 us -> 29.7 us
  local copies, waits for them, and re-layouts: 3.88 us -> 1.67 us
    ppermute x0 -> x12, waiting for transfers between devices: none -> 77 us  [exchange(): moved.append(lax.ppermute(bundles[mask], ('bx', 'by'), pairs))]
    all_to_all x4 -> x2, waiting for transfers between devices: 45.4 us -> 0.01 us  [deal(): return lax.all_to_all(pieces, ('bx', 'by'), 0, 0, tiled=True)]
    ppermute x0 -> x12, starting transfers between devices: none -> 16.8 us  [exchange(): moved.append(lax.ppermute(bundles[mask], ('bx', 'by'), pairs))]
    pallas_call x6 -> x9, Pallas kernels: 50.2 us -> 33.5 us  [the longest x2 23.8 us: levels(): pl.pallas_call(partial(levels_kernel, chunk, by_masks), in_specs=[in_smem...]
    all_to_all x4 -> x2, starting transfers between devices: 24.3 us -> 12.8 us  [deal(): return lax.all_to_all(pieces, ('bx', 'by'), 0, 0, tiled=True)]
    pallas_call x2 -> x1, Pallas kernels: 7.72 us -> 4 us  [pack(): pl.pallas_call(pack_kernel, grid=(4,), in_specs=[pl.BlockSpec((2, 16, 16,...]
    unnamed x26 -> x24, local copies, waits for them, and re-layouts: 3.25 us -> 1.04 us
  transfers between devices with their start and end apart: 6 -> 16, of which waited for: 5 -> 14; matrix products, arithmetic and copies ran while one was open for 1% -> 1% of each run, Pallas kernels for 37% -> 21%
where the time goes in v3:
time: 152 us; the launch traced here: 151 us
  waiting for transfers between devices  81.3 us (53%)
  Pallas kernels  37.5 us (25%)
  starting transfers between devices  29.7 us (20%)
  local copies, waits for them, and re-layouts  1.67 us (1%)
    ppermute x12, waiting for transfers between devices, exchange(): moved.append(lax.ppermute(bundles[mask], ('bx', 'by'), pairs))  77 us
    pallas_call x2, Pallas kernels, levels(): pl.pallas_call(partial(levels_kernel, chunk, by_masks), in_specs=[in_smem...  23.8 us
    ppermute x12, starting transfers between devices, exchange(): moved.append(lax.ppermute(bundles[mask], ('bx', 'by'), pairs))  16.8 us
    all_to_all x2, starting transfers between devices, deal(): return lax.all_to_all(pieces, ('bx', 'by'), 0, 0, tiled=True)  12.8 us
    pallas_call x2, Pallas kernels, unpack(): pl.pallas_call(kernel, grid=grid, in_specs=in_specs, out_specs=out_spec,...  4.94 us
    ppermute x2, waiting for transfers between devices, partner_2(): return lax.ppermute(value, axis, pairs)  4.33 us
    pallas_call x1, Pallas kernels, pack(): pl.pallas_call(pack_kernel, grid=(4,), in_specs=[pl.BlockSpec((2, 16, 16,...  4 us
  transfers between devices with their start and end apart: 16, of which 14 were waited for; matrix products, arithmetic and copies ran while one was open for 1% of the time, Pallas kernels for 21%

profile of v3, /device:TPU:10, one launch (start us, length us, event | category | flops | bytes accessed | tf_op | source)
XLA Modules:
  0.0 151.3 jit_solution(17745449651593236135)
XLA Ops:
  0.0 4.0 %pack.1 = f32[16,16,8,128]{3,2,1,0:T(8,128)} custom-call(f32[2,16,16,1024]{3,2,1,0:T(8,128)} %bitcast.30), custom_call_target="tpu_custom_call" | custom-call | flops 1000000 | bytes 2097152 | tf_op jit(solution)/shard_map/pack/pallas_call | solution.py:306
  4.0 7.2 %all-to-all-start.1 = ((f32[16,16,8,128]{3,2,1,0:T(8,128)}), f32[16,16,8,128]{3,2,1,0:T(8,128)}, u32[]{:S(2)}, u32[]{:S(2)}) async-start(f32[16,16,8,128]{3,2,1,0:T(8,128)} %pack.1), calls=%async_computation.1 | async-start | bytes 2097152 | tf_op jit(solution)/shard_map/all_to_all | solution.py:735
  11.3 1.7 %pack_masks.1 = (f32[4,16,8,128]{3,2,1,0:T(8,128)S(1)}, f32[4,16,8,128]{3,2,1,0:T(8,128)S(1)}, f32[4,16,8,128]{3,2,1,0:T(8,128)S(1)}, f32[4,16,8,128]{3,2,1,0:T(8,128)S(1)}) custom-call(s32[2]{0:T(128)S(1)} %pad_add_fusion.ids, f32[2,16,16,1024]{3,2,1,0:T(8,128)S(1)} %bitcast.31), custom_call_target="tpu_custom_call" | custom-call | flops 1000000 | bytes 2097152 | tf_op jit(solution)/shard_map/pack_masks/pallas_call | solution.py:335
  13.1 1.5 %collective-permute-start = (f32[4,16,8,128]{3,2,1,0:T(8,128)S(1)}, f32[4,16,8,128]{3,2,1,0:T(8,128)S(1)}, u32[]{:S(2)}, u32[]{:S(2)}) collective-permute-start(f32[4,16,8,128]{3,2,1,0:T(8,128)S(1)} %get-tuple-element.22), channel_id=1, source_target_pairs={{0,2},{2,0},{4,6},{6,4},{8,10},{10,8},{12,14},{14,12},{16,18},{18,... | collective-permute-start | bytes 786440 | tf_op jit(solution)/shard_map/ppermute | solution.py:374
  15.2 1.5 collective-permute-start.2
  16.6 6.2 %collective-permute-done.refs_1_ = f32[4,16,8,128]{3,2,1,0:T(8,128)S(1)} collective-permute-done((f32[4,16,8,128]{3,2,1,0:T(8,128)S(1)}, f32[4,16,8,128]{3,2,1,0:T(8,128)S(1)}, u32[]{:S(2)}, u32[]{:S(2)}) %collective-permute-start) | collective-permute-done | bytes 262176 | tf_op jit(solution)/shard_map/ppermute | solution.py:374
  22.8 4.3 %collective-permute-done.1.refs_2_ = f32[4,16,8,128]{3,2,1,0:T(8,128)S(1)} collective-permute-done((f32[4,16,8,128]{3,2,1,0:T(8,128)S(1)}, f32[4,16,8,128]{3,2,1,0:T(8,128)S(1)}, u32[]{:S(2)}, u32[]{:S(2)}) %collective-permute-start.1) | collective-permute-done | bytes 262176 | tf_op jit(solution)/shard_map/ppermute | solution.py:374
  27.1 7.9 %collective-permute-done.2.refs_3_ = f32[4,16,8,128]{3,2,1,0:T(8,128)S(1)} collective-permute-done((f32[4,16,8,128]{3,2,1,0:T(8,128)S(1)}, f32[4,16,8,128]{3,2,1,0:T(8,128)S(1)}, u32[]{:S(2)}, u32[]{:S(2)}) %collective-permute-start.2) | collective-permute-done | bytes 262176 | tf_op jit(solution)/shard_map/ppermute | solution.py:374
  35.1 2.5 %collective-permute-start.3 = (f32[4,16,8,128]{3,2,1,0:T(8,128)S(1)}, f32[4,16,8,128]{3,2,1,0:T(8,128)S(1)}, u32[]{:S(2)}, u32[]{:S(2)}) collective-permute-start(f32[4,16,8,128]{3,2,1,0:T(8,128)S(1)} %get-tuple-element.26), channel_id=1, source_target_pairs={{0,8},{2,10},{4,12},{6,14},{8,0},{10,2},{12,4},{14,6},{16,24},{18,... | collective-permute-start | bytes 786440 | tf_op jit(solution)/shard_map/ppermute | solution.py:374
  37.6 3.6 %collective-permute-start.4 = (f32[4,16,8,128]{3,2,1,0:T(8,128)S(1)}, f32[4,16,8,128]{3,2,1,0:T(8,128)S(1)}, u32[]{:S(2)}, u32[]{:S(2)}) collective-permute-start(f32[4,16,8,128]{3,2,1,0:T(8,128)S(1)} %get-tuple-element.27), channel_id=1, source_target_pairs={{0,16},{2,18},{4,20},{6,22},{8,24},{10,26},{12,28},{14,30},{16,0},... | collective-permute-start | bytes 786440 | tf_op jit(solution)/shard_map/ppermute | solution.py:374
  41.2 5.0 %collective-permute-done.3.refs_1_ = f32[4,16,8,128]{3,2,1,0:T(8,128)S(1)} collective-permute-done((f32[4,16,8,128]{3,2,1,0:T(8,128)S(1)}, f32[4,16,8,128]{3,2,1,0:T(8,128)S(1)}, u32[]{:S(2)}, u32[]{:S(2)}) %collective-permute-start.3) | collective-permute-done | bytes 262176 | tf_op jit(solution)/shard_map/ppermute | solution.py:374
  46.2 12.1 %collective-permute-done.4.refs_2_ = f32[4,16,8,128]{3,2,1,0:T(8,128)S(1)} collective-permute-done((f32[4,16,8,128]{3,2,1,0:T(8,128)S(1)}, f32[4,16,8,128]{3,2,1,0:T(8,128)S(1)}, u32[]{:S(2)}, u32[]{:S(2)}) %collective-permute-start.4) | collective-permute-done | bytes 262176 | tf_op jit(solution)/shard_map/ppermute | solution.py:374
  58.3 4.7 %collective-permute-done.5.refs_3_ = f32[4,16,8,128]{3,2,1,0:T(8,128)S(1)} collective-permute-done((f32[4,16,8,128]{3,2,1,0:T(8,128)S(1)}, f32[4,16,8,128]{3,2,1,0:T(8,128)S(1)}, u32[]{:S(2)}, u32[]{:S(2)}) %collective-permute-start.5) | collective-permute-done | bytes 262176 | tf_op jit(solution)/shard_map/ppermute | solution.py:374
  63.0 0.7 join.2.own
  65.1 1.4 collective-permute-done.6.other
  66.6 11.7 %levels.2 = f32[16,16,8,128]{3,2,1,0:T(8,128)S(1)} custom-call(s32[2]{0:T(128)S(1)} %pad_add_fusion.ids, f32[496]{0:T(512)S(1)} %copy-done.9, f32[8,2,16,8,128]{4,3,2,1,0:T(8,128)S(1)} %join.2.own, f32[8,2,16,8,128]{4,3,2,1,0:T(8,128)} %collective-permute-done.6.other, f32[31,128]{1,0:T(8,128)S(1)} %tile.24.speeds, f32[8,128]{1,0:T(8,128)S(1)} %copy-done.8, ...), custom_call_target="tpu_custom_call" | custom-call | flops 100000000 | bytes 8388608 | tf_op jit(solution)/shard_map/levels/pallas_call | solution.py:602
  78.4 1.0 copy-done.3
  79.3 5.6 %all-to-all-start = ((f32[16,16,8,128]{3,2,1,0:T(8,128)}), f32[16,16,8,128]{3,2,1,0:T(8,128)S(1)}, u32[]{:S(2)}, u32[]{:S(2)}) async-start(f32[16,16,8,128]{3,2,1,0:T(8,128)} %copy-done.3), calls=%async_computation | async-start | bytes 2097152 | tf_op jit(solution)/shard_map/all_to_all | solution.py:735
  85.0 2.3 %join.3.own = f32[8,2,16,8,128]{4,3,2,1,0:T(8,128)} custom-call(f32[16,16,8,128]{3,2,1,0:T(8,128)} %all-to-all-done.1.in_ref), custom_call_target="tpu_custom_call" | custom-call | flops 1000000 | bytes 2097152 | tf_op jit(solution)/shard_map/join/pallas_call | solution.py:415
  87.4 2.9 %collective-permute-done.7.other = f32[8,2,16,8,128]{4,3,2,1,0:T(8,128)} collective-permute-done((f32[8,2,16,8,128]{4,3,2,1,0:T(8,128)}, f32[8,2,16,8,128]{4,3,2,1,0:T(8,128)}, u32[]{:S(2)}, u32[]{:S(2)}) %collective-permute-start.7) | collective-permute-done | bytes 1048608 | tf_op jit(solution)/shard_map/ppermute | solution.py:20
  90.3 12.1 %levels.3 = (f32[4,16,8,128]{3,2,1,0:T(8,128)S(1)}, f32[4,16,8,128]{3,2,1,0:T(8,128)S(1)}, f32[4,16,8,128]{3,2,1,0:T(8,128)S(1)}, f32[4,16,8,128]{3,2,1,0:T(8,128)S(1)}) custom-call(s32[2]{0:T(128)S(1)} %pad_add_fusion.ids, f32[496]{0:T(512)S(1)} %copy-done.9, f32[8,2,16,8,128]{4,3,2,1,0:T(8,128)} %join.3.own, ...), custom_call_target="tpu_custom_call" | custom-call | flops 100000000 | bytes 8388608 | tf_op jit(solution)/shard_map/levels/pallas_call | solution.py:602
  103.0 2.4 %collective-permute-start.9 = (f32[4,16,8,128]{3,2,1,0:T(8,128)S(1)}, f32[4,16,8,128]{3,2,1,0:T(8,128)S(1)}, u32[]{:S(2)}, u32[]{:S(2)}) collective-permute-start(f32[4,16,8,128]{3,2,1,0:T(8,128)S(1)} %get-tuple-element.31), channel_id=1, source_target_pairs={{0,16},{2,18},{4,20},{6,22},{8,24},{10,26},{12,28},{14,30},{16,0},... | collective-permute-start | bytes 786440 | tf_op jit(solution)/shard_map/ppermute | solution.py:374
  105.9 7.6 %collective-permute-done.8.refs_1_ = f32[4,16,8,128]{3,2,1,0:T(8,128)S(1)} collective-permute-done((f32[4,16,8,128]{3,2,1,0:T(8,128)S(1)}, f32[4,16,8,128]{3,2,1,0:T(8,128)S(1)}, u32[]{:S(2)}, u32[]{:S(2)}) %collective-permute-start.8) | collective-permute-done | bytes 262176 | tf_op jit(solution)/shard_map/ppermute | solution.py:374
  113.5 11.8 %collective-permute-done.9.refs_2_ = f32[4,16,8,128]{3,2,1,0:T(8,128)S(1)} collective-permute-done((f32[4,16,8,128]{3,2,1,0:T(8,128)S(1)}, f32[4,16,8,128]{3,2,1,0:T(8,128)S(1)}, u32[]{:S(2)}, u32[]{:S(2)}) %collective-permute-start.9) | collective-permute-done | bytes 262176 | tf_op jit(solution)/shard_map/ppermute | solution.py:374
  125.3 6.8 %collective-permute-done.10.refs_3_ = f32[4,16,8,128]{3,2,1,0:T(8,128)S(1)} collective-permute-done((f32[4,16,8,128]{3,2,1,0:T(8,128)S(1)}, f32[4,16,8,128]{3,2,1,0:T(8,128)S(1)}, u32[]{:S(2)}, u32[]{:S(2)}) %collective-permute-start.10) | collective-permute-done | bytes 262176 | tf_op jit(solution)/shard_map/ppermute | solution.py:374
  132.1 1.5 %collective-permute-start.11 = (f32[4,16,8,128]{3,2,1,0:T(8,128)S(1)}, f32[4,16,8,128]{3,2,1,0:T(8,128)S(1)}, u32[]{:S(2)}, u32[]{:S(2)}) collective-permute-start(f32[4,16,8,128]{3,2,1,0:T(8,128)S(1)} %get-tuple-element.34), channel_id=1, source_target_pairs={{0,2},{2,0},{4,6},{6,4},{8,10},{10,8},{12,14},{14,12},{16,18},{18,... | collective-permute-start | bytes 786440 | tf_op jit(solution)/shard_map/ppermute | solution.py:374
  134.2 1.5 collective-permute-start.13
  135.7 4.8 %collective-permute-done.11.refs_1_ = f32[4,16,8,128]{3,2,1,0:T(8,128)S(1)} collective-permute-done((f32[4,16,8,128]{3,2,1,0:T(8,128)S(1)}, f32[4,16,8,128]{3,2,1,0:T(8,128)S(1)}, u32[]{:S(2)}, u32[]{:S(2)}) %collective-permute-start.11) | collective-permute-done | bytes 262176 | tf_op jit(solution)/shard_map/ppermute | solution.py:374
  140.5 2.4 %collective-permute-done.12.refs_2_ = f32[4,16,8,128]{3,2,1,0:T(8,128)S(1)} collective-permute-done((f32[4,16,8,128]{3,2,1,0:T(8,128)S(1)}, f32[4,16,8,128]{3,2,1,0:T(8,128)S(1)}, u32[]{:S(2)}, u32[]{:S(2)}) %collective-permute-start.12) | collective-permute-done | bytes 262176 | tf_op jit(solution)/shard_map/ppermute | solution.py:374
  142.9 3.4 %collective-permute-done.13.refs_3_ = f32[4,16,8,128]{3,2,1,0:T(8,128)S(1)} collective-permute-done((f32[4,16,8,128]{3,2,1,0:T(8,128)S(1)}, f32[4,16,8,128]{3,2,1,0:T(8,128)S(1)}, u32[]{:S(2)}, u32[]{:S(2)}) %collective-permute-start.13) | collective-permute-done | bytes 262176 | tf_op jit(solution)/shard_map/ppermute | solution.py:374
  146.3 2.7 %unpack.2.refs_1_ = f32[2,16,16,1024]{3,2,1,0:T(8,128)} custom-call(s32[2]{0:T(128)S(1)} %pad_add_fusion.ids, f32[4,16,8,128]{3,2,1,0:T(8,128)S(1)} %get-tuple-element.33.refs_0_, f32[4,16,8,128]{3,2,1,0:T(8,128)S(1)} %collective-permute-done.11.refs_1_, f32[4,16,8,128]{3,2,1,0:T(8,128)S(1)} %collective-permute-done.12.refs_2_, ...), custom_call_target="tpu_custom_call" | custom-call | flops 1000000 | bytes 2097152 | tf_op jit(solution)/shard_map/unpack/pallas_call | solution.py:670
  149.0 2.2 %unpack.3 = f32[2,16,16,1024]{3,2,1,0:T(8,128)} custom-call(f32[16,16,8,128]{3,2,1,0:T(8,128)S(1)} %all-to-all-done.refs_0_, f32[2,16,16,1024]{3,2,1,0:T(8,128)} %unpack.2.refs_1_), custom_call_target="tpu_custom_call", output_to_operand_aliasing={{}: (1, {})} | custom-call | flops 1000000 | bytes 2097152 | tf_op jit(solution)/shard_map/unpack/pallas_call | solution.py:670
  (58 shorter events, 4.0 us)
Async XLA Ops:
  0.0 64.3 %copy-start = (f32[4,4]{1,0:T(4,128)S(1)}, f32[4,4]{1,0:T(4,128)}, u32[]{:S(2)}) copy-start(f32[4,4]{1,0:T(4,128)} %param.20) | copy-start | bytes 196
  0.0 11.3 %copy-start.1 = (f32[1,1,2,16,16,1024]{5,4,3,2,1,0:T(8,128)S(1)}, f32[1,1,2,16,16,1024]{5,4,3,2,1,0:T(8,128)}, u32[]{:S(2)}) copy-start(f32[1,1,2,16,16,1024]{5,4,3,2,1,0:T(8,128)} %param.19) | copy-start | bytes 6291460
  4.0 75.3 %all-to-all-start.1 = ((f32[16,16,8,128]{3,2,1,0:T(8,128)}), f32[16,16,8,128]{3,2,1,0:T(8,128)}, u32[]{:S(2)}, u32[]{:S(2)}) async-start(f32[16,16,8,128]{3,2,1,0:T(8,128)} %pack.1), calls=%async_computation.1 | async-start | bytes 2097152 | tf_op jit(solution)/shard_map/all_to_all | solution.py:735
  13.0 51.1 %copy-start.10 = (f32[31]{0:T(128)S(1)}, f32[31]{0:T(128)}, u32[]{:S(2)}) copy-start(f32[31]{0:T(128)} %constant.82) | copy-start | bytes 376
  13.0 51.1 %copy-start.11 = (f32[31]{0:T(128)S(1)}, f32[31]{0:T(128)}, u32[]{:S(2)}) copy-start(f32[31]{0:T(128)} %constant.71.clone) | copy-start | bytes 376
  13.0 53.6 %copy-start.2 = (f32[496,8,128]{2,1,0:T(8,128)S(1)}, f32[496,8,128]{2,1,0:T(8,128)}, u32[]{:S(2)}) copy-start(f32[496,8,128]{2,1,0:T(8,128)} %constant.74.clone.lengths) | copy-start | bytes 6094852
  13.0 53.6 %copy-start.4 = (bf16[256,256]{1,0:T(8,128)(2,1)S(1)}, bf16[256,256]{1,0:T(8,128)(2,1)}, u32[]{:S(2)}) copy-start(bf16[256,256]{1,0:T(8,128)(2,1)} %constant.78.clone.first_table) | copy-start | bytes 393220
  13.0 53.5 %copy-start.5 = (f32[2,4,8,128]{3,2,1,0:T(8,128)S(1)}, f32[2,4,8,128]{3,2,1,0:T(8,128)}, u32[]{:S(2)}) copy-start(f32[2,4,8,128]{3,2,1,0:T(8,128)} %constant.77.clone.last_lengths) | copy-start | bytes 98308
  13.0 53.5 %copy-start.6 = (f32[4,8,128]{2,1,0:T(8,128)S(1)}, f32[4,8,128]{2,1,0:T(8,128)}, u32[]{:S(2)}) copy-start(f32[4,8,128]{2,1,0:T(8,128)} %constant.76.clone.last_two) | copy-start | bytes 49156
  13.0 53.5 %copy-start.7 = (f32[2,8,128]{2,1,0:T(8,128)S(1)}, f32[2,8,128]{2,1,0:T(8,128)}, u32[]{:S(2)}) copy-start(f32[2,8,128]{2,1,0:T(8,128)} %constant.75.clone.last_one) | copy-start | bytes 24580
  13.0 53.5 %copy-start.8 = (f32[8,128]{1,0:T(8,128)S(1)}, f32[8,128]{1,0:T(8,128)}, u32[]{:S(2)}) copy-start(f32[8,128]{1,0:T(8,128)} %constant.73.clone.waves) | copy-start | bytes 12292
  13.1 53.5 %copy-start.9 = (f32[496]{0:T(512)S(1)}, f32[496]{0:T(512)}, u32[]{:S(2)}) copy-start(f32[496]{0:T(512)} %constant.72.clone.nodes) | copy-start | bytes 5956
  13.1 9.8 %collective-permute-start = (f32[4,16,8,128]{3,2,1,0:T(8,128)S(1)}, f32[4,16,8,128]{3,2,1,0:T(8,128)S(1)}, u32[]{:S(2)}, u32[]{:S(2)}) collective-permute-start(f32[4,16,8,128]{3,2,1,0:T(8,128)S(1)} %get-tuple-element.22), channel_id=1, source_target_pairs={{0,2},{2,0},{4,6},{6,4},{8,10},{10,8},{12,14},{14,12},{16,18},{18,... | collective-permute-start | bytes 786440 | tf_op jit(solution)/shard_map/ppermute | solution.py:374
  14.6 12.5 %collective-permute-start.1 = (f32[4,16,8,128]{3,2,1,0:T(8,128)S(1)}, f32[4,16,8,128]{3,2,1,0:T(8,128)S(1)}, u32[]{:S(2)}, u32[]{:S(2)}) collective-permute-start(f32[4,16,8,128]{3,2,1,0:T(8,128)S(1)} %get-tuple-element.23), channel_id=1, source_target_pairs={{0,4},{2,6},{4,0},{6,2},{8,12},{10,14},{12,8},{14,10},{16,20},{18,... | collective-permute-start | bytes 786440 | tf_op jit(solution)/shard_map/ppermute | solution.py:374
  15.2 19.9 %collective-permute-start.2 = (f32[4,16,8,128]{3,2,1,0:T(8,128)S(1)}, f32[4,16,8,128]{3,2,1,0:T(8,128)S(1)}, u32[]{:S(2)}, u32[]{:S(2)}) collective-permute-start(f32[4,16,8,128]{3,2,1,0:T(8,128)S(1)} %get-tuple-element.24), channel_id=1, source_target_pairs={{0,6},{2,4},{4,2},{6,0},{8,14},{10,12},{12,10},{14,8},{16,22},{18,... | collective-permute-start | bytes 786440 | tf_op jit(solution)/shard_map/ppermute | solution.py:374
  35.1 11.1 %collective-permute-start.3 = (f32[4,16,8,128]{3,2,1,0:T(8,128)S(1)}, f32[4,16,8,128]{3,2,1,0:T(8,128)S(1)}, u32[]{:S(2)}, u32[]{:S(2)}) collective-permute-start(f32[4,16,8,128]{3,2,1,0:T(8,128)S(1)} %get-tuple-element.26), channel_id=1, source_target_pairs={{0,8},{2,10},{4,12},{6,14},{8,0},{10,2},{12,4},{14,6},{16,24},{18,... | collective-permute-start | bytes 786440 | tf_op jit(solution)/shard_map/ppermute | solution.py:374
  37.6 20.7 %collective-permute-start.4 = (f32[4,16,8,128]{3,2,1,0:T(8,128)S(1)}, f32[4,16,8,128]{3,2,1,0:T(8,128)S(1)}, u32[]{:S(2)}, u32[]{:S(2)}) collective-permute-start(f32[4,16,8,128]{3,2,1,0:T(8,128)S(1)} %get-tuple-element.27), channel_id=1, source_target_pairs={{0,16},{2,18},{4,20},{6,22},{8,24},{10,26},{12,28},{14,30},{16,0},... | collective-permute-start | bytes 786440 | tf_op jit(solution)/shard_map/ppermute | solution.py:374
  41.2 21.8 %collective-permute-start.5 = (f32[4,16,8,128]{3,2,1,0:T(8,128)S(1)}, f32[4,16,8,128]{3,2,1,0:T(8,128)S(1)}, u32[]{:S(2)}, u32[]{:S(2)}) collective-permute-start(f32[4,16,8,128]{3,2,1,0:T(8,128)S(1)} %get-tuple-element.28), channel_id=1, source_target_pairs={{0,24},{2,26},{4,28},{6,30},{8,16},{10,18},{12,20},{14,22},{16,8},... | collective-permute-start | bytes 786440 | tf_op jit(solution)/shard_map/ppermute | solution.py:374
  63.7 2.9 %collective-permute-start.6 = (f32[8,2,16,8,128]{4,3,2,1,0:T(8,128)S(1)}, f32[8,2,16,8,128]{4,3,2,1,0:T(8,128)}, u32[]{:S(2)}, u32[]{:S(2)}) collective-permute-start(f32[8,2,16,8,128]{4,3,2,1,0:T(8,128)S(1)} %join.2.own), channel_id=1, source_target_pairs={{0,1},{1,0},{2,3},{3,2},{4,5},{5,4},{6,7},{7,6},{8,9},{9,8},{10,11... | collective-permute-start | bytes 3145736 | tf_op jit(solution)/shard_map/ppermute | solution.py:20
  78.4 1.0 copy-start.3
  79.3 69.7 %all-to-all-start = ((f32[16,16,8,128]{3,2,1,0:T(8,128)}), f32[16,16,8,128]{3,2,1,0:T(8,128)S(1)}, u32[]{:S(2)}, u32[]{:S(2)}) async-start(f32[16,16,8,128]{3,2,1,0:T(8,128)} %copy-done.3), calls=%async_computation | async-start | bytes 2097152 | tf_op jit(solution)/shard_map/all_to_all | solution.py:735
  87.3 3.0 %collective-permute-start.7 = (f32[8,2,16,8,128]{4,3,2,1,0:T(8,128)}, f32[8,2,16,8,128]{4,3,2,1,0:T(8,128)}, u32[]{:S(2)}, u32[]{:S(2)}) collective-permute-start(f32[8,2,16,8,128]{4,3,2,1,0:T(8,128)} %join.3.own), channel_id=1, source_target_pairs={{0,1},{1,0},{2,3},{3,2},{4,5},{5,4},{6,7},{7,6},{8,9},{9,8},{10,11... | collective-permute-start | bytes 3145736 | tf_op jit(solution)/shard_map/ppermute | solution.py:20
  102.3 11.2 %collective-permute-start.8 = (f32[4,16,8,128]{3,2,1,0:T(8,128)S(1)}, f32[4,16,8,128]{3,2,1,0:T(8,128)S(1)}, u32[]{:S(2)}, u32[]{:S(2)}) collective-permute-start(f32[4,16,8,128]{3,2,1,0:T(8,128)S(1)} %get-tuple-element.30), channel_id=1, source_target_pairs={{0,8},{2,10},{4,12},{6,14},{8,0},{10,2},{12,4},{14,6},{16,24},{18,... | collective-permute-start | bytes 786440 | tf_op jit(solution)/shard_map/ppermute | solution.py:374
  103.0 22.3 %collective-permute-start.9 = (f32[4,16,8,128]{3,2,1,0:T(8,128)S(1)}, f32[4,16,8,128]{3,2,1,0:T(8,128)S(1)}, u32[]{:S(2)}, u32[]{:S(2)}) collective-permute-start(f32[4,16,8,128]{3,2,1,0:T(8,128)S(1)} %get-tuple-element.31), channel_id=1, source_target_pairs={{0,16},{2,18},{4,20},{6,22},{8,24},{10,26},{12,28},{14,30},{16,0},... | collective-permute-start | bytes 786440 | tf_op jit(solution)/shard_map/ppermute | solution.py:374
  105.3 26.7 %collective-permute-start.10 = (f32[4,16,8,128]{3,2,1,0:T(8,128)S(1)}, f32[4,16,8,128]{3,2,1,0:T(8,128)S(1)}, u32[]{:S(2)}, u32[]{:S(2)}) collective-permute-start(f32[4,16,8,128]{3,2,1,0:T(8,128)S(1)} %get-tuple-element.32), channel_id=1, source_target_pairs={{0,24},{2,26},{4,28},{6,30},{8,16},{10,18},{12,20},{14,22},{16,8},... | collective-permute-start | bytes 786440 | tf_op jit(solution)/shard_map/ppermute | solution.py:374
  132.1 8.4 %collective-permute-start.11 = (f32[4,16,8,128]{3,2,1,0:T(8,128)S(1)}, f32[4,16,8,128]{3,2,1,0:T(8,128)S(1)}, u32[]{:S(2)}, u32[]{:S(2)}) collective-permute-start(f32[4,16,8,128]{3,2,1,0:T(8,128)S(1)} %get-tuple-element.34), channel_id=1, source_target_pairs={{0,2},{2,0},{4,6},{6,4},{8,10},{10,8},{12,14},{14,12},{16,18},{18,... | collective-permute-start | bytes 786440 | tf_op jit(solution)/shard_map/ppermute | solution.py:374
  133.7 9.2 %collective-permute-start.12 = (f32[4,16,8,128]{3,2,1,0:T(8,128)S(1)}, f32[4,16,8,128]{3,2,1,0:T(8,128)S(1)}, u32[]{:S(2)}, u32[]{:S(2)}) collective-permute-start(f32[4,16,8,128]{3,2,1,0:T(8,128)S(1)} %get-tuple-element.35), channel_id=1, source_target_pairs={{0,4},{2,6},{4,0},{6,2},{8,12},{10,14},{12,8},{14,10},{16,20},{18,... | collective-permute-start | bytes 786440 | tf_op jit(solution)/shard_map/ppermute | solution.py:374
  134.2 12.1 %collective-permute-start.13 = (f32[4,16,8,128]{3,2,1,0:T(8,128)S(1)}, f32[4,16,8,128]{3,2,1,0:T(8,128)S(1)}, u32[]{:S(2)}, u32[]{:S(2)}) collective-permute-start(f32[4,16,8,128]{3,2,1,0:T(8,128)S(1)} %get-tuple-element.36), channel_id=1, source_target_pairs={{0,6},{2,4},{4,2},{6,0},{8,14},{10,12},{12,10},{14,8},{16,22},{18,... | collective-permute-start | bytes 786440 | tf_op jit(solution)/shard_map/ppermute | solution.py:374

commit v4 on v3

--- a/solution.py
+++ b/solution.py
@@ -298,81 +298,87 @@
             tiles[j, t1] = tile
 
 
-def pack_kernel(in_ref, out_ref):
-    pack_rows(in_ref, slice(None), out_ref)
-
-
-def pack(weights, chunk):
+def entry_of(bundles, z_first, mz, xy):
+    return bundles[mz].at[xy] if z_first else bundles[0].at[xy, mz]
+
+
+def in_bundles(z_first):
+    shapes = [BUNDLE] * 4 if z_first else [(4,) + BUNDLE]
+    return [jax.ShapeDtypeStruct(shape, jnp.float32) for shape in shapes]
+
+
+def whole_blocks(shapes):
+    def zeros(rank):
+        return lambda i: (0,) * rank
+
+    return [pl.BlockSpec(shape.shape, zeros(len(shape.shape))) for shape in shapes]
+
+
+def pack_kernel(z_first, ids, in_ref, *refs):
+    outs, tiles = refs[:-1], refs[-1]
+    for mz in range(4):
+        group = mz ^ (ids[0] // 4)
+        pack_rows(in_ref, pl.ds(pl.multiple_of(group * 128, 128), 128), tiles)
+        for xy in range(4):
+            entry_of(outs, z_first, mz, xy)[...] = tiles[xy]
+
+
+BUNDLE = (4, 16, 8, 128)
+
+
+def pack(weights, ids, chunk, z_first):
     return pl.pallas_call(
-        pack_kernel,
-        grid=(4,),
-        in_specs=[pl.BlockSpec((2, 16, 16, 128), lambda i: (0, 0, 0, 4 * chunk + i))],
-        out_specs=pl.BlockSpec((4, 16, 8, 128), lambda i: (i, 0, 0, 0)),
-        out_shape=jax.ShapeDtypeStruct((PIECES, 16, 8, 128), jnp.float32),
-        cost_estimate=pl.CostEstimate(flops=10**6, bytes_accessed=2**21, transcendentals=0),
-        name="pack",
-    )(weights)
-
-
-def pack_masks_kernel(ids, in_ref, *refs):
-    outs, tiles = refs[:4], refs[4]
-    me = ids[0]
-
-    def step(mz, carry):
-        group = mz ^ (me // 4)
-        pack_rows(in_ref, pl.ds(pl.multiple_of(group * 128, 128), 128), tiles)
-        for mxy in range(4):
-            outs[mxy][mz] = tiles[mxy ^ (me % 4)]
-        return carry
-
-    lax.fori_loop(0, 4, step, 0)
-
-
-BUNDLE = (4, 16, 8, 128)
-
-
-def pack_masks(weights, ids, chunk):
-    return pl.pallas_call(
-        pack_masks_kernel,
+        partial(pack_kernel, z_first),
         grid=(1,),
         in_specs=[
             pl.BlockSpec(memory_space=pltpu.SMEM),
             pl.BlockSpec((2, 16, 16, 512), lambda i: (0, 0, 0, chunk)),
         ],
-        out_specs=[pl.BlockSpec(BUNDLE, lambda i: (0, 0, 0, 0))] * 4,
-        out_shape=[jax.ShapeDtypeStruct(BUNDLE, jnp.float32)] * 4,
+        out_specs=whole_blocks(in_bundles(z_first)),
+        out_shape=in_bundles(z_first),
         scratch_shapes=[pltpu.VMEM(BUNDLE, jnp.float32)],
         compiler_params=pltpu.CompilerParams(vmem_limit_bytes=VMEM_LIMIT),
-        cost_estimate=pl.CostEstimate(flops=10**6, bytes_accessed=2**21, transcendentals=0),
-        name="pack_masks",
+        cost_estimate=pl.CostEstimate(flops=1000, bytes_accessed=1000, transcendentals=0),
+        name="pack",
     )(ids, weights)
 
 
-def regroup_kernel(*refs):
-    for first in range(4):
-        for second in range(4):
-            refs[4 + second][first] = refs[first][second]
-
-
-def regroup(bundles):
+def regroup_kernel(z_first, *refs):
+    count = 4 if z_first else 1
+    outs = refs[-(5 - count) :]
+    for mz in range(4):
+        for xy in range(4):
+            piece = entry_of(refs, z_first, mz, xy)[...]
+            entry_of(outs, not z_first, mz, xy)[...] = piece
+
+
+def regroup(bundles, z_first, after=()):
     in_vmem = pl.BlockSpec(memory_space=pltpu.VMEM)
+    shapes = in_bundles(not z_first)
     return pl.pallas_call(
-        regroup_kernel,
-        in_specs=[in_vmem] * 4,
-        out_specs=[in_vmem] * 4,
-        out_shape=[jax.ShapeDtypeStruct(BUNDLE, jnp.float32)] * 4,
+        partial(regroup_kernel, z_first),
+        in_specs=[in_vmem] * len(bundles) + [pl.BlockSpec(memory_space=pl.ANY)] * len(after),
+        out_specs=[in_vmem] * len(shapes),
+        out_shape=shapes,
         compiler_params=pltpu.CompilerParams(vmem_limit_bytes=VMEM_LIMIT),
-        cost_estimate=pl.CostEstimate(flops=10**5, bytes_accessed=2**21, transcendentals=0),
+        cost_estimate=pl.CostEstimate(flops=1000, bytes_accessed=1000, transcendentals=0),
         name="regroup",
-    )(*bundles)
-
-
-def exchange(bundles, unit):
+    )(*bundles, *after)
+
+
+def cross_z(bundles):
     moved = [bundles[0]]
     for mask in range(1, 4):
-        pairs = [(source, source ^ (mask * unit)) for source in range(PIECES)]
+        pairs = [(source, source ^ (4 * mask)) for source in range(PIECES)]
         moved.append(lax.ppermute(bundles[mask], ("bx", "by"), pairs))
     return moved
+
+
+def cross_xy(bundles):
+    groups = [[4 * z + xy for xy in range(4)] for z in range(4)]
+    return [
+        lax.all_to_all(bundles[0], ("bx", "by"), 0, 0, axis_index_groups=groups, tiled=True)
+    ]
 
 
 def merge_halves(out_ref, box, t1, low, high):
@@ -381,53 +387,37 @@
     out_ref[box, 1, t1] = jnp.where(upper, pltpu.roll(low, 4, 0), high)
 
 
-def join_kernel(in_ref, out_ref):
-    def step(box, carry):
-        for t1 in range(16):
-            merge_halves(out_ref, box, t1, in_ref[2 * box, t1], in_ref[2 * box + 1, t1])
-        return carry
-
-    lax.fori_loop(0, 8, step, 0)
-
-
-def join_masks_kernel(ids, *refs):
-    bundles, out_ref = refs[:4], refs[4]
-    me = ids[0]
-    is_low = jnp.broadcast_to(me % 2, (8, 128)) == 0
+def join_kernel(z_first, ids, *refs):
+    bundles, out_ref = refs[:4], refs[-1]
     for mz in range(4):
-        for mx in range(2):
-            box = (2 * mz + mx) ^ (me // 2)
+        for x in range(2):
+            box = 2 * (mz ^ (ids[0] // 4)) + x
             for t1 in range(16):
-                mine = bundles[mz][2 * mx, t1]
-                partner = bundles[mz][2 * mx + 1, t1]
-                low = jnp.where(is_low, mine, partner)
-                high = jnp.where(is_low, partner, mine)
+                low = entry_of(bundles, z_first, mz, 2 * x)[t1]
+                high = entry_of(bundles, z_first, mz, 2 * x + 1)[t1]
                 merge_halves(out_ref, box, t1, low, high)
 
 
-def join(received, ids=None):
+def join(received, ids, z_first, after=()):
     in_vmem = pl.BlockSpec(memory_space=pltpu.VMEM)
-    if ids is None:
-        kernel, operands, in_specs = join_kernel, [received], [in_vmem]
-    else:
-        kernel, operands = join_masks_kernel, [ids, *received]
-        in_specs = [pl.BlockSpec(memory_space=pltpu.SMEM)] + [in_vmem] * 4
     return pl.pallas_call(
-        kernel,
-        in_specs=in_specs,
+        partial(join_kernel, z_first),
+        in_specs=[pl.BlockSpec(memory_space=pltpu.SMEM)]
+        + [in_vmem] * len(received)
+        + [pl.BlockSpec(memory_space=pl.ANY)] * len(after),
         out_specs=in_vmem,
         out_shape=jax.ShapeDtypeStruct((8, 2, 16, 8, 128), jnp.float32),
         compiler_params=pltpu.CompilerParams(vmem_limit_bytes=VMEM_LIMIT),
-        cost_estimate=pl.CostEstimate(flops=10**6, bytes_accessed=2**21, transcendentals=0),
+        cost_estimate=pl.CostEstimate(flops=1000, bytes_accessed=1000, transcendentals=0),
         name="join",
-    )(*operands)
+    )(ids, *received, *after)
 
 
 def levels_kernel(
-    chunk, by_masks, ids, nodes, own, other, speeds, waves, lengths, last_one, last_two,
+    chunk, z_first, ids, nodes, own, other, speeds, waves, lengths, last_one, last_two,
     last_lengths, first_table, second_table, *refs,
 ):
-    outs = refs[:4] if by_masks else refs[0]
+    outs = refs[:-6]
     boxes_a, boxes_b, sums, turned, mixed, last_phase = refs[-6:]
     row = (chunk * PIECES + ids[0]).astype(jnp.float32)
     core = ids[1]
@@ -576,34 +566,26 @@
                 out[high * 4 + a] = real * cosine - imag * sine
                 out[8 + high * 4 + a] = real * sine + imag * cosine
 
-    def finish_row(major, carry):
-        for minor in range(4):
-            if by_masks:
-                finish_box((4 * minor + major) ^ ids[0], outs[minor].at[major])
-            else:
-                finish_box(4 * major + minor, outs.at[4 * major + minor])
+    def finish_row(xy, carry):
+        for mz in range(4):
+            target = 4 * (mz ^ (ids[0] // 4)) + xy
+            finish_box(target, entry_of(outs, z_first, mz, xy))
         return carry
 
     lax.fori_loop(0, 4, finish_row, 0)
 
 
-def levels(chunk, by_masks, ids, own, other, speeds):
+def levels(chunk, z_first, ids, own, other, speeds):
     nodes, waves, lengths = node_tables()
     last_one, last_two, last_lengths = final_tables()
     tables = (waves, lengths, last_one, last_two, last_lengths, first_weights(), second_weights())
     in_vmem = pl.BlockSpec(memory_space=pltpu.VMEM)
     in_smem = pl.BlockSpec(memory_space=pltpu.SMEM)
-    if by_masks:
-        out_shape = [jax.ShapeDtypeStruct(BUNDLE, jnp.float32)] * 4
-        out_specs = [in_vmem] * 4
-    else:
-        out_shape = jax.ShapeDtypeStruct((PIECES, 16, 8, 128), jnp.float32)
-        out_specs = in_vmem
     return pl.pallas_call(
-        partial(levels_kernel, chunk, by_masks),
+        partial(levels_kernel, chunk, z_first),
         in_specs=[in_smem, in_smem] + [in_vmem] * 10,
-        out_specs=out_specs,
-        out_shape=out_shape,
+        out_specs=[in_vmem] * len(in_bundles(z_first)),
+        out_shape=in_bundles(z_first),
         scratch_shapes=[
             pltpu.VMEM((8, 2, 16, 8, 128), jnp.float32),
             pltpu.VMEM((8, 2, 16, 8, 128), jnp.float32),
@@ -613,7 +595,7 @@
             pltpu.VMEM((2, 4, 8, 128), jnp.float32),
         ],
         compiler_params=pltpu.CompilerParams(vmem_limit_bytes=VMEM_LIMIT),
-        cost_estimate=pl.CostEstimate(flops=10**8, bytes_accessed=2**23, transcendentals=0),
+        cost_estimate=pl.CostEstimate(flops=1000, bytes_accessed=1000, transcendentals=0),
         name="levels",
     )(ids, jnp.asarray(nodes), own, other, speeds, *[jnp.asarray(table) for table in tables])
 
@@ -631,52 +613,35 @@
                 out_ref[part, high * 8 + t1, :, lanes] = rows[block, pl.ds(t1, 16, stride=8), :]
 
 
-def unpack_kernel(*refs):
-    unpack_rows(refs[0], refs[-1], refs[-2], slice(None))
-
-
-def unpack_masks_kernel(ids, *refs):
+def unpack_kernel(z_first, ids, *refs):
     bundles, out_ref, tiles, rows = refs[:4], refs[-3], refs[-2], refs[-1]
     me = ids[0]
-
-    def step(mz, carry):
+    for mz in range(4):
         group = mz ^ (me // 4)
-        for mxy in range(4):
-            tiles[mxy ^ (me % 4)] = bundles[mxy][mz]
+        for xy in range(4):
+            tiles[xy] = entry_of(bundles, z_first, mz, xy)[...]
         unpack_rows(tiles, rows, out_ref, pl.ds(pl.multiple_of(group * 128, 128), 128))
-        return carry
-
-    lax.fori_loop(0, 4, step, 0)
-
-
-def unpack(received, chunk, earlier, ids=None):
-    rows = pltpu.VMEM((4, 128, 128), jnp.float32)
-    if ids is None:
-        kernel, operands, grid = unpack_kernel, [received], (4,)
-        in_specs = [pl.BlockSpec((4, 16, 8, 128), lambda i: (i, 0, 0, 0))]
-        out_spec = pl.BlockSpec((2, 16, 16, 128), lambda i: (0, 0, 0, 4 * chunk + i))
-        scratch = [rows]
-    else:
-        kernel, operands, grid = unpack_masks_kernel, [ids, *received], (1,)
-        in_specs = [pl.BlockSpec(memory_space=pltpu.SMEM)]
-        in_specs += [pl.BlockSpec(BUNDLE, lambda i: (0, 0, 0, 0))] * 4
-        out_spec = pl.BlockSpec((2, 16, 16, 512), lambda i: (0, 0, 0, chunk))
-        scratch = [pltpu.VMEM(BUNDLE, jnp.float32), rows]
+
+
+def unpack(received, ids, chunk, z_first, earlier):
+    operands = [ids, *received]
+    in_specs = [pl.BlockSpec(memory_space=pltpu.SMEM)]
+    in_specs += whole_blocks(in_bundles(z_first))
     aliases = {}
     if earlier is not None:
         aliases = {len(operands): 0}
         operands.append(earlier)
         in_specs.append(pl.BlockSpec(memory_space=pl.ANY))
     return pl.pallas_call(
-        kernel,
-        grid=grid,
+        partial(unpack_kernel, z_first),
+        grid=(1,),
         in_specs=in_specs,
-        out_specs=out_spec,
+        out_specs=pl.BlockSpec((2, 16, 16, 512), lambda i: (0, 0, 0, chunk)),
         out_shape=jax.ShapeDtypeStruct((2, 16, 16, 1024), jnp.float32),
-        scratch_shapes=scratch,
+        scratch_shapes=[pltpu.VMEM(BUNDLE, jnp.float32), pltpu.VMEM((4, 128, 128), jnp.float32)],
         input_output_aliases=aliases,
         compiler_params=pltpu.CompilerParams(vmem_limit_bytes=VMEM_LIMIT),
-        cost_estimate=pl.CostEstimate(flops=10**6, bytes_accessed=2**21, transcendentals=0),
+        cost_estimate=pl.CostEstimate(flops=1000, bytes_accessed=1000, transcendentals=0),
         name="unpack",
     )(*operands)
 
@@ -713,26 +678,26 @@
     ids = jnp.stack([me, core]).astype(jnp.int32)
     speeds = speed_tables(speed_modes, core)
 
-    first = deal(pack(local, 0))
-    near = exchange(pack_masks(local, ids, 1), 1)
-    second = exchange(regroup(near), 4)
-
-    own = join(first)
+    z_crossed = cross_z(pack(local, ids, 0, True))
+    xy_crossed = cross_xy(pack(local, ids, 1, False))
+    grouped = regroup(xy_crossed, False, z_crossed[1:])
+    first = cross_xy(regroup(z_crossed, True, grouped[:1]))
+    second = cross_z(grouped)
+
+    own = join(first, ids, False)
     result = levels(0, True, ids, own, partner_2(own, "cores", 0), speeds[0])
-    far = exchange(result, 4)
-    back_first = exchange(regroup(far), 1)
-
-    own = join(second, ids)
+    z_crossed = cross_z(result)
+
+    own = join(second, ids, True, result[:1])
     result = levels(1, False, ids, own, partner_2(own, "cores", 0), speeds[1])
-    back_second = deal(result)
-
-    out = unpack(back_first, 0, None, ids)
-    out = unpack(back_second, 1, out)
+    xy_crossed = cross_xy(result)
+
+    grouped = regroup(xy_crossed, False, z_crossed[1:])
+    first = cross_xy(regroup(z_crossed, True, grouped[:1]))
+    second = cross_z(grouped)
+    out = unpack(first, ids, 0, False, None)
+    out = unpack(second, ids, 1, True, out)
     return out.reshape(weights.shape)
-
-
-def deal(pieces):
-    return lax.all_to_all(pieces, ("bx", "by"), 0, 0, tiled=True)
 
 
 def solution(mesh):

time: 152 us -> 180 us (1.18)
  local copies, waits for them, and re-layouts: 1.67 us -> 17 us
  Pallas kernels: 37.5 us -> 46.7 us
  other arithmetic: 0.2 us -> 2.12 us
    all_to_all x2 -> x4, waiting for transfers between devices: 0.01 us -> 20.2 us  [cross_xy(): lax.all_to_all(bundles[0], ('bx', 'by'), 0, 0, axis_index_groups=groups,...]
    ppermute x12, waiting for transfers between devices: 77 us -> 58.7 us  [cross_z(): moved.append(lax.ppermute(bundles[mask], ('bx', 'by'), pairs))]
    pallas_call x10 -> x12, Pallas kernels: 37.5 us -> 46.7 us  [the longest x2 23.6 us: levels(): pl.pallas_call(partial(levels_kernel, chunk, z_first), in_specs=[in_smem,...]
    unnamed x24 -> x58, local copies, waits for them, and re-layouts: 1.04 us -> 9.66 us
    all_to_all x2 -> x4, starting transfers between devices: 12.8 us -> 17 us  [cross_xy(): lax.all_to_all(bundles[0], ('bx', 'by'), 0, 0, axis_index_groups=groups,...]
    ppermute x12, starting transfers between devices: 16.8 us -> 14 us  [cross_z(): moved.append(lax.ppermute(bundles[mask], ('bx', 'by'), pairs))]
  transfers between devices with their start and end apart: 16 -> 18, of which waited for: 14 -> 13; matrix products, arithmetic and copies ran while one was open for 1% -> 6% of each run, Pallas kernels for 21% -> 12%
where the time goes in v4:
time: 180 us; the launch traced here: 179 us
  waiting for transfers between devices  81.5 us (45%)
  Pallas kernels  46.7 us (26%)
  starting transfers between devices  31.1 us (17%)
  local copies, waits for them, and re-layouts  17 us (9%)
  other arithmetic  2.12 us (1%)
    ppermute x12, waiting for transfers between devices, cross_z(): moved.append(lax.ppermute(bundles[mask], ('bx', 'by'), pairs))  58.7 us
    pallas_call x2, Pallas kernels, levels(): pl.pallas_call(partial(levels_kernel, chunk, z_first), in_specs=[in_smem,...  23.6 us
    all_to_all x4, waiting for transfers between devices, cross_xy(): lax.all_to_all(bundles[0], ('bx', 'by'), 0, 0, axis_index_groups=groups,...  20.2 us
    all_to_all x4, starting transfers between devices, cross_xy(): lax.all_to_all(bundles[0], ('bx', 'by'), 0, 0, axis_index_groups=groups,...  17 us
    ppermute x12, starting transfers between devices, cross_z(): moved.append(lax.ppermute(bundles[mask], ('bx', 'by'), pairs))  14 us
    pallas_call x2, Pallas kernels, unpack(): pl.pallas_call(partial(unpack_kernel, z_first), grid=(1,), in_specs=in_sp...  10.7 us
    unnamed x58, local copies, waits for them, and re-layouts  9.66 us
    pallas_call x2, Pallas kernels, pack(): pl.pallas_call(partial(pack_kernel, z_first), grid=(1,), in_specs=[pl.Blo...  8.48 us
  transfers between devices with their start and end apart: 18, of which 13 were waited for; matrix products, arithmetic and copies ran while one was open for 6% of the time, Pallas kernels for 12%

profile of v4, /device:TPU:10, one launch (start us, length us, event | category | flops | bytes accessed | tf_op | source)
XLA Modules:
  0.0 179.5 jit_solution(3540526443836594723)
XLA Ops:
  0.1 1.6 copy-done.1
  1.7 4.2 %pack.2 = f32[4,4,16,8,128]{4,3,2,1,0:T(8,128)S(1)} custom-call(s32[2]{0:T(128)S(1)} %pad_add_fusion.ids, f32[2,16,16,1024]{3,2,1,0:T(8,128)S(1)} %bitcast.30), custom_call_target="tpu_custom_call" | custom-call | flops 1000 | bytes 1000 | tf_op jit(solution)/shard_map/pack/pallas_call | solution.py:330
  6.9 4.2 %all-to-all-start = ((f32[4,4,16,8,128]{4,3,2,1,0:T(8,128)}), f32[4,4,16,8,128]{4,3,2,1,0:T(8,128)S(1)}, u32[]{:S(2)}, u32[]{:S(2)}) async-start(f32[4,4,16,8,128]{4,3,2,1,0:T(8,128)} %copy-done.5), calls=%async_computation | async-start | bytes 2097152 | tf_op jit(solution)/shard_map/all_to_all | solution.py:380
  11.1 4.2 %pack.3 = (f32[4,16,8,128]{3,2,1,0:T(8,128)S(1)}, f32[4,16,8,128]{3,2,1,0:T(8,128)S(1)}, f32[4,16,8,128]{3,2,1,0:T(8,128)S(1)}, f32[4,16,8,128]{3,2,1,0:T(8,128)S(1)}) custom-call(s32[2]{0:T(128)S(1)} %pad_add_fusion.ids, f32[2,16,16,1024]{3,2,1,0:T(8,128)S(1)} %bitcast.31), custom_call_target="tpu_custom_call" | custom-call | flops 1000 | bytes 1000 | tf_op jit(solution)/shard_map/pack/pallas_call | solution.py:330
  16.5 2.6 %collective-permute-start.1 = (f32[4,16,8,128]{3,2,1,0:T(8,128)S(1)}, f32[4,16,8,128]{3,2,1,0:T(8,128)S(1)}, u32[]{:S(2)}, u32[]{:S(2)}) collective-permute-start(f32[4,16,8,128]{3,2,1,0:T(8,128)S(1)} %get-tuple-element.22), channel_id=1, source_target_pairs={{0,16},{2,18},{4,20},{6,22},{8,24},{10,26},{12,28},{14,30},{16,0},... | collective-permute-start | bytes 786440 | tf_op jit(solution)/shard_map/ppermute | solution.py:373
  19.6 6.6 %collective-permute-done.refs_1_ = f32[4,16,8,128]{3,2,1,0:T(8,128)S(1)} collective-permute-done((f32[4,16,8,128]{3,2,1,0:T(8,128)S(1)}, f32[4,16,8,128]{3,2,1,0:T(8,128)S(1)}, u32[]{:S(2)}, u32[]{:S(2)}) %collective-permute-start) | collective-permute-done | bytes 262176 | tf_op jit(solution)/shard_map/ppermute | solution.py:373
  26.1 11.0 %collective-permute-done.1.refs_2_ = f32[4,16,8,128]{3,2,1,0:T(8,128)S(1)} collective-permute-done((f32[4,16,8,128]{3,2,1,0:T(8,128)S(1)}, f32[4,16,8,128]{3,2,1,0:T(8,128)S(1)}, u32[]{:S(2)}, u32[]{:S(2)}) %collective-permute-start.1) | collective-permute-done | bytes 262176 | tf_op jit(solution)/shard_map/ppermute | solution.py:373
  37.1 4.6 %collective-permute-done.2.refs_3_ = f32[4,16,8,128]{3,2,1,0:T(8,128)S(1)} collective-permute-done((f32[4,16,8,128]{3,2,1,0:T(8,128)S(1)}, f32[4,16,8,128]{3,2,1,0:T(8,128)S(1)}, u32[]{:S(2)}, u32[]{:S(2)}) %collective-permute-start.2) | collective-permute-done | bytes 262176 | tf_op jit(solution)/shard_map/ppermute | solution.py:373
  45.9 4.3 %all-to-all-start.1 = ((f32[4,4,16,8,128]{4,3,2,1,0:T(8,128)}), f32[4,4,16,8,128]{4,3,2,1,0:T(8,128)S(1)}, u32[]{:S(2)}, u32[]{:S(2)}) async-start(f32[4,4,16,8,128]{4,3,2,1,0:T(8,128)} %copy-done.6), calls=%async_computation.1 | async-start | bytes 2097152 | tf_op jit(solution)/shard_map/all_to_all | solution.py:380
  50.3 11.6 %all-to-all-done.1.refs_0_ = f32[4,4,16,8,128]{4,3,2,1,0:T(8,128)S(1)} async-done(((f32[4,4,16,8,128]{4,3,2,1,0:T(8,128)}), f32[4,4,16,8,128]{4,3,2,1,0:T(8,128)S(1)}, u32[]{:S(2)}, u32[]{:S(2)}) %all-to-all-start.1) | async-done | bytes 1048608 | tf_op jit(solution)/shard_map/all_to_all | solution.py:380
  61.8 1.6 join.2.own
  64.2 1.2 convert_element_type.45
  69.8 3.0 %collective-permute-start.4 = (f32[4,16,8,128]{3,2,1,0:T(8,128)}, f32[4,16,8,128]{3,2,1,0:T(8,128)}, u32[]{:S(2)}, u32[]{:S(2)}) collective-permute-start(f32[4,16,8,128]{3,2,1,0:T(8,128)} %copy-done.20), channel_id=1, source_target_pairs={{0,16},{2,18},{4,20},{6,22},{8,24},{10,26},{12,28},{14,30},{16,0},... | collective-permute-start | bytes 786440 | tf_op jit(solution)/shard_map/ppermute | solution.py:373
  74.0 1.3 slice_bitcast_fusion
  78.3 11.8 %levels.2 = (f32[4,16,8,128]{3,2,1,0:T(8,128)S(1)}, f32[4,16,8,128]{3,2,1,0:T(8,128)S(1)}, f32[4,16,8,128]{3,2,1,0:T(8,128)S(1)}, f32[4,16,8,128]{3,2,1,0:T(8,128)S(1)}) custom-call(s32[2]{0:T(128)S(1)} %pad_add_fusion.ids, f32[496]{0:T(512)S(1)} %copy-done.17, f32[8,2,16,8,128]{4,3,2,1,0:T(8,128)} %join.2.own, ...), custom_call_target="tpu_custom_call" | custom-call | flops 1000 | bytes 1000 | tf_op jit(solution)/shard_map/levels/pallas_call | solution.py:584
  91.1 5.8 %collective-permute-done.5.refs_3_ = f32[4,16,8,128]{3,2,1,0:T(8,128)} collective-permute-done((f32[4,16,8,128]{3,2,1,0:T(8,128)}, f32[4,16,8,128]{3,2,1,0:T(8,128)}, u32[]{:S(2)}, u32[]{:S(2)}) %collective-permute-start.5) | collective-permute-done | bytes 262176 | tf_op jit(solution)/shard_map/ppermute | solution.py:373
  96.9 1.2 join.3.own
  98.4 2.6 %collective-permute-done.7.other = f32[8,2,16,8,128]{4,3,2,1,0:T(8,128)} collective-permute-done((f32[8,2,16,8,128]{4,3,2,1,0:T(8,128)S(1)}, f32[8,2,16,8,128]{4,3,2,1,0:T(8,128)}, u32[]{:S(2)}, u32[]{:S(2)}) %collective-permute-start.7) | collective-permute-done | bytes 1048608 | tf_op jit(solution)/shard_map/ppermute | solution.py:20
  101.0 11.8 %levels.3 = f32[4,4,16,8,128]{4,3,2,1,0:T(8,128)S(1)} custom-call(s32[2]{0:T(128)S(1)} %pad_add_fusion.ids, f32[496]{0:T(512)S(1)} %copy-done.18, f32[8,2,16,8,128]{4,3,2,1,0:T(8,128)S(1)} %join.3.own, f32[8,2,16,8,128]{4,3,2,1,0:T(8,128)} %collective-permute-done.7.other, f32[31,128]{1,0:T(8,128)S(1)} %tile.26.speeds, f32[8,128]{1,0:T(8,128)S(1)} %copy-done.16, ...), custom_call_target="tpu_custom_call" | custom-call | flops 1000 | bytes 1000 | tf_op jit(solution)/shard_map/levels/pallas_call | solution.py:584
  113.8 4.2 %all-to-all-start.2 = ((f32[4,4,16,8,128]{4,3,2,1,0:T(8,128)}), f32[4,4,16,8,128]{4,3,2,1,0:T(8,128)S(1)}, u32[]{:S(2)}, u32[]{:S(2)}) async-start(f32[4,4,16,8,128]{4,3,2,1,0:T(8,128)} %copy-done.4), calls=%async_computation.2 | async-start | bytes 2097152 | tf_op jit(solution)/shard_map/all_to_all | solution.py:380
  118.0 3.0 %collective-permute-start.9 = (f32[4,16,8,128]{3,2,1,0:T(8,128)S(1)}, f32[4,16,8,128]{3,2,1,0:T(8,128)S(1)}, u32[]{:S(2)}, u32[]{:S(2)}) collective-permute-start(f32[4,16,8,128]{3,2,1,0:T(8,128)S(1)} %copy-done.25), channel_id=1, source_target_pairs={{0,16},{2,18},{4,20},{6,22},{8,24},{10,26},{12,28},{14,30},{16,0},... | collective-permute-start | bytes 786440 | tf_op jit(solution)/shard_map/ppermute | solution.py:373
  121.5 7.2 %collective-permute-done.8.refs_1_ = f32[4,16,8,128]{3,2,1,0:T(8,128)S(1)} collective-permute-done((f32[4,16,8,128]{3,2,1,0:T(8,128)S(1)}, f32[4,16,8,128]{3,2,1,0:T(8,128)S(1)}, u32[]{:S(2)}, u32[]{:S(2)}) %collective-permute-start.8) | collective-permute-done | bytes 262176 | tf_op jit(solution)/shard_map/ppermute | solution.py:373
  128.7 10.3 %collective-permute-done.9.refs_2_ = f32[4,16,8,128]{3,2,1,0:T(8,128)S(1)} collective-permute-done((f32[4,16,8,128]{3,2,1,0:T(8,128)S(1)}, f32[4,16,8,128]{3,2,1,0:T(8,128)S(1)}, u32[]{:S(2)}, u32[]{:S(2)}) %collective-permute-start.9) | collective-permute-done | bytes 262176 | tf_op jit(solution)/shard_map/ppermute | solution.py:373
  139.0 5.1 %collective-permute-done.10.refs_3_ = f32[4,16,8,128]{3,2,1,0:T(8,128)S(1)} collective-permute-done((f32[4,16,8,128]{3,2,1,0:T(8,128)S(1)}, f32[4,16,8,128]{3,2,1,0:T(8,128)S(1)}, u32[]{:S(2)}, u32[]{:S(2)}) %collective-permute-start.10) | collective-permute-done | bytes 262176 | tf_op jit(solution)/shard_map/ppermute | solution.py:373
  144.2 1.0 regroup.7
  145.3 4.2 %all-to-all-start.3 = ((f32[4,4,16,8,128]{4,3,2,1,0:T(8,128)}), f32[4,4,16,8,128]{4,3,2,1,0:T(8,128)S(1)}, u32[]{:S(2)}, u32[]{:S(2)}) async-start(f32[4,4,16,8,128]{4,3,2,1,0:T(8,128)} %regroup.7), calls=%async_computation.3 | async-start | bytes 2097152 | tf_op jit(solution)/shard_map/all_to_all | solution.py:380
  149.5 3.0 %collective-permute-start.12 = (f32[4,16,8,128]{3,2,1,0:T(8,128)S(1)}, f32[4,16,8,128]{3,2,1,0:T(8,128)S(1)}, u32[]{:S(2)}, u32[]{:S(2)}) collective-permute-start(f32[4,16,8,128]{3,2,1,0:T(8,128)S(1)} %get-tuple-element.35), channel_id=1, source_target_pairs={{0,16},{2,18},{4,20},{6,22},{8,24},{10,26},{12,28},{14,30},{16,0},... | collective-permute-start | bytes 786440 | tf_op jit(solution)/shard_map/ppermute | solution.py:373
  153.0 8.7 %all-to-all-done.3.refs_0_ = f32[4,4,16,8,128]{4,3,2,1,0:T(8,128)S(1)} async-done(((f32[4,4,16,8,128]{4,3,2,1,0:T(8,128)}), f32[4,4,16,8,128]{4,3,2,1,0:T(8,128)S(1)}, u32[]{:S(2)}, u32[]{:S(2)}) %all-to-all-start.3) | async-done | bytes 1048608 | tf_op jit(solution)/shard_map/all_to_all | solution.py:380
  161.6 5.3 %unpack.2.refs_4_ = f32[2,16,16,1024]{3,2,1,0:T(8,128)} custom-call(s32[2]{0:T(128)S(1)} %pad_add_fusion.ids, f32[4,4,16,8,128]{4,3,2,1,0:T(8,128)S(1)} %all-to-all-done.3.refs_0_), custom_call_target="tpu_custom_call" | custom-call | flops 1000 | bytes 1000 | tf_op jit(solution)/shard_map/unpack/pallas_call | solution.py:635
  167.0 3.0 %collective-permute-done.12.refs_2_ = f32[4,16,8,128]{3,2,1,0:T(8,128)S(1)} collective-permute-done((f32[4,16,8,128]{3,2,1,0:T(8,128)S(1)}, f32[4,16,8,128]{3,2,1,0:T(8,128)S(1)}, u32[]{:S(2)}, u32[]{:S(2)}) %collective-permute-start.12) | collective-permute-done | bytes 262176 | tf_op jit(solution)/shard_map/ppermute | solution.py:373
  169.9 4.2 %collective-permute-done.13.refs_3_ = f32[4,16,8,128]{3,2,1,0:T(8,128)S(1)} collective-permute-done((f32[4,16,8,128]{3,2,1,0:T(8,128)S(1)}, f32[4,16,8,128]{3,2,1,0:T(8,128)S(1)}, u32[]{:S(2)}, u32[]{:S(2)}) %collective-permute-start.13) | collective-permute-done | bytes 262176 | tf_op jit(solution)/shard_map/ppermute | solution.py:373
  174.2 5.3 %unpack.3 = f32[2,16,16,1024]{3,2,1,0:T(8,128)} custom-call(s32[2]{0:T(128)S(1)} %pad_add_fusion.ids, f32[4,16,8,128]{3,2,1,0:T(8,128)S(1)} %get-tuple-element.33.refs_4_.refs_0_, f32[4,16,8,128]{3,2,1,0:T(8,128)S(1)} %collective-permute-done.11.refs_1_, f32[4,16,8,128]{3,2,1,0:T(8,128)S(1)} %collective-permute-done.12.refs_2_, ...), custom_call_target="tpu_custom_call", output_to_operand_aliasing={{}: (5, {})} | custom-call | flops 1000 | bytes 1000 | tf_op jit(solution)/shard_map/unpack/pallas_call | solution.py:635
  (98 shorter events, 19.1 us)
Async XLA Ops:
  0.0 69.1 %copy-start = (f32[4,4]{1,0:T(4,128)S(1)}, f32[4,4]{1,0:T(4,128)}, u32[]{:S(2)}) copy-start(f32[4,4]{1,0:T(4,128)} %param.20) | copy-start | bytes 196
  1.7 9.5 %copy-start.2 = (f32[1,1,2,16,16,1024]{5,4,3,2,1,0:T(8,128)S(1)}, f32[1,1,2,16,16,1024]{5,4,3,2,1,0:T(8,128)}, u32[]{:S(2)}) copy-start(f32[1,1,2,16,16,1024]{5,4,3,2,1,0:T(8,128)} %param.19) | copy-start | bytes 6291460
  6.9 34.8 %all-to-all-start = ((f32[4,4,16,8,128]{4,3,2,1,0:T(8,128)}), f32[4,4,16,8,128]{4,3,2,1,0:T(8,128)S(1)}, u32[]{:S(2)}, u32[]{:S(2)}) async-start(f32[4,4,16,8,128]{4,3,2,1,0:T(8,128)} %copy-done.5), calls=%async_computation | async-start | bytes 2097152 | tf_op jit(solution)/shard_map/all_to_all | solution.py:380
  16.1 10.0 %collective-permute-start = (f32[4,16,8,128]{3,2,1,0:T(8,128)S(1)}, f32[4,16,8,128]{3,2,1,0:T(8,128)S(1)}, u32[]{:S(2)}, u32[]{:S(2)}) collective-permute-start(f32[4,16,8,128]{3,2,1,0:T(8,128)S(1)} %get-tuple-element.21), channel_id=1, source_target_pairs={{0,8},{2,10},{4,12},{6,14},{8,0},{10,2},{12,4},{14,6},{16,24},{18,... | collective-permute-start | bytes 786440 | tf_op jit(solution)/shard_map/ppermute | solution.py:373
  16.5 20.6 %collective-permute-start.1 = (f32[4,16,8,128]{3,2,1,0:T(8,128)S(1)}, f32[4,16,8,128]{3,2,1,0:T(8,128)S(1)}, u32[]{:S(2)}, u32[]{:S(2)}) collective-permute-start(f32[4,16,8,128]{3,2,1,0:T(8,128)S(1)} %get-tuple-element.22), channel_id=1, source_target_pairs={{0,16},{2,18},{4,20},{6,22},{8,24},{10,26},{12,28},{14,30},{16,0},... | collective-permute-start | bytes 786440 | tf_op jit(solution)/shard_map/ppermute | solution.py:373
  19.1 22.6 %collective-permute-start.2 = (f32[4,16,8,128]{3,2,1,0:T(8,128)S(1)}, f32[4,16,8,128]{3,2,1,0:T(8,128)S(1)}, u32[]{:S(2)}, u32[]{:S(2)}) collective-permute-start(f32[4,16,8,128]{3,2,1,0:T(8,128)S(1)} %get-tuple-element.23), channel_id=1, source_target_pairs={{0,24},{2,26},{4,28},{6,30},{8,16},{10,18},{12,20},{14,22},{16,8},... | collective-permute-start | bytes 786440 | tf_op jit(solution)/shard_map/ppermute | solution.py:373
  45.9 31.0 %copy-start.3 = (f32[496,8,128]{2,1,0:T(8,128)S(1)}, f32[496,8,128]{2,1,0:T(8,128)}, u32[]{:S(2)}) copy-start(f32[496,8,128]{2,1,0:T(8,128)} %constant.74.clone.lengths) | copy-start | bytes 6094852
  45.9 31.0 %copy-start.9 = (bf16[256,256]{1,0:T(8,128)(2,1)S(1)}, bf16[256,256]{1,0:T(8,128)(2,1)}, u32[]{:S(2)}) copy-start(bf16[256,256]{1,0:T(8,128)(2,1)} %constant.78.clone.first_table) | copy-start | bytes 393220
  45.9 31.0 %copy-start.12 = (f32[2,4,8,128]{3,2,1,0:T(8,128)S(1)}, f32[2,4,8,128]{3,2,1,0:T(8,128)}, u32[]{:S(2)}) copy-start(f32[2,4,8,128]{3,2,1,0:T(8,128)} %constant.77.clone.last_lengths) | copy-start | bytes 98308
  45.9 31.1 %copy-start.13 = (f32[4,8,128]{2,1,0:T(8,128)S(1)}, f32[4,8,128]{2,1,0:T(8,128)}, u32[]{:S(2)}) copy-start(f32[4,8,128]{2,1,0:T(8,128)} %constant.76.clone.last_two) | copy-start | bytes 49156
  45.9 31.1 %copy-start.14 = (f32[2,8,128]{2,1,0:T(8,128)S(1)}, f32[2,8,128]{2,1,0:T(8,128)}, u32[]{:S(2)}) copy-start(f32[2,8,128]{2,1,0:T(8,128)} %constant.75.clone.last_one) | copy-start | bytes 24580
  45.9 15.9 %all-to-all-start.1 = ((f32[4,4,16,8,128]{4,3,2,1,0:T(8,128)}), f32[4,4,16,8,128]{4,3,2,1,0:T(8,128)S(1)}, u32[]{:S(2)}, u32[]{:S(2)}) async-start(f32[4,4,16,8,128]{4,3,2,1,0:T(8,128)} %copy-done.6), calls=%async_computation.1 | async-start | bytes 2097152 | tf_op jit(solution)/shard_map/all_to_all | solution.py:380
  63.4 13.5 %collective-permute-start.6 = (f32[8,2,16,8,128]{4,3,2,1,0:T(8,128)}, f32[8,2,16,8,128]{4,3,2,1,0:T(8,128)S(1)}, u32[]{:S(2)}, u32[]{:S(2)}) collective-permute-start(f32[8,2,16,8,128]{4,3,2,1,0:T(8,128)} %join.2.own), channel_id=1, source_target_pairs={{0,1},{1,0},{2,3},{3,2},{4,5},{5,4},{6,7},{7,6},{8,9},{9,8},{10,11... | collective-permute-start | bytes 3145736 | tf_op jit(solution)/shard_map/ppermute | solution.py:20
  69.7 20.5 %collective-permute-start.3 = (f32[4,16,8,128]{3,2,1,0:T(8,128)}, f32[4,16,8,128]{3,2,1,0:T(8,128)}, u32[]{:S(2)}, u32[]{:S(2)}) collective-permute-start(f32[4,16,8,128]{3,2,1,0:T(8,128)} %copy-done.21), channel_id=1, source_target_pairs={{0,8},{2,10},{4,12},{6,14},{8,0},{10,2},{12,4},{14,6},{16,24},{18,... | collective-permute-start | bytes 786440 | tf_op jit(solution)/shard_map/ppermute | solution.py:373
  69.8 21.3 %collective-permute-start.4 = (f32[4,16,8,128]{3,2,1,0:T(8,128)}, f32[4,16,8,128]{3,2,1,0:T(8,128)}, u32[]{:S(2)}, u32[]{:S(2)}) collective-permute-start(f32[4,16,8,128]{3,2,1,0:T(8,128)} %copy-done.20), channel_id=1, source_target_pairs={{0,16},{2,18},{4,20},{6,22},{8,24},{10,26},{12,28},{14,30},{16,0},... | collective-permute-start | bytes 786440 | tf_op jit(solution)/shard_map/ppermute | solution.py:373
  72.8 24.1 %collective-permute-start.5 = (f32[4,16,8,128]{3,2,1,0:T(8,128)}, f32[4,16,8,128]{3,2,1,0:T(8,128)}, u32[]{:S(2)}, u32[]{:S(2)}) collective-permute-start(f32[4,16,8,128]{3,2,1,0:T(8,128)} %copy-done.19), channel_id=1, source_target_pairs={{0,24},{2,26},{4,28},{6,30},{8,16},{10,18},{12,20},{14,22},{16,8},... | collective-permute-start | bytes 786440 | tf_op jit(solution)/shard_map/ppermute | solution.py:373
  90.1 8.1 %copy-start.22 = (f32[4,16,8,128]{3,2,1,0:T(8,128)}, f32[4,16,8,128]{3,2,1,0:T(8,128)S(1)}, u32[]{:S(2)}) copy-start(f32[4,16,8,128]{3,2,1,0:T(8,128)S(1)} %get-tuple-element.32) | copy-start | bytes 786436
  90.1 8.1 %copy-start.24 = (f32[4,16,8,128]{3,2,1,0:T(8,128)}, f32[4,16,8,128]{3,2,1,0:T(8,128)S(1)}, u32[]{:S(2)}) copy-start(f32[4,16,8,128]{3,2,1,0:T(8,128)S(1)} %get-tuple-element.31) | copy-start | bytes 786436
  90.1 8.1 %copy-start.26 = (f32[4,16,8,128]{3,2,1,0:T(8,128)}, f32[4,16,8,128]{3,2,1,0:T(8,128)S(1)}, u32[]{:S(2)}) copy-start(f32[4,16,8,128]{3,2,1,0:T(8,128)S(1)} %get-tuple-element.30) | copy-start | bytes 786436
  90.2 8.1 %copy-start.28 = (f32[31,32]{1,0:T(8,128)S(1)}, f32[31,32]{1,0:T(8,128)}, u32[]{:S(2)}) copy-start(f32[31,32]{1,0:T(8,128)} %get-tuple-element.37) | copy-start | bytes 11908
  90.2 10.8 %copy-start.16 = (f32[8,128]{1,0:T(8,128)S(1)}, f32[8,128]{1,0:T(8,128)}, u32[]{:S(2)}) copy-start(f32[8,128]{1,0:T(8,128)} %constant.73.clone.waves) | copy-start | bytes 12292
  90.2 10.8 %copy-start.18 = (f32[496]{0:T(512)S(1)}, f32[496]{0:T(512)}, u32[]{:S(2)}) copy-start(f32[496]{0:T(512)} %constant.72.clone.nodes) | copy-start | bytes 5956
  98.1 2.9 %collective-permute-start.7 = (f32[8,2,16,8,128]{4,3,2,1,0:T(8,128)S(1)}, f32[8,2,16,8,128]{4,3,2,1,0:T(8,128)}, u32[]{:S(2)}, u32[]{:S(2)}) collective-permute-start(f32[8,2,16,8,128]{4,3,2,1,0:T(8,128)S(1)} %join.3.own), channel_id=1, source_target_pairs={{0,1},{1,0},{2,3},{3,2},{4,5},{5,4},{6,7},{7,6},{8,9},{9,8},{10,11... | collective-permute-start | bytes 3145736 | tf_op jit(solution)/shard_map/ppermute | solution.py:20
  113.8 30.5 %copy-start.8 = (f32[4,16,8,128]{3,2,1,0:T(8,128)S(1)}, f32[4,16,8,128]{3,2,1,0:T(8,128)}, u32[]{:S(2)}) copy-start(f32[4,16,8,128]{3,2,1,0:T(8,128)} %copy-done.7) | copy-start | bytes 786436
  113.8 30.4 %all-to-all-start.2 = ((f32[4,4,16,8,128]{4,3,2,1,0:T(8,128)}), f32[4,4,16,8,128]{4,3,2,1,0:T(8,128)S(1)}, u32[]{:S(2)}, u32[]{:S(2)}) async-start(f32[4,4,16,8,128]{4,3,2,1,0:T(8,128)} %copy-done.4), calls=%async_computation.2 | async-start | bytes 2097152 | tf_op jit(solution)/shard_map/all_to_all | solution.py:380
  118.0 10.7 %collective-permute-start.8 = (f32[4,16,8,128]{3,2,1,0:T(8,128)S(1)}, f32[4,16,8,128]{3,2,1,0:T(8,128)S(1)}, u32[]{:S(2)}, u32[]{:S(2)}) collective-permute-start(f32[4,16,8,128]{3,2,1,0:T(8,128)S(1)} %copy-done.27), channel_id=1, source_target_pairs={{0,8},{2,10},{4,12},{6,14},{8,0},{10,2},{12,4},{14,6},{16,24},{18,... | collective-permute-start | bytes 786440 | tf_op jit(solution)/shard_map/ppermute | solution.py:373
  118.0 21.0 %collective-permute-start.9 = (f32[4,16,8,128]{3,2,1,0:T(8,128)S(1)}, f32[4,16,8,128]{3,2,1,0:T(8,128)S(1)}, u32[]{:S(2)}, u32[]{:S(2)}) collective-permute-start(f32[4,16,8,128]{3,2,1,0:T(8,128)S(1)} %copy-done.25), channel_id=1, source_target_pairs={{0,16},{2,18},{4,20},{6,22},{8,24},{10,26},{12,28},{14,30},{16,0},... | collective-permute-start | bytes 786440 | tf_op jit(solution)/shard_map/ppermute | solution.py:373
  121.0 23.1 %collective-permute-start.10 = (f32[4,16,8,128]{3,2,1,0:T(8,128)S(1)}, f32[4,16,8,128]{3,2,1,0:T(8,128)S(1)}, u32[]{:S(2)}, u32[]{:S(2)}) collective-permute-start(f32[4,16,8,128]{3,2,1,0:T(8,128)S(1)} %copy-done.23), channel_id=1, source_target_pairs={{0,24},{2,26},{4,28},{6,30},{8,16},{10,18},{12,20},{14,22},{16,8},... | collective-permute-start | bytes 786440 | tf_op jit(solution)/shard_map/ppermute | solution.py:373
  145.3 16.4 %all-to-all-start.3 = ((f32[4,4,16,8,128]{4,3,2,1,0:T(8,128)}), f32[4,4,16,8,128]{4,3,2,1,0:T(8,128)S(1)}, u32[]{:S(2)}, u32[]{:S(2)}) async-start(f32[4,4,16,8,128]{4,3,2,1,0:T(8,128)} %regroup.7), calls=%async_computation.3 | async-start | bytes 2097152 | tf_op jit(solution)/shard_map/all_to_all | solution.py:380
  149.5 17.5 %collective-permute-start.11 = (f32[4,16,8,128]{3,2,1,0:T(8,128)S(1)}, f32[4,16,8,128]{3,2,1,0:T(8,128)S(1)}, u32[]{:S(2)}, u32[]{:S(2)}) collective-permute-start(f32[4,16,8,128]{3,2,1,0:T(8,128)S(1)} %get-tuple-element.34), channel_id=1, source_target_pairs={{0,8},{2,10},{4,12},{6,14},{8,0},{10,2},{12,4},{14,6},{16,24},{18,... | collective-permute-start | bytes 786440 | tf_op jit(solution)/shard_map/ppermute | solution.py:373
  149.5 20.5 %collective-permute-start.12 = (f32[4,16,8,128]{3,2,1,0:T(8,128)S(1)}, f32[4,16,8,128]{3,2,1,0:T(8,128)S(1)}, u32[]{:S(2)}, u32[]{:S(2)}) collective-permute-start(f32[4,16,8,128]{3,2,1,0:T(8,128)S(1)} %get-tuple-element.35), channel_id=1, source_target_pairs={{0,16},{2,18},{4,20},{6,22},{8,24},{10,26},{12,28},{14,30},{16,0},... | collective-permute-start | bytes 786440 | tf_op jit(solution)/shard_map/ppermute | solution.py:373
  152.5 21.7 %collective-permute-start.13 = (f32[4,16,8,128]{3,2,1,0:T(8,128)S(1)}, f32[4,16,8,128]{3,2,1,0:T(8,128)S(1)}, u32[]{:S(2)}, u32[]{:S(2)}) collective-permute-start(f32[4,16,8,128]{3,2,1,0:T(8,128)S(1)} %get-tuple-element.36), channel_id=1, source_target_pairs={{0,24},{2,26},{4,28},{6,30},{8,16},{10,18},{12,20},{14,22},{16,8},... | collective-permute-start | bytes 786440 | tf_op jit(solution)/shard_map/ppermute | solution.py:373
  (15 other events, 33.4 us)

commit v5 on v3

--- a/solution.py
+++ b/solution.py
@@ -299,16 +299,22 @@
 
 
 def pack_kernel(in_ref, out_ref):
-    pack_rows(in_ref, slice(None), out_ref)
+    def step(group, carry):
+        lanes = pl.ds(pl.multiple_of(group * 128, 128), 128)
+        pack_rows(in_ref, lanes, out_ref.at[pl.ds(4 * group, 4)])
+        return carry
+
+    lax.fori_loop(0, 4, step, 0)
 
 
 def pack(weights, chunk):
     return pl.pallas_call(
         pack_kernel,
-        grid=(4,),
-        in_specs=[pl.BlockSpec((2, 16, 16, 128), lambda i: (0, 0, 0, 4 * chunk + i))],
-        out_specs=pl.BlockSpec((4, 16, 8, 128), lambda i: (i, 0, 0, 0)),
+        grid=(1,),
+        in_specs=[pl.BlockSpec((2, 16, 16, 512), lambda i: (0, 0, 0, chunk))],
+        out_specs=pl.BlockSpec((PIECES, 16, 8, 128), lambda i: (0, 0, 0, 0)),
         out_shape=jax.ShapeDtypeStruct((PIECES, 16, 8, 128), jnp.float32),
+        compiler_params=pltpu.CompilerParams(vmem_limit_bytes=VMEM_LIMIT),
         cost_estimate=pl.CostEstimate(flops=10**6, bytes_accessed=2**21, transcendentals=0),
         name="pack",
     )(weights)
@@ -381,7 +387,9 @@
     out_ref[box, 1, t1] = jnp.where(upper, pltpu.roll(low, 4, 0), high)
 
 
-def join_kernel(in_ref, out_ref):
+def join_kernel(in_ref, *refs):
+    out_ref = refs[-1]
+
     def step(box, carry):
         for t1 in range(16):
             merge_halves(out_ref, box, t1, in_ref[2 * box, t1], in_ref[2 * box + 1, t1])
@@ -391,7 +399,7 @@
 
 
 def join_masks_kernel(ids, *refs):
-    bundles, out_ref = refs[:4], refs[4]
+    bundles, out_ref = refs[:4], refs[-1]
     me = ids[0]
     is_low = jnp.broadcast_to(me % 2, (8, 128)) == 0
     for mz in range(4):
@@ -405,7 +413,7 @@
                 merge_halves(out_ref, box, t1, low, high)
 
 
-def join(received, ids=None):
+def join(received, ids=None, after=()):
     in_vmem = pl.BlockSpec(memory_space=pltpu.VMEM)
     if ids is None:
         kernel, operands, in_specs = join_kernel, [received], [in_vmem]
@@ -414,20 +422,20 @@
         in_specs = [pl.BlockSpec(memory_space=pltpu.SMEM)] + [in_vmem] * 4
     return pl.pallas_call(
         kernel,
-        in_specs=in_specs,
+        in_specs=in_specs + [pl.BlockSpec(memory_space=pl.ANY)] * len(after),
         out_specs=in_vmem,
         out_shape=jax.ShapeDtypeStruct((8, 2, 16, 8, 128), jnp.float32),
         compiler_params=pltpu.CompilerParams(vmem_limit_bytes=VMEM_LIMIT),
-        cost_estimate=pl.CostEstimate(flops=10**6, bytes_accessed=2**21, transcendentals=0),
+        cost_estimate=pl.CostEstimate(flops=1000, bytes_accessed=1000, transcendentals=0),
         name="join",
-    )(*operands)
+    )(*operands, *after)
 
 
 def levels_kernel(
-    chunk, by_masks, ids, nodes, own, other, speeds, waves, lengths, last_one, last_two,
+    chunk, ids, nodes, own, other, speeds, waves, lengths, last_one, last_two,
     last_lengths, first_table, second_table, *refs,
 ):
-    outs = refs[:4] if by_masks else refs[0]
+    outs = refs[0]
     boxes_a, boxes_b, sums, turned, mixed, last_phase = refs[-6:]
     row = (chunk * PIECES + ids[0]).astype(jnp.float32)
     core = ids[1]
@@ -578,32 +586,23 @@
 
     def finish_row(major, carry):
         for minor in range(4):
-            if by_masks:
-                finish_box((4 * minor + major) ^ ids[0], outs[minor].at[major])
-            else:
-                finish_box(4 * major + minor, outs.at[4 * major + minor])
+            finish_box(4 * major + minor, outs.at[4 * major + minor])
         return carry
 
     lax.fori_loop(0, 4, finish_row, 0)
 
 
-def levels(chunk, by_masks, ids, own, other, speeds):
+def levels(chunk, ids, own, other, speeds):
     nodes, waves, lengths = node_tables()
     last_one, last_two, last_lengths = final_tables()
     tables = (waves, lengths, last_one, last_two, last_lengths, first_weights(), second_weights())
     in_vmem = pl.BlockSpec(memory_space=pltpu.VMEM)
     in_smem = pl.BlockSpec(memory_space=pltpu.SMEM)
-    if by_masks:
-        out_shape = [jax.ShapeDtypeStruct(BUNDLE, jnp.float32)] * 4
-        out_specs = [in_vmem] * 4
-    else:
-        out_shape = jax.ShapeDtypeStruct((PIECES, 16, 8, 128), jnp.float32)
-        out_specs = in_vmem
     return pl.pallas_call(
-        partial(levels_kernel, chunk, by_masks),
+        partial(levels_kernel, chunk),
         in_specs=[in_smem, in_smem] + [in_vmem] * 10,
-        out_specs=out_specs,
-        out_shape=out_shape,
+        out_specs=in_vmem,
+        out_shape=jax.ShapeDtypeStruct((PIECES, 16, 8, 128), jnp.float32),
         scratch_shapes=[
             pltpu.VMEM((8, 2, 16, 8, 128), jnp.float32),
             pltpu.VMEM((8, 2, 16, 8, 128), jnp.float32),
@@ -613,7 +612,9 @@
             pltpu.VMEM((2, 4, 8, 128), jnp.float32),
         ],
         compiler_params=pltpu.CompilerParams(vmem_limit_bytes=VMEM_LIMIT),
-        cost_estimate=pl.CostEstimate(flops=10**8, bytes_accessed=2**23, transcendentals=0),
+        cost_estimate=pl.CostEstimate(
+            flops=1000, bytes_accessed=4 * 10**8 if chunk else 1000, transcendentals=0
+        ),
         name="levels",
     )(ids, jnp.asarray(nodes), own, other, speeds, *[jnp.asarray(table) for table in tables])
 
@@ -635,45 +636,21 @@
     unpack_rows(refs[0], refs[-1], refs[-2], slice(None))
 
 
-def unpack_masks_kernel(ids, *refs):
-    bundles, out_ref, tiles, rows = refs[:4], refs[-3], refs[-2], refs[-1]
-    me = ids[0]
-
-    def step(mz, carry):
-        group = mz ^ (me // 4)
-        for mxy in range(4):
-            tiles[mxy ^ (me % 4)] = bundles[mxy][mz]
-        unpack_rows(tiles, rows, out_ref, pl.ds(pl.multiple_of(group * 128, 128), 128))
-        return carry
-
-    lax.fori_loop(0, 4, step, 0)
-
-
-def unpack(received, chunk, earlier, ids=None):
-    rows = pltpu.VMEM((4, 128, 128), jnp.float32)
-    if ids is None:
-        kernel, operands, grid = unpack_kernel, [received], (4,)
-        in_specs = [pl.BlockSpec((4, 16, 8, 128), lambda i: (i, 0, 0, 0))]
-        out_spec = pl.BlockSpec((2, 16, 16, 128), lambda i: (0, 0, 0, 4 * chunk + i))
-        scratch = [rows]
-    else:
-        kernel, operands, grid = unpack_masks_kernel, [ids, *received], (1,)
-        in_specs = [pl.BlockSpec(memory_space=pltpu.SMEM)]
-        in_specs += [pl.BlockSpec(BUNDLE, lambda i: (0, 0, 0, 0))] * 4
-        out_spec = pl.BlockSpec((2, 16, 16, 512), lambda i: (0, 0, 0, chunk))
-        scratch = [pltpu.VMEM(BUNDLE, jnp.float32), rows]
+def unpack(received, chunk, earlier):
+    operands = [received]
+    in_specs = [pl.BlockSpec((4, 16, 8, 128), lambda i: (i, 0, 0, 0))]
     aliases = {}
     if earlier is not None:
-        aliases = {len(operands): 0}
+        aliases = {1: 0}
         operands.append(earlier)
         in_specs.append(pl.BlockSpec(memory_space=pl.ANY))
     return pl.pallas_call(
-        kernel,
-        grid=grid,
+        unpack_kernel,
+        grid=(4,),
         in_specs=in_specs,
-        out_specs=out_spec,
+        out_specs=pl.BlockSpec((2, 16, 16, 128), lambda i: (0, 0, 0, 4 * chunk + i)),
         out_shape=jax.ShapeDtypeStruct((2, 16, 16, 1024), jnp.float32),
-        scratch_shapes=scratch,
+        scratch_shapes=[pltpu.VMEM((4, 128, 128), jnp.float32)],
         input_output_aliases=aliases,
         compiler_params=pltpu.CompilerParams(vmem_limit_bytes=VMEM_LIMIT),
         cost_estimate=pl.CostEstimate(flops=10**6, bytes_accessed=2**21, transcendentals=0),
@@ -718,15 +695,13 @@
     second = exchange(regroup(near), 4)
 
     own = join(first)
-    result = levels(0, True, ids, own, partner_2(own, "cores", 0), speeds[0])
-    far = exchange(result, 4)
-    back_first = exchange(regroup(far), 1)
-
-    own = join(second, ids)
-    result = levels(1, False, ids, own, partner_2(own, "cores", 0), speeds[1])
-    back_second = deal(result)
-
-    out = unpack(back_first, 0, None, ids)
+    first = levels(0, ids, own, partner_2(own, "cores", 0), speeds[0])
+    back_first = deal(first)
+
+    own = join(second, ids, [first])
+    back_second = deal(levels(1, ids, own, partner_2(own, "cores", 0), speeds[1]))
+
+    out = unpack(back_first, 0, None)
     out = unpack(back_second, 1, out)
     return out.reshape(weights.shape)
 

time: 152 us -> 165 us (1.086)
  waiting for transfers between devices: 81.3 us -> 94.9 us
  local copies, waits for them, and re-layouts: 1.67 us -> 5.45 us
  Pallas kernels: 37.5 us -> 34.8 us
  starting transfers between devices: 29.7 us -> 27.9 us
    all_to_all x2 -> x3, waiting for transfers between devices: 0.01 us -> 49.6 us  [deal(): return lax.all_to_all(pieces, ('bx', 'by'), 0, 0, tiled=True)]
    ppermute x12 -> x6, waiting for transfers between devices: 77 us -> 40.9 us  [exchange(): moved.append(lax.ppermute(bundles[mask], ('bx', 'by'), pairs))]
    ppermute x12 -> x6, starting transfers between devices: 16.8 us -> 9.83 us  [exchange(): moved.append(lax.ppermute(bundles[mask], ('bx', 'by'), pairs))]
    all_to_all x2 -> x3, starting transfers between devices: 12.8 us -> 18 us  [deal(): return lax.all_to_all(pieces, ('bx', 'by'), 0, 0, tiled=True)]
    unnamed x24 -> x32, local copies, waits for them, and re-layouts: 1.04 us -> 4.82 us
    pallas_call x7, Pallas kernels: 35.7 us -> 33.1 us  [the longest x2 24.7 us: levels(): pl.pallas_call(partial(levels_kernel, chunk), in_specs=[in_smem, in_smem]...]
  transfers between devices with their start and end apart: 16 -> 11, of which waited for: 14 -> 10; matrix products, arithmetic and copies ran while one was open for 1% -> 1% of each run, Pallas kernels for 21% -> 11%
where the time goes in v5:
time: 165 us; the launch traced here: 164 us
  waiting for transfers between devices  94.9 us (58%)
  Pallas kernels  34.8 us (21%)
  starting transfers between devices  27.9 us (17%)
  local copies, waits for them, and re-layouts  5.45 us (3%)
    all_to_all x3, waiting for transfers between devices, deal(): return lax.all_to_all(pieces, ('bx', 'by'), 0, 0, tiled=True)  49.6 us
    ppermute x6, waiting for transfers between devices, exchange(): moved.append(lax.ppermute(bundles[mask], ('bx', 'by'), pairs))  40.9 us
    pallas_call x2, Pallas kernels, levels(): pl.pallas_call(partial(levels_kernel, chunk), in_specs=[in_smem, in_smem]...  24.7 us
    all_to_all x3, starting transfers between devices, deal(): return lax.all_to_all(pieces, ('bx', 'by'), 0, 0, tiled=True)  18 us
    ppermute x6, starting transfers between devices, exchange(): moved.append(lax.ppermute(bundles[mask], ('bx', 'by'), pairs))  9.83 us
    unnamed x32, local copies, waits for them, and re-layouts  4.82 us
    pallas_call x2, Pallas kernels, unpack(): pl.pallas_call(unpack_kernel, grid=(4,), in_specs=in_specs, out_specs=pl....  4.51 us
    ppermute x2, waiting for transfers between devices, partner_2(): return lax.ppermute(value, axis, pairs)  4.47 us
  transfers between devices with their start and end apart: 11, of which 10 were waited for; matrix products, arithmetic and copies ran while one was open for 1% of the time, Pallas kernels for 11%

profile of v5, /device:TPU:10, one launch (start us, length us, event | category | flops | bytes accessed | tf_op | source)
XLA Modules:
  0.0 164.2 jit_solution(17701225457029253124)
XLA Ops:
  0.0 1.6 copy-done.1
  1.6 2.1 %pack.1 = f32[16,16,8,128]{3,2,1,0:T(8,128)} custom-call(f32[2,16,16,1024]{3,2,1,0:T(8,128)S(1)} %bitcast.30), custom_call_target="tpu_custom_call" | custom-call | flops 1000000 | bytes 2097152 | tf_op jit(solution)/shard_map/pack/pallas_call | solution.py:311
  3.8 7.3 %all-to-all-start = ((f32[16,16,8,128]{3,2,1,0:T(8,128)}), f32[16,16,8,128]{3,2,1,0:T(8,128)S(1)}, u32[]{:S(2)}, u32[]{:S(2)}) async-start(f32[16,16,8,128]{3,2,1,0:T(8,128)} %pack.1), calls=%async_computation | async-start | bytes 2097152 | tf_op jit(solution)/shard_map/all_to_all | solution.py:710
  11.1 0.1 stack.94
  11.3 25.7 %all-to-all-done.in_ref = f32[16,16,8,128]{3,2,1,0:T(8,128)S(1)} async-done(((f32[16,16,8,128]{3,2,1,0:T(8,128)}), f32[16,16,8,128]{3,2,1,0:T(8,128)S(1)}, u32[]{:S(2)}, u32[]{:S(2)}) %all-to-all-start) | async-done | bytes 1048608 | tf_op jit(solution)/shard_map/all_to_all | solution.py:710
  37.0 1.0 copy-done.6
  38.0 1.2 copy-done.7
  39.2 0.1 join.2.own
  39.7 0.6 fusion.1
  40.6 1.6 collective-permute-done.6.other
  42.2 12.7 %levels.2.refs_4_ = f32[16,16,8,128]{3,2,1,0:T(8,128)} custom-call(s32[2]{0:T(128)S(1)} %pad_add_fusion.ids, f32[496]{0:T(512)S(1)} %copy-done.13, f32[8,2,16,8,128]{4,3,2,1,0:T(8,128)S(1)} %join.2.own, f32[8,2,16,8,128]{4,3,2,1,0:T(8,128)} %collective-permute-done.6.other, f32[31,128]{1,0:T(8,128)S(1)} %tile.24.speeds, f32[8,128]{1,0:T(8,128)S(1)} %copy-done.12, ...), custom_call_target="tpu_custom_call" | custom-call | flops 1000 | bytes 1000 | tf_op jit(solution)/shard_map/levels/pallas_call | solution.py:601
  54.9 4.5 %all-to-all-start.2 = ((f32[16,16,8,128]{3,2,1,0:T(8,128)}), f32[16,16,8,128]{3,2,1,0:T(8,128)S(1)}, u32[]{:S(2)}, u32[]{:S(2)}) async-start(f32[16,16,8,128]{3,2,1,0:T(8,128)} %levels.2.refs_4_), calls=%async_computation.2 | async-start | bytes 2097152 | tf_op jit(solution)/shard_map/all_to_all | solution.py:710
  59.4 1.7 %pack_masks.1 = (f32[4,16,8,128]{3,2,1,0:T(8,128)S(1)}, f32[4,16,8,128]{3,2,1,0:T(8,128)S(1)}, f32[4,16,8,128]{3,2,1,0:T(8,128)S(1)}, f32[4,16,8,128]{3,2,1,0:T(8,128)S(1)}) custom-call(s32[2]{0:T(128)S(1)} %pad_add_fusion.ids, f32[2,16,16,1024]{3,2,1,0:T(8,128)S(1)} %bitcast.31), custom_call_target="tpu_custom_call" | custom-call | flops 1000000 | bytes 2097152 | tf_op jit(solution)/shard_map/pack_masks/pallas_call | solution.py:341
  61.1 1.5 collective-permute-start
  62.6 0.6 collective-permute-start.1
  63.2 1.5 collective-permute-start.2
  64.7 6.4 %collective-permute-done.refs_1_ = f32[4,16,8,128]{3,2,1,0:T(8,128)S(1)} collective-permute-done((f32[4,16,8,128]{3,2,1,0:T(8,128)S(1)}, f32[4,16,8,128]{3,2,1,0:T(8,128)S(1)}, u32[]{:S(2)}, u32[]{:S(2)}) %collective-permute-start) | collective-permute-done | bytes 262176 | tf_op jit(solution)/shard_map/ppermute | solution.py:380
  71.0 4.3 %collective-permute-done.1.refs_2_ = f32[4,16,8,128]{3,2,1,0:T(8,128)S(1)} collective-permute-done((f32[4,16,8,128]{3,2,1,0:T(8,128)S(1)}, f32[4,16,8,128]{3,2,1,0:T(8,128)S(1)}, u32[]{:S(2)}, u32[]{:S(2)}) %collective-permute-start.1) | collective-permute-done | bytes 262176 | tf_op jit(solution)/shard_map/ppermute | solution.py:380
  75.3 8.3 %collective-permute-done.2.refs_3_ = f32[4,16,8,128]{3,2,1,0:T(8,128)S(1)} collective-permute-done((f32[4,16,8,128]{3,2,1,0:T(8,128)S(1)}, f32[4,16,8,128]{3,2,1,0:T(8,128)S(1)}, u32[]{:S(2)}, u32[]{:S(2)}) %collective-permute-start.2) | collective-permute-done | bytes 262176 | tf_op jit(solution)/shard_map/ppermute | solution.py:380
  83.7 2.8 %collective-permute-start.3 = (f32[4,16,8,128]{3,2,1,0:T(8,128)S(1)}, f32[4,16,8,128]{3,2,1,0:T(8,128)S(1)}, u32[]{:S(2)}, u32[]{:S(2)}) collective-permute-start(f32[4,16,8,128]{3,2,1,0:T(8,128)S(1)} %get-tuple-element.18), channel_id=1, source_target_pairs={{0,8},{2,10},{4,12},{6,14},{8,0},{10,2},{12,4},{14,6},{16,24},{18,... | collective-permute-start | bytes 786440 | tf_op jit(solution)/shard_map/ppermute | solution.py:380
  86.4 3.5 %collective-permute-start.4 = (f32[4,16,8,128]{3,2,1,0:T(8,128)S(1)}, f32[4,16,8,128]{3,2,1,0:T(8,128)S(1)}, u32[]{:S(2)}, u32[]{:S(2)}) collective-permute-start(f32[4,16,8,128]{3,2,1,0:T(8,128)S(1)} %get-tuple-element.19), channel_id=1, source_target_pairs={{0,16},{2,18},{4,20},{6,22},{8,24},{10,26},{12,28},{14,30},{16,0},... | collective-permute-start | bytes 786440 | tf_op jit(solution)/shard_map/ppermute | solution.py:380
  90.0 6.8 %collective-permute-done.3.refs_1_ = f32[4,16,8,128]{3,2,1,0:T(8,128)S(1)} collective-permute-done((f32[4,16,8,128]{3,2,1,0:T(8,128)S(1)}, f32[4,16,8,128]{3,2,1,0:T(8,128)S(1)}, u32[]{:S(2)}, u32[]{:S(2)}) %collective-permute-start.3) | collective-permute-done | bytes 262176 | tf_op jit(solution)/shard_map/ppermute | solution.py:380
  96.8 10.4 %collective-permute-done.4.refs_2_ = f32[4,16,8,128]{3,2,1,0:T(8,128)S(1)} collective-permute-done((f32[4,16,8,128]{3,2,1,0:T(8,128)S(1)}, f32[4,16,8,128]{3,2,1,0:T(8,128)S(1)}, u32[]{:S(2)}, u32[]{:S(2)}) %collective-permute-start.4) | collective-permute-done | bytes 262176 | tf_op jit(solution)/shard_map/ppermute | solution.py:380
  107.2 4.7 %collective-permute-done.5.refs_3_ = f32[4,16,8,128]{3,2,1,0:T(8,128)S(1)} collective-permute-done((f32[4,16,8,128]{3,2,1,0:T(8,128)S(1)}, f32[4,16,8,128]{3,2,1,0:T(8,128)S(1)}, u32[]{:S(2)}, u32[]{:S(2)}) %collective-permute-start.5) | collective-permute-done | bytes 262176 | tf_op jit(solution)/shard_map/ppermute | solution.py:380
  111.9 1.6 join.3.own
  113.6 2.9 %collective-permute-done.7.other = f32[8,2,16,8,128]{4,3,2,1,0:T(8,128)} collective-permute-done((f32[8,2,16,8,128]{4,3,2,1,0:T(8,128)}, f32[8,2,16,8,128]{4,3,2,1,0:T(8,128)}, u32[]{:S(2)}, u32[]{:S(2)}) %collective-permute-start.7) | collective-permute-done | bytes 1048608 | tf_op jit(solution)/shard_map/ppermute | solution.py:20
  116.5 12.0 %levels.3 = f32[16,16,8,128]{3,2,1,0:T(8,128)S(1)} custom-call(s32[2]{0:T(128)S(1)} %pad_add_fusion.ids, f32[496]{0:T(512)S(1)} %copy-done.13, f32[8,2,16,8,128]{4,3,2,1,0:T(8,128)} %join.3.own, f32[8,2,16,8,128]{4,3,2,1,0:T(8,128)} %collective-permute-done.7.other, f32[31,128]{1,0:T(8,128)S(1)} %tile.26.speeds, f32[8,128]{1,0:T(8,128)S(1)} %copy-done.12, ...), custom_call_target="tpu_custom_call" | custom-call | flops 1000 | bytes 400000000 | tf_op jit(solution)/shard_map/levels/pallas_call | solution.py:601
  128.6 1.0 copy-done.5
  129.6 6.1 %all-to-all-start.1 = ((f32[16,16,8,128]{3,2,1,0:T(8,128)}), f32[16,16,8,128]{3,2,1,0:T(8,128)S(1)}, u32[]{:S(2)}, u32[]{:S(2)}) async-start(f32[16,16,8,128]{3,2,1,0:T(8,128)} %copy-done.5), calls=%async_computation.1 | async-start | bytes 2097152 | tf_op jit(solution)/shard_map/all_to_all | solution.py:710
  135.7 2.3 %unpack.2.refs_1_ = f32[2,16,16,1024]{3,2,1,0:T(8,128)} custom-call(f32[16,16,8,128]{3,2,1,0:T(8,128)S(1)} %all-to-all-done.2.refs_0_), custom_call_target="tpu_custom_call" | custom-call | flops 1000000 | bytes 2097152 | tf_op jit(solution)/shard_map/unpack/pallas_call | solution.py:647
  138.0 23.9 %all-to-all-done.1.refs_0_ = f32[16,16,8,128]{3,2,1,0:T(8,128)S(1)} async-done(((f32[16,16,8,128]{3,2,1,0:T(8,128)}), f32[16,16,8,128]{3,2,1,0:T(8,128)S(1)}, u32[]{:S(2)}, u32[]{:S(2)}) %all-to-all-start.1) | async-done | bytes 1048608 | tf_op jit(solution)/shard_map/all_to_all | solution.py:710
  161.9 2.2 %unpack.3 = f32[2,16,16,1024]{3,2,1,0:T(8,128)} custom-call(f32[16,16,8,128]{3,2,1,0:T(8,128)S(1)} %all-to-all-done.1.refs_0_, f32[2,16,16,1024]{3,2,1,0:T(8,128)} %unpack.2.refs_1_), custom_call_target="tpu_custom_call", output_to_operand_aliasing={{}: (1, {})} | custom-call | flops 1000000 | bytes 2097152 | tf_op jit(solution)/shard_map/unpack/pallas_call | solution.py:647
  (55 shorter events, 0.9 us)
Async XLA Ops:
  0.0 39.7 %copy-start = (f32[4,4]{1,0:T(4,128)S(1)}, f32[4,4]{1,0:T(4,128)}, u32[]{:S(2)}) copy-start(f32[4,4]{1,0:T(4,128)} %param.20) | copy-start | bytes 196
  0.0 1.6 copy-start.1
  1.6 9.6 %copy-start.14 = (f32[31]{0:T(128)S(1)}, f32[31]{0:T(128)}, u32[]{:S(2)}) copy-start(f32[31]{0:T(128)} %constant.71.clone) | copy-start | bytes 376
  1.6 9.7 %copy-start.15 = (f32[31]{0:T(128)S(1)}, f32[31]{0:T(128)}, u32[]{:S(2)}) copy-start(f32[31]{0:T(128)} %constant.82) | copy-start | bytes 376
  1.6 40.6 %copy-start.10 = (f32[4,8,128]{2,1,0:T(8,128)S(1)}, f32[4,8,128]{2,1,0:T(8,128)}, u32[]{:S(2)}) copy-start(f32[4,8,128]{2,1,0:T(8,128)} %constant.76.clone.last_two) | copy-start | bytes 49156
  1.6 40.6 %copy-start.11 = (f32[2,8,128]{2,1,0:T(8,128)S(1)}, f32[2,8,128]{2,1,0:T(8,128)}, u32[]{:S(2)}) copy-start(f32[2,8,128]{2,1,0:T(8,128)} %constant.75.clone.last_one) | copy-start | bytes 24580
  1.6 40.6 %copy-start.13 = (f32[496]{0:T(512)S(1)}, f32[496]{0:T(512)}, u32[]{:S(2)}) copy-start(f32[496]{0:T(512)} %constant.72.clone.nodes) | copy-start | bytes 5956
  3.7 38.4 %copy-start.3 = (f32[496,8,128]{2,1,0:T(8,128)S(1)}, f32[496,8,128]{2,1,0:T(8,128)}, u32[]{:S(2)}) copy-start(f32[496,8,128]{2,1,0:T(8,128)} %constant.74.clone.lengths) | copy-start | bytes 6094852
  3.7 38.4 %copy-start.8 = (bf16[256,256]{1,0:T(8,128)(2,1)S(1)}, bf16[256,256]{1,0:T(8,128)(2,1)}, u32[]{:S(2)}) copy-start(bf16[256,256]{1,0:T(8,128)(2,1)} %constant.78.clone.first_table) | copy-start | bytes 393220
  3.8 38.5 %copy-start.9 = (f32[2,4,8,128]{3,2,1,0:T(8,128)S(1)}, f32[2,4,8,128]{3,2,1,0:T(8,128)}, u32[]{:S(2)}) copy-start(f32[2,4,8,128]{3,2,1,0:T(8,128)} %constant.77.clone.last_lengths) | copy-start | bytes 98308
  3.8 38.5 %copy-start.12 = (f32[8,128]{1,0:T(8,128)S(1)}, f32[8,128]{1,0:T(8,128)}, u32[]{:S(2)}) copy-start(f32[8,128]{1,0:T(8,128)} %constant.73.clone.waves) | copy-start | bytes 12292
  3.8 33.3 %all-to-all-start = ((f32[16,16,8,128]{3,2,1,0:T(8,128)}), f32[16,16,8,128]{3,2,1,0:T(8,128)S(1)}, u32[]{:S(2)}, u32[]{:S(2)}) async-start(f32[16,16,8,128]{3,2,1,0:T(8,128)} %pack.1), calls=%async_computation | async-start | bytes 2097152 | tf_op jit(solution)/shard_map/all_to_all | solution.py:710
  37.0 1.0 copy-start.6
  38.0 1.2 copy-start.7
  39.3 2.9 %collective-permute-start.6 = (f32[8,2,16,8,128]{4,3,2,1,0:T(8,128)S(1)}, f32[8,2,16,8,128]{4,3,2,1,0:T(8,128)}, u32[]{:S(2)}, u32[]{:S(2)}) collective-permute-start(f32[8,2,16,8,128]{4,3,2,1,0:T(8,128)S(1)} %join.2.own), channel_id=1, source_target_pairs={{0,1},{1,0},{2,3},{3,2},{4,5},{5,4},{6,7},{7,6},{8,9},{9,8},{10,11... | collective-permute-start | bytes 3145736 | tf_op jit(solution)/shard_map/ppermute | solution.py:20
  54.9 4.5 %copy-start.2 = (f32[1,1,2,16,16,1024]{5,4,3,2,1,0:T(8,128)S(1)}, f32[1,1,2,16,16,1024]{5,4,3,2,1,0:T(8,128)}, u32[]{:S(2)}) copy-start(f32[1,1,2,16,16,1024]{5,4,3,2,1,0:T(8,128)} %param.19) | copy-start | bytes 6291460
  54.9 74.6 %all-to-all-start.2 = ((f32[16,16,8,128]{3,2,1,0:T(8,128)}), f32[16,16,8,128]{3,2,1,0:T(8,128)S(1)}, u32[]{:S(2)}, u32[]{:S(2)}) async-start(f32[16,16,8,128]{3,2,1,0:T(8,128)} %levels.2.refs_4_), calls=%async_computation.2 | async-start | bytes 2097152 | tf_op jit(solution)/shard_map/all_to_all | solution.py:710
  61.1 9.9 %collective-permute-start = (f32[4,16,8,128]{3,2,1,0:T(8,128)S(1)}, f32[4,16,8,128]{3,2,1,0:T(8,128)S(1)}, u32[]{:S(2)}, u32[]{:S(2)}) collective-permute-start(f32[4,16,8,128]{3,2,1,0:T(8,128)S(1)} %get-tuple-element.14), channel_id=1, source_target_pairs={{0,2},{2,0},{4,6},{6,4},{8,10},{10,8},{12,14},{14,12},{16,18},{18,... | collective-permute-start | bytes 786440 | tf_op jit(solution)/shard_map/ppermute | solution.py:380
  62.6 12.7 %collective-permute-start.1 = (f32[4,16,8,128]{3,2,1,0:T(8,128)S(1)}, f32[4,16,8,128]{3,2,1,0:T(8,128)S(1)}, u32[]{:S(2)}, u32[]{:S(2)}) collective-permute-start(f32[4,16,8,128]{3,2,1,0:T(8,128)S(1)} %get-tuple-element.15), channel_id=1, source_target_pairs={{0,4},{2,6},{4,0},{6,2},{8,12},{10,14},{12,8},{14,10},{16,20},{18,... | collective-permute-start | bytes 786440 | tf_op jit(solution)/shard_map/ppermute | solution.py:380
  63.2 20.4 %collective-permute-start.2 = (f32[4,16,8,128]{3,2,1,0:T(8,128)S(1)}, f32[4,16,8,128]{3,2,1,0:T(8,128)S(1)}, u32[]{:S(2)}, u32[]{:S(2)}) collective-permute-start(f32[4,16,8,128]{3,2,1,0:T(8,128)S(1)} %get-tuple-element.16), channel_id=1, source_target_pairs={{0,6},{2,4},{4,2},{6,0},{8,14},{10,12},{12,10},{14,8},{16,22},{18,... | collective-permute-start | bytes 786440 | tf_op jit(solution)/shard_map/ppermute | solution.py:380
  83.6 32.9 %copy-start.4 = (f32[496,8,128]{2,1,0:T(8,128)S(1)}, f32[496,8,128]{2,1,0:T(8,128)}, u32[]{:S(2)}) copy-start(f32[496,8,128]{2,1,0:T(8,128)} %constant.74.clone.lengths) | copy-start | bytes 6094852
  83.7 13.1 %collective-permute-start.3 = (f32[4,16,8,128]{3,2,1,0:T(8,128)S(1)}, f32[4,16,8,128]{3,2,1,0:T(8,128)S(1)}, u32[]{:S(2)}, u32[]{:S(2)}) collective-permute-start(f32[4,16,8,128]{3,2,1,0:T(8,128)S(1)} %get-tuple-element.18), channel_id=1, source_target_pairs={{0,8},{2,10},{4,12},{6,14},{8,0},{10,2},{12,4},{14,6},{16,24},{18,... | collective-permute-start | bytes 786440 | tf_op jit(solution)/shard_map/ppermute | solution.py:380
  86.4 20.7 %collective-permute-start.4 = (f32[4,16,8,128]{3,2,1,0:T(8,128)S(1)}, f32[4,16,8,128]{3,2,1,0:T(8,128)S(1)}, u32[]{:S(2)}, u32[]{:S(2)}) collective-permute-start(f32[4,16,8,128]{3,2,1,0:T(8,128)S(1)} %get-tuple-element.19), channel_id=1, source_target_pairs={{0,16},{2,18},{4,20},{6,22},{8,24},{10,26},{12,28},{14,30},{16,0},... | collective-permute-start | bytes 786440 | tf_op jit(solution)/shard_map/ppermute | solution.py:380
  90.0 21.9 %collective-permute-start.5 = (f32[4,16,8,128]{3,2,1,0:T(8,128)S(1)}, f32[4,16,8,128]{3,2,1,0:T(8,128)S(1)}, u32[]{:S(2)}, u32[]{:S(2)}) collective-permute-start(f32[4,16,8,128]{3,2,1,0:T(8,128)S(1)} %get-tuple-element.20), channel_id=1, source_target_pairs={{0,24},{2,26},{4,28},{6,30},{8,16},{10,18},{12,20},{14,22},{16,8},... | collective-permute-start | bytes 786440 | tf_op jit(solution)/shard_map/ppermute | solution.py:380
  113.5 3.0 %collective-permute-start.7 = (f32[8,2,16,8,128]{4,3,2,1,0:T(8,128)}, f32[8,2,16,8,128]{4,3,2,1,0:T(8,128)}, u32[]{:S(2)}, u32[]{:S(2)}) collective-permute-start(f32[8,2,16,8,128]{4,3,2,1,0:T(8,128)} %join.3.own), channel_id=1, source_target_pairs={{0,1},{1,0},{2,3},{3,2},{4,5},{5,4},{6,7},{7,6},{8,9},{9,8},{10,11... | collective-permute-start | bytes 3145736 | tf_op jit(solution)/shard_map/ppermute | solution.py:20
  128.6 1.0 copy-start.5
  129.6 32.3 %all-to-all-start.1 = ((f32[16,16,8,128]{3,2,1,0:T(8,128)}), f32[16,16,8,128]{3,2,1,0:T(8,128)S(1)}, u32[]{:S(2)}, u32[]{:S(2)}) async-start(f32[16,16,8,128]{3,2,1,0:T(8,128)} %copy-done.5), calls=%async_computation.1 | async-start | bytes 2097152 | tf_op jit(solution)/shard_map/all_to_all | solution.py:710

commit v6 on v5

--- a/solution.py
+++ b/solution.py
@@ -320,21 +320,28 @@
     )(weights)
 
 
+BUNDLE = (4, 16, 8, 128)
+
+
+def bundles_of(by_z):
+    shapes = [(4,) + BUNDLE] if by_z else [BUNDLE] * 4
+    return [jax.ShapeDtypeStruct(shape, jnp.float32) for shape in shapes]
+
+
+def entry_of(bundles, by_z, z, mask):
+    return bundles[0].at[z, mask] if by_z else bundles[mask].at[z]
+
+
 def pack_masks_kernel(ids, in_ref, *refs):
     outs, tiles = refs[:4], refs[4]
-    me = ids[0]
-
-    def step(mz, carry):
-        group = mz ^ (me // 4)
-        pack_rows(in_ref, pl.ds(pl.multiple_of(group * 128, 128), 128), tiles)
-        for mxy in range(4):
-            outs[mxy][mz] = tiles[mxy ^ (me % 4)]
+
+    def step(z, carry):
+        pack_rows(in_ref, pl.ds(pl.multiple_of(z * 128, 128), 128), tiles)
+        for mask in range(4):
+            outs[mask][z] = tiles[mask ^ (ids[0] % 4)]
         return carry
 
     lax.fori_loop(0, 4, step, 0)
-
-
-BUNDLE = (4, 16, 8, 128)
 
 
 def pack_masks(weights, ids, chunk):
@@ -346,7 +353,7 @@
             pl.BlockSpec((2, 16, 16, 512), lambda i: (0, 0, 0, chunk)),
         ],
         out_specs=[pl.BlockSpec(BUNDLE, lambda i: (0, 0, 0, 0))] * 4,
-        out_shape=[jax.ShapeDtypeStruct(BUNDLE, jnp.float32)] * 4,
+        out_shape=bundles_of(False),
         scratch_shapes=[pltpu.VMEM(BUNDLE, jnp.float32)],
         compiler_params=pltpu.CompilerParams(vmem_limit_bytes=VMEM_LIMIT),
         cost_estimate=pl.CostEstimate(flops=10**6, bytes_accessed=2**21, transcendentals=0),
@@ -354,31 +361,44 @@
     )(ids, weights)
 
 
-def regroup_kernel(*refs):
-    for first in range(4):
-        for second in range(4):
-            refs[4 + second][first] = refs[first][second]
-
-
-def regroup(bundles):
+def regroup_kernel(by_z, *refs):
+    outs = refs[-4:] if by_z else refs[-1:]
+
+    def step(z, carry):
+        for mask in range(4):
+            entry_of(outs, not by_z, z, mask)[...] = entry_of(refs, by_z, z, mask)[...]
+        return carry
+
+    lax.fori_loop(0, 4, step, 0)
+
+
+def regroup(bundles, by_z, after=()):
     in_vmem = pl.BlockSpec(memory_space=pltpu.VMEM)
+    shapes = bundles_of(not by_z)
     return pl.pallas_call(
-        regroup_kernel,
-        in_specs=[in_vmem] * 4,
-        out_specs=[in_vmem] * 4,
-        out_shape=[jax.ShapeDtypeStruct(BUNDLE, jnp.float32)] * 4,
+        partial(regroup_kernel, by_z),
+        in_specs=[in_vmem] * len(bundles) + [pl.BlockSpec(memory_space=pl.ANY)] * len(after),
+        out_specs=[in_vmem] * len(shapes),
+        out_shape=shapes,
         compiler_params=pltpu.CompilerParams(vmem_limit_bytes=VMEM_LIMIT),
         cost_estimate=pl.CostEstimate(flops=10**5, bytes_accessed=2**21, transcendentals=0),
         name="regroup",
-    )(*bundles)
-
-
-def exchange(bundles, unit):
+    )(*bundles, *after)
+
+
+def cross_xy(bundles):
     moved = [bundles[0]]
     for mask in range(1, 4):
-        pairs = [(source, source ^ (mask * unit)) for source in range(PIECES)]
+        pairs = [(source, source ^ mask) for source in range(PIECES)]
         moved.append(lax.ppermute(bundles[mask], ("bx", "by"), pairs))
     return moved
+
+
+def deal_z(bundles):
+    groups = [[4 * z + xy for z in range(4)] for xy in range(4)]
+    return [
+        lax.all_to_all(bundles[0], ("bx", "by"), 0, 0, axis_index_groups=groups, tiled=True)
+    ]
 
 
 def merge_halves(out_ref, box, t1, low, high):
@@ -399,43 +419,47 @@
 
 
 def join_masks_kernel(ids, *refs):
-    bundles, out_ref = refs[:4], refs[-1]
+    bundles, out_ref = refs[:1], refs[-1]
     me = ids[0]
     is_low = jnp.broadcast_to(me % 2, (8, 128)) == 0
-    for mz in range(4):
+
+    def step(z, carry):
         for mx in range(2):
-            box = (2 * mz + mx) ^ (me // 2)
+            box = 2 * z + (mx ^ (me // 2 % 2))
             for t1 in range(16):
-                mine = bundles[mz][2 * mx, t1]
-                partner = bundles[mz][2 * mx + 1, t1]
+                mine = entry_of(bundles, True, z, 2 * mx)[t1]
+                partner = entry_of(bundles, True, z, 2 * mx + 1)[t1]
                 low = jnp.where(is_low, mine, partner)
                 high = jnp.where(is_low, partner, mine)
                 merge_halves(out_ref, box, t1, low, high)
+        return carry
+
+    lax.fori_loop(0, 4, step, 0)
 
 
 def join(received, ids=None, after=()):
     in_vmem = pl.BlockSpec(memory_space=pltpu.VMEM)
     if ids is None:
-        kernel, operands, in_specs = join_kernel, [received], [in_vmem]
+        kernel, operands, in_specs = join_kernel, received, [in_vmem]
     else:
         kernel, operands = join_masks_kernel, [ids, *received]
-        in_specs = [pl.BlockSpec(memory_space=pltpu.SMEM)] + [in_vmem] * 4
+        in_specs = [pl.BlockSpec(memory_space=pltpu.SMEM), in_vmem]
     return pl.pallas_call(
         kernel,
         in_specs=in_specs + [pl.BlockSpec(memory_space=pl.ANY)] * len(after),
         out_specs=in_vmem,
         out_shape=jax.ShapeDtypeStruct((8, 2, 16, 8, 128), jnp.float32),
         compiler_params=pltpu.CompilerParams(vmem_limit_bytes=VMEM_LIMIT),
-        cost_estimate=pl.CostEstimate(flops=1000, bytes_accessed=1000, transcendentals=0),
+        cost_estimate=pl.CostEstimate(flops=10**6, bytes_accessed=2**21, transcendentals=0),
         name="join",
     )(*operands, *after)
 
 
 def levels_kernel(
-    chunk, ids, nodes, own, other, speeds, waves, lengths, last_one, last_two,
+    chunk, by_z, ids, nodes, own, other, speeds, waves, lengths, last_one, last_two,
     last_lengths, first_table, second_table, *refs,
 ):
-    outs = refs[0]
+    outs = refs[:-6]
     boxes_a, boxes_b, sums, turned, mixed, last_phase = refs[-6:]
     row = (chunk * PIECES + ids[0]).astype(jnp.float32)
     core = ids[1]
@@ -584,25 +608,25 @@
                 out[high * 4 + a] = real * cosine - imag * sine
                 out[8 + high * 4 + a] = real * sine + imag * cosine
 
-    def finish_row(major, carry):
-        for minor in range(4):
-            finish_box(4 * major + minor, outs.at[4 * major + minor])
+    def finish_row(z, carry):
+        for mask in range(4):
+            finish_box(4 * z + (mask ^ (ids[0] % 4)), entry_of(outs, by_z, z, mask))
         return carry
 
     lax.fori_loop(0, 4, finish_row, 0)
 
 
-def levels(chunk, ids, own, other, speeds):
+def levels(chunk, by_z, ids, own, other, speeds):
     nodes, waves, lengths = node_tables()
     last_one, last_two, last_lengths = final_tables()
     tables = (waves, lengths, last_one, last_two, last_lengths, first_weights(), second_weights())
     in_vmem = pl.BlockSpec(memory_space=pltpu.VMEM)
     in_smem = pl.BlockSpec(memory_space=pltpu.SMEM)
     return pl.pallas_call(
-        partial(levels_kernel, chunk),
+        partial(levels_kernel, chunk, by_z),
         in_specs=[in_smem, in_smem] + [in_vmem] * 10,
-        out_specs=in_vmem,
-        out_shape=jax.ShapeDtypeStruct((PIECES, 16, 8, 128), jnp.float32),
+        out_specs=[in_vmem] * len(bundles_of(by_z)),
+        out_shape=bundles_of(by_z),
         scratch_shapes=[
             pltpu.VMEM((8, 2, 16, 8, 128), jnp.float32),
             pltpu.VMEM((8, 2, 16, 8, 128), jnp.float32),
@@ -612,9 +636,7 @@
             pltpu.VMEM((2, 4, 8, 128), jnp.float32),
         ],
         compiler_params=pltpu.CompilerParams(vmem_limit_bytes=VMEM_LIMIT),
-        cost_estimate=pl.CostEstimate(
-            flops=1000, bytes_accessed=4 * 10**8 if chunk else 1000, transcendentals=0
-        ),
+        cost_estimate=pl.CostEstimate(flops=10**8, bytes_accessed=2**23, transcendentals=0),
         name="levels",
     )(ids, jnp.asarray(nodes), own, other, speeds, *[jnp.asarray(table) for table in tables])
 
@@ -632,25 +654,32 @@
                 out_ref[part, high * 8 + t1, :, lanes] = rows[block, pl.ds(t1, 16, stride=8), :]
 
 
-def unpack_kernel(*refs):
-    unpack_rows(refs[0], refs[-1], refs[-2], slice(None))
-
-
-def unpack(received, chunk, earlier):
-    operands = [received]
-    in_specs = [pl.BlockSpec((4, 16, 8, 128), lambda i: (i, 0, 0, 0))]
+def unpack_kernel(by_z, ids, *refs):
+    bundles, out_ref, tiles, rows = refs[:-3], refs[-3], refs[-2], refs[-1]
+    for mask in range(4):
+        tiles[mask ^ (ids[0] % 4)] = entry_of(bundles, by_z, 0, mask)[...]
+    unpack_rows(tiles, rows, out_ref, slice(None))
+
+
+def unpack(received, ids, chunk, by_z, earlier):
+    operands = [ids, *received]
+    in_specs = [pl.BlockSpec(memory_space=pltpu.SMEM)]
+    if by_z:
+        in_specs.append(pl.BlockSpec((1,) + BUNDLE, lambda z: (z, 0, 0, 0, 0)))
+    else:
+        in_specs += [pl.BlockSpec((1,) + BUNDLE[1:], lambda z: (z, 0, 0, 0))] * 4
     aliases = {}
     if earlier is not None:
-        aliases = {1: 0}
+        aliases = {len(operands): 0}
         operands.append(earlier)
         in_specs.append(pl.BlockSpec(memory_space=pl.ANY))
     return pl.pallas_call(
-        unpack_kernel,
+        partial(unpack_kernel, by_z),
         grid=(4,),
         in_specs=in_specs,
-        out_specs=pl.BlockSpec((2, 16, 16, 128), lambda i: (0, 0, 0, 4 * chunk + i)),
+        out_specs=pl.BlockSpec((2, 16, 16, 128), lambda z: (0, 0, 0, 4 * chunk + z)),
         out_shape=jax.ShapeDtypeStruct((2, 16, 16, 1024), jnp.float32),
-        scratch_shapes=[pltpu.VMEM((4, 128, 128), jnp.float32)],
+        scratch_shapes=[pltpu.VMEM(BUNDLE, jnp.float32), pltpu.VMEM((4, 128, 128), jnp.float32)],
         input_output_aliases=aliases,
         compiler_params=pltpu.CompilerParams(vmem_limit_bytes=VMEM_LIMIT),
         cost_estimate=pl.CostEstimate(flops=10**6, bytes_accessed=2**21, transcendentals=0),
@@ -691,18 +720,21 @@
     speeds = speed_tables(speed_modes, core)
 
     first = deal(pack(local, 0))
-    near = exchange(pack_masks(local, ids, 1), 1)
-    second = exchange(regroup(near), 4)
-
-    own = join(first)
-    first = levels(0, ids, own, partner_2(own, "cores", 0), speeds[0])
-    back_first = deal(first)
-
-    own = join(second, ids, [first])
-    back_second = deal(levels(1, ids, own, partner_2(own, "cores", 0), speeds[1]))
-
-    out = unpack(back_first, 0, None)
-    out = unpack(back_second, 1, out)
+    grouped = regroup(cross_xy(pack_masks(local, ids, 1)), False)
+    second = deal_z(grouped)
+
+    own = join([first], None, grouped)
+    first = levels(0, True, ids, own, partner_2(own, "cores", 0), speeds[0])
+    back_first = deal_z(first)
+
+    own = join(second, ids, first)
+    second = levels(1, False, ids, own, partner_2(own, "cores", 0), speeds[1])
+    grouped = regroup(cross_xy(second), False)
+    back_second = deal_z(grouped)
+
+    back_first = cross_xy(regroup(back_first, True, grouped))
+    out = unpack(back_first, ids, 0, False, None)
+    out = unpack(back_second, ids, 1, True, out)
     return out.reshape(weights.shape)
 
 

time: 165 us -> 141 us (0.85)
  the two profiles are of different devices: /device:TPU:10 before, /device:TPU:0 now
where the time goes in v6:
time: 141 us; the launch traced here: 140 us
  waiting for transfers between devices  63.1 us (45%)
  Pallas kernels  37.9 us (27%)
  starting transfers between devices  33.5 us (24%)
  local copies, waits for them, and re-layouts  4.63 us (3%)
    ppermute x9, waiting for transfers between devices, cross_xy(): moved.append(lax.ppermute(bundles[mask], ('bx', 'by'), pairs))  42.4 us
    pallas_call x2, Pallas kernels, levels(): pl.pallas_call(partial(levels_kernel, chunk, by_z), in_specs=[in_smem, in...  24.8 us
    all_to_all x3, waiting for transfers between devices, deal_z(): lax.all_to_all(bundles[0], ('bx', 'by'), 0, 0, axis_index_groups=groups,...  16.3 us
    all_to_all x3, starting transfers between devices, deal_z(): lax.all_to_all(bundles[0], ('bx', 'by'), 0, 0, axis_index_groups=groups,...  14.4 us
    ppermute x9, starting transfers between devices, cross_xy(): moved.append(lax.ppermute(bundles[mask], ('bx', 'by'), pairs))  10.7 us
    all_to_all x1, starting transfers between devices, deal(): return lax.all_to_all(pieces, ('bx', 'by'), 0, 0, tiled=True)  8.31 us
    pallas_call x2, Pallas kernels, unpack(): pl.pallas_call(partial(unpack_kernel, by_z), grid=(4,), in_specs=in_specs...  5.68 us
    ppermute x2, waiting for transfers between devices, partner_2(): return lax.ppermute(value, axis, pairs)  4.33 us
  transfers between devices with their start and end apart: 15, of which 12 were waited for; matrix products, arithmetic and copies ran while one was open for 1% of the time, Pallas kernels for 24%

profile of v6, /device:TPU:0, one launch (start us, length us, event | category | flops | bytes accessed | tf_op | source)
XLA Modules:
  0.0 140.2 jit_solution(6621310472574666237)
XLA Ops:
  0.0 1.6 %copy-done.1 = f32[1,1,2,16,16,1024]{5,4,3,2,1,0:T(8,128)S(1)} copy-done((f32[1,1,2,16,16,1024]{5,4,3,2,1,0:T(8,128)S(1)}, f32[1,1,2,16,16,1024]{5,4,3,2,1,0:T(8,128)}, u32[]{:S(2)}) %copy-start.1) | copy-done | bytes 2097176
  1.6 1.1 pack.1
  2.8 1.0 copy-done.6
  3.7 8.3 %all-to-all-start.1 = ((f32[16,16,8,128]{3,2,1,0:T(8,128)}), f32[16,16,8,128]{3,2,1,0:T(8,128)S(1)}, u32[]{:S(2)}, u32[]{:S(2)}) async-start(f32[16,16,8,128]{3,2,1,0:T(8,128)} %copy-done.6), calls=%async_computation.1 | async-start | bytes 2097152 | tf_op jit(solution)/shard_map/all_to_all | solution.py:742
  12.1 1.7 %pack_masks.1 = (f32[4,16,8,128]{3,2,1,0:T(8,128)S(1)}, f32[4,16,8,128]{3,2,1,0:T(8,128)S(1)}, f32[4,16,8,128]{3,2,1,0:T(8,128)S(1)}, f32[4,16,8,128]{3,2,1,0:T(8,128)S(1)}) custom-call(s32[2]{0:T(128)S(1)} %pad_add_fusion.ids, f32[2,16,16,1024]{3,2,1,0:T(8,128)S(1)} %bitcast.31), custom_call_target="tpu_custom_call" | custom-call | flops 1000000 | bytes 2097152 | tf_op jit(solution)/shard_map/pack_masks/pallas_call | solution.py:348
  13.8 2.0 %collective-permute-start = (f32[4,16,8,128]{3,2,1,0:T(8,128)S(1)}, f32[4,16,8,128]{3,2,1,0:T(8,128)S(1)}, u32[]{:S(2)}, u32[]{:S(2)}) collective-permute-start(f32[4,16,8,128]{3,2,1,0:T(8,128)S(1)} %get-tuple-element.18), channel_id=1, source_target_pairs={{0,2},{2,0},{4,6},{6,4},{8,10},{10,8},{12,14},{14,12},{16,18},{18,... | collective-permute-start | bytes 786440 | tf_op jit(solution)/shard_map/ppermute | solution.py:393
  15.8 1.5 %collective-permute-start.1 = (f32[4,16,8,128]{3,2,1,0:T(8,128)S(1)}, f32[4,16,8,128]{3,2,1,0:T(8,128)S(1)}, u32[]{:S(2)}, u32[]{:S(2)}) collective-permute-start(f32[4,16,8,128]{3,2,1,0:T(8,128)S(1)} %get-tuple-element.19), channel_id=1, source_target_pairs={{0,4},{2,6},{4,0},{6,2},{8,12},{10,14},{12,8},{14,10},{16,20},{18,... | collective-permute-start | bytes 786440 | tf_op jit(solution)/shard_map/ppermute | solution.py:393
  17.4 12.6 %collective-permute-done.refs_1_ = f32[4,16,8,128]{3,2,1,0:T(8,128)S(1)} collective-permute-done((f32[4,16,8,128]{3,2,1,0:T(8,128)S(1)}, f32[4,16,8,128]{3,2,1,0:T(8,128)S(1)}, u32[]{:S(2)}, u32[]{:S(2)}) %collective-permute-start) | collective-permute-done | bytes 262176 | tf_op jit(solution)/shard_map/ppermute | solution.py:393
  29.9 8.0 %collective-permute-done.2.refs_3_ = f32[4,16,8,128]{3,2,1,0:T(8,128)S(1)} collective-permute-done((f32[4,16,8,128]{3,2,1,0:T(8,128)S(1)}, f32[4,16,8,128]{3,2,1,0:T(8,128)S(1)}, u32[]{:S(2)}, u32[]{:S(2)}) %collective-permute-start.2) | collective-permute-done | bytes 262176 | tf_op jit(solution)/shard_map/ppermute | solution.py:393
  37.9 1.0 regroup.3.refs_0_
  39.1 5.9 %all-to-all-start = ((f32[4,4,16,8,128]{4,3,2,1,0:T(8,128)}), f32[4,4,16,8,128]{4,3,2,1,0:T(8,128)}, u32[]{:S(2)}, u32[]{:S(2)}) async-start(f32[4,4,16,8,128]{4,3,2,1,0:T(8,128)} %regroup.3.refs_0_), calls=%async_computation | async-start | bytes 2097152 | tf_op jit(solution)/shard_map/all_to_all | solution.py:400
  45.0 1.4 copy-done.5
  47.9 1.4 %collective-permute-done.3.other = f32[8,2,16,8,128]{4,3,2,1,0:T(8,128)} collective-permute-done((f32[8,2,16,8,128]{4,3,2,1,0:T(8,128)S(1)}, f32[8,2,16,8,128]{4,3,2,1,0:T(8,128)}, u32[]{:S(2)}, u32[]{:S(2)}) %collective-permute-start.3) | collective-permute-done | bytes 1048608 | tf_op jit(solution)/shard_map/ppermute | solution.py:20
  49.4 12.8 %levels.2.refs_1_ = f32[4,4,16,8,128]{4,3,2,1,0:T(8,128)} custom-call(s32[2]{0:T(128)S(1)} %pad_add_fusion.ids, f32[496]{0:T(512)S(1)} %copy-done.12, f32[8,2,16,8,128]{4,3,2,1,0:T(8,128)S(1)} %join.2.own, f32[8,2,16,8,128]{4,3,2,1,0:T(8,128)} %collective-permute-done.3.other, f32[31,128]{1,0:T(8,128)S(1)} %tile.24.speeds, f32[8,128]{1,0:T(8,128)S(1)} %copy-done.11, ...), custom_call_target="tpu_custom_call" | custom-call | flops 100000000 | bytes 8388608 | tf_op jit(solution)/shard_map/levels/pallas_call | solution.py:625
  62.1 8.1 %all-to-all-done.refs_0_ = f32[4,4,16,8,128]{4,3,2,1,0:T(8,128)} async-done(((f32[4,4,16,8,128]{4,3,2,1,0:T(8,128)}), f32[4,4,16,8,128]{4,3,2,1,0:T(8,128)}, u32[]{:S(2)}, u32[]{:S(2)}) %all-to-all-start) | async-done | bytes 1048608 | tf_op jit(solution)/shard_map/all_to_all | solution.py:400
  70.3 3.5 %all-to-all-start.3 = ((f32[4,4,16,8,128]{4,3,2,1,0:T(8,128)}), f32[4,4,16,8,128]{4,3,2,1,0:T(8,128)S(1)}, u32[]{:S(2)}, u32[]{:S(2)}) async-start(f32[4,4,16,8,128]{4,3,2,1,0:T(8,128)} %levels.2.refs_1_), calls=%async_computation.3 | async-start | bytes 2097152 | tf_op jit(solution)/shard_map/all_to_all | solution.py:400
  73.8 2.3 %join.3.own = f32[8,2,16,8,128]{4,3,2,1,0:T(8,128)} custom-call(s32[2]{0:T(128)S(1)} %pad_add_fusion.ids, f32[4,4,16,8,128]{4,3,2,1,0:T(8,128)} %all-to-all-done.refs_0_, f32[4,4,16,8,128]{4,3,2,1,0:T(8,128)} %levels.2.refs_1_), custom_call_target="tpu_custom_call" | custom-call | flops 1000000 | bytes 2097152 | tf_op jit(solution)/shard_map/join/pallas_call | solution.py:447
  76.2 2.9 %collective-permute-done.4.other = f32[8,2,16,8,128]{4,3,2,1,0:T(8,128)} collective-permute-done((f32[8,2,16,8,128]{4,3,2,1,0:T(8,128)}, f32[8,2,16,8,128]{4,3,2,1,0:T(8,128)}, u32[]{:S(2)}, u32[]{:S(2)}) %collective-permute-start.4) | collective-permute-done | bytes 1048608 | tf_op jit(solution)/shard_map/ppermute | solution.py:20
  79.1 12.1 %levels.3 = (f32[4,16,8,128]{3,2,1,0:T(8,128)S(1)}, f32[4,16,8,128]{3,2,1,0:T(8,128)S(1)}, f32[4,16,8,128]{3,2,1,0:T(8,128)S(1)}, f32[4,16,8,128]{3,2,1,0:T(8,128)S(1)}) custom-call(s32[2]{0:T(128)S(1)} %pad_add_fusion.ids, f32[496]{0:T(512)S(1)} %copy-done.12, f32[8,2,16,8,128]{4,3,2,1,0:T(8,128)} %join.3.own, ...), custom_call_target="tpu_custom_call" | custom-call | flops 100000000 | bytes 8388608 | tf_op jit(solution)/shard_map/levels/pallas_call | solution.py:625
  92.7 2.1 %collective-permute-start.7 = (f32[4,16,8,128]{3,2,1,0:T(8,128)S(1)}, f32[4,16,8,128]{3,2,1,0:T(8,128)S(1)}, u32[]{:S(2)}, u32[]{:S(2)}) collective-permute-start(f32[4,16,8,128]{3,2,1,0:T(8,128)S(1)} %get-tuple-element.24), channel_id=1, source_target_pairs={{0,6},{2,4},{4,2},{6,0},{8,14},{10,12},{12,10},{14,8},{16,22},{18,... | collective-permute-start | bytes 786440 | tf_op jit(solution)/shard_map/ppermute | solution.py:393
  94.8 4.9 %collective-permute-done.5.refs_1_ = f32[4,16,8,128]{3,2,1,0:T(8,128)S(1)} collective-permute-done((f32[4,16,8,128]{3,2,1,0:T(8,128)S(1)}, f32[4,16,8,128]{3,2,1,0:T(8,128)S(1)}, u32[]{:S(2)}, u32[]{:S(2)}) %collective-permute-start.5) | collective-permute-done | bytes 262176 | tf_op jit(solution)/shard_map/ppermute | solution.py:393
  99.6 1.6 %collective-permute-done.6.refs_2_ = f32[4,16,8,128]{3,2,1,0:T(8,128)S(1)} collective-permute-done((f32[4,16,8,128]{3,2,1,0:T(8,128)S(1)}, f32[4,16,8,128]{3,2,1,0:T(8,128)S(1)}, u32[]{:S(2)}, u32[]{:S(2)}) %collective-permute-start.6) | collective-permute-done | bytes 262176 | tf_op jit(solution)/shard_map/ppermute | solution.py:393
  101.2 5.2 %collective-permute-done.7.refs_3_ = f32[4,16,8,128]{3,2,1,0:T(8,128)S(1)} collective-permute-done((f32[4,16,8,128]{3,2,1,0:T(8,128)S(1)}, f32[4,16,8,128]{3,2,1,0:T(8,128)S(1)}, u32[]{:S(2)}, u32[]{:S(2)}) %collective-permute-start.7) | collective-permute-done | bytes 262176 | tf_op jit(solution)/shard_map/ppermute | solution.py:393
  106.4 1.0 regroup.4.refs_1_
  107.5 5.0 %all-to-all-start.2 = ((f32[4,4,16,8,128]{4,3,2,1,0:T(8,128)}), f32[4,4,16,8,128]{4,3,2,1,0:T(8,128)S(1)}, u32[]{:S(2)}, u32[]{:S(2)}) async-start(f32[4,4,16,8,128]{4,3,2,1,0:T(8,128)} %regroup.4.refs_1_), calls=%async_computation.2 | async-start | bytes 2097152 | tf_op jit(solution)/shard_map/all_to_all | solution.py:400
  114.4 1.8 %collective-permute-start.10 = (f32[4,16,8,128]{3,2,1,0:T(8,128)S(1)}, f32[4,16,8,128]{3,2,1,0:T(8,128)S(1)}, u32[]{:S(2)}, u32[]{:S(2)}) collective-permute-start(f32[4,16,8,128]{3,2,1,0:T(8,128)S(1)} %get-tuple-element.28), channel_id=1, source_target_pairs={{0,6},{2,4},{4,2},{6,0},{8,14},{10,12},{12,10},{14,8},{16,22},{18,... | collective-permute-start | bytes 786440 | tf_op jit(solution)/shard_map/ppermute | solution.py:393
  116.1 4.8 %collective-permute-done.8.refs_1_ = f32[4,16,8,128]{3,2,1,0:T(8,128)S(1)} collective-permute-done((f32[4,16,8,128]{3,2,1,0:T(8,128)S(1)}, f32[4,16,8,128]{3,2,1,0:T(8,128)S(1)}, u32[]{:S(2)}, u32[]{:S(2)}) %collective-permute-start.8) | collective-permute-done | bytes 262176 | tf_op jit(solution)/shard_map/ppermute | solution.py:393
  121.0 1.7 %collective-permute-done.9.refs_2_ = f32[4,16,8,128]{3,2,1,0:T(8,128)S(1)} collective-permute-done((f32[4,16,8,128]{3,2,1,0:T(8,128)S(1)}, f32[4,16,8,128]{3,2,1,0:T(8,128)S(1)}, u32[]{:S(2)}, u32[]{:S(2)}) %collective-permute-start.9) | collective-permute-done | bytes 262176 | tf_op jit(solution)/shard_map/ppermute | solution.py:393
  122.7 3.7 %collective-permute-done.10.refs_3_ = f32[4,16,8,128]{3,2,1,0:T(8,128)S(1)} collective-permute-done((f32[4,16,8,128]{3,2,1,0:T(8,128)S(1)}, f32[4,16,8,128]{3,2,1,0:T(8,128)S(1)}, u32[]{:S(2)}, u32[]{:S(2)}) %collective-permute-start.10) | collective-permute-done | bytes 262176 | tf_op jit(solution)/shard_map/ppermute | solution.py:393
  126.4 2.8 %unpack.2.refs_1_ = f32[2,16,16,1024]{3,2,1,0:T(8,128)} custom-call(s32[2]{0:T(128)S(1)} %pad_add_fusion.ids, f32[4,16,8,128]{3,2,1,0:T(8,128)S(1)} %get-tuple-element.25.refs_0_, f32[4,16,8,128]{3,2,1,0:T(8,128)S(1)} %collective-permute-done.8.refs_1_, f32[4,16,8,128]{3,2,1,0:T(8,128)S(1)} %collective-permute-done.9.refs_2_, ...), custom_call_target="tpu_custom_call" | custom-call | flops 1000000 | bytes 2097152 | tf_op jit(solution)/shard_map/unpack/pallas_call | solution.py:676
  129.2 8.2 %all-to-all-done.2.refs_0_ = f32[4,4,16,8,128]{4,3,2,1,0:T(8,128)S(1)} async-done(((f32[4,4,16,8,128]{4,3,2,1,0:T(8,128)}), f32[4,4,16,8,128]{4,3,2,1,0:T(8,128)S(1)}, u32[]{:S(2)}, u32[]{:S(2)}) %all-to-all-start.2) | async-done | bytes 1048608 | tf_op jit(solution)/shard_map/all_to_all | solution.py:400
  137.4 2.8 %unpack.3 = f32[2,16,16,1024]{3,2,1,0:T(8,128)} custom-call(s32[2]{0:T(128)S(1)} %pad_add_fusion.ids, f32[4,4,16,8,128]{4,3,2,1,0:T(8,128)S(1)} %all-to-all-done.2.refs_0_, f32[2,16,16,1024]{3,2,1,0:T(8,128)} %unpack.2.refs_1_), custom_call_target="tpu_custom_call", output_to_operand_aliasing={{}: (2, {})} | custom-call | flops 1000000 | bytes 2097152 | tf_op jit(solution)/shard_map/unpack/pallas_call | solution.py:676
  (63 shorter events, 5.1 us)
Async XLA Ops:
  0.0 47.1 %copy-start = (f32[4,4]{1,0:T(4,128)S(1)}, f32[4,4]{1,0:T(4,128)}, u32[]{:S(2)}) copy-start(f32[4,4]{1,0:T(4,128)} %param.20) | copy-start | bytes 196
  0.0 1.6 %copy-start.1 = (f32[1,1,2,16,16,1024]{5,4,3,2,1,0:T(8,128)S(1)}, f32[1,1,2,16,16,1024]{5,4,3,2,1,0:T(8,128)}, u32[]{:S(2)}) copy-start(f32[1,1,2,16,16,1024]{5,4,3,2,1,0:T(8,128)} %param.19) | copy-start | bytes 6291460
  1.6 10.5 %copy-start.2 = (f32[1,1,2,16,16,1024]{5,4,3,2,1,0:T(8,128)S(1)}, f32[1,1,2,16,16,1024]{5,4,3,2,1,0:T(8,128)}, u32[]{:S(2)}) copy-start(f32[1,1,2,16,16,1024]{5,4,3,2,1,0:T(8,128)} %param.19) | copy-start | bytes 6291460
  2.8 1.0 copy-start.6
  3.7 35.2 %all-to-all-start.1 = ((f32[16,16,8,128]{3,2,1,0:T(8,128)}), f32[16,16,8,128]{3,2,1,0:T(8,128)S(1)}, u32[]{:S(2)}, u32[]{:S(2)}) async-start(f32[16,16,8,128]{3,2,1,0:T(8,128)} %copy-done.6), calls=%async_computation.1 | async-start | bytes 2097152 | tf_op jit(solution)/shard_map/all_to_all | solution.py:742
  13.8 16.1 %collective-permute-start = (f32[4,16,8,128]{3,2,1,0:T(8,128)S(1)}, f32[4,16,8,128]{3,2,1,0:T(8,128)S(1)}, u32[]{:S(2)}, u32[]{:S(2)}) collective-permute-start(f32[4,16,8,128]{3,2,1,0:T(8,128)S(1)} %get-tuple-element.18), channel_id=1, source_target_pairs={{0,2},{2,0},{4,6},{6,4},{8,10},{10,8},{12,14},{14,12},{16,18},{18,... | collective-permute-start | bytes 786440 | tf_op jit(solution)/shard_map/ppermute | solution.py:393
  15.8 14.1 %collective-permute-start.1 = (f32[4,16,8,128]{3,2,1,0:T(8,128)S(1)}, f32[4,16,8,128]{3,2,1,0:T(8,128)S(1)}, u32[]{:S(2)}, u32[]{:S(2)}) collective-permute-start(f32[4,16,8,128]{3,2,1,0:T(8,128)S(1)} %get-tuple-element.19), channel_id=1, source_target_pairs={{0,4},{2,6},{4,0},{6,2},{8,12},{10,14},{12,8},{14,10},{16,20},{18,... | collective-permute-start | bytes 786440 | tf_op jit(solution)/shard_map/ppermute | solution.py:393
  17.3 20.7 %collective-permute-start.2 = (f32[4,16,8,128]{3,2,1,0:T(8,128)S(1)}, f32[4,16,8,128]{3,2,1,0:T(8,128)S(1)}, u32[]{:S(2)}, u32[]{:S(2)}) collective-permute-start(f32[4,16,8,128]{3,2,1,0:T(8,128)S(1)} %get-tuple-element.20), channel_id=1, source_target_pairs={{0,6},{2,4},{4,2},{6,0},{8,14},{10,12},{12,10},{14,8},{16,22},{18,... | collective-permute-start | bytes 786440 | tf_op jit(solution)/shard_map/ppermute | solution.py:393
  39.0 6.0 %copy-start.4 = (f32[16,16,8,128]{3,2,1,0:T(8,128)}, f32[16,16,8,128]{3,2,1,0:T(8,128)S(1)}, u32[]{:S(2)}) copy-start(f32[16,16,8,128]{3,2,1,0:T(8,128)S(1)} %all-to-all-done.1.in_ref) | copy-start | bytes 3145732
  39.0 7.8 %copy-start.13 = (f32[31]{0:T(128)S(1)}, f32[31]{0:T(128)}, u32[]{:S(2)}) copy-start(f32[31]{0:T(128)} %constant.82) | copy-start | bytes 376
  39.0 7.8 %copy-start.14 = (f32[31]{0:T(128)S(1)}, f32[31]{0:T(128)}, u32[]{:S(2)}) copy-start(f32[31]{0:T(128)} %constant.71.clone) | copy-start | bytes 376
  39.0 10.3 %copy-start.7 = (bf16[256,256]{1,0:T(8,128)(2,1)S(1)}, bf16[256,256]{1,0:T(8,128)(2,1)}, u32[]{:S(2)}) copy-start(bf16[256,256]{1,0:T(8,128)(2,1)} %constant.78.clone.first_table) | copy-start | bytes 393220
  39.0 10.3 %copy-start.8 = (f32[2,4,8,128]{3,2,1,0:T(8,128)S(1)}, f32[2,4,8,128]{3,2,1,0:T(8,128)}, u32[]{:S(2)}) copy-start(f32[2,4,8,128]{3,2,1,0:T(8,128)} %constant.77.clone.last_lengths) | copy-start | bytes 98308
  39.0 10.3 %copy-start.9 = (f32[4,8,128]{2,1,0:T(8,128)S(1)}, f32[4,8,128]{2,1,0:T(8,128)}, u32[]{:S(2)}) copy-start(f32[4,8,128]{2,1,0:T(8,128)} %constant.76.clone.last_two) | copy-start | bytes 49156
  39.0 10.3 %copy-start.10 = (f32[2,8,128]{2,1,0:T(8,128)S(1)}, f32[2,8,128]{2,1,0:T(8,128)}, u32[]{:S(2)}) copy-start(f32[2,8,128]{2,1,0:T(8,128)} %constant.75.clone.last_one) | copy-start | bytes 24580
  39.0 10.3 %copy-start.11 = (f32[8,128]{1,0:T(8,128)S(1)}, f32[8,128]{1,0:T(8,128)}, u32[]{:S(2)}) copy-start(f32[8,128]{1,0:T(8,128)} %constant.73.clone.waves) | copy-start | bytes 12292
  39.1 10.3 %copy-start.12 = (f32[496]{0:T(512)S(1)}, f32[496]{0:T(512)}, u32[]{:S(2)}) copy-start(f32[496]{0:T(512)} %constant.72.clone.nodes) | copy-start | bytes 5956
  39.1 31.2 %all-to-all-start = ((f32[4,4,16,8,128]{4,3,2,1,0:T(8,128)}), f32[4,4,16,8,128]{4,3,2,1,0:T(8,128)}, u32[]{:S(2)}, u32[]{:S(2)}) async-start(f32[4,4,16,8,128]{4,3,2,1,0:T(8,128)} %regroup.3.refs_0_), calls=%async_computation | async-start | bytes 2097152 | tf_op jit(solution)/shard_map/all_to_all | solution.py:400
  45.0 4.4 %copy-start.3 = (f32[496,8,128]{2,1,0:T(8,128)S(1)}, f32[496,8,128]{2,1,0:T(8,128)}, u32[]{:S(2)}) copy-start(f32[496,8,128]{2,1,0:T(8,128)} %constant.74.clone.lengths) | copy-start | bytes 6094852
  45.0 1.4 copy-start.5
  46.5 2.9 %collective-permute-start.3 = (f32[8,2,16,8,128]{4,3,2,1,0:T(8,128)S(1)}, f32[8,2,16,8,128]{4,3,2,1,0:T(8,128)}, u32[]{:S(2)}, u32[]{:S(2)}) collective-permute-start(f32[8,2,16,8,128]{4,3,2,1,0:T(8,128)S(1)} %join.2.own), channel_id=1, source_target_pairs={{0,1},{1,0},{2,3},{3,2},{4,5},{5,4},{6,7},{7,6},{8,9},{9,8},{10,11... | collective-permute-start | bytes 3145736 | tf_op jit(solution)/shard_map/ppermute | solution.py:20
  70.3 37.2 %all-to-all-start.3 = ((f32[4,4,16,8,128]{4,3,2,1,0:T(8,128)}), f32[4,4,16,8,128]{4,3,2,1,0:T(8,128)S(1)}, u32[]{:S(2)}, u32[]{:S(2)}) async-start(f32[4,4,16,8,128]{4,3,2,1,0:T(8,128)} %levels.2.refs_1_), calls=%async_computation.3 | async-start | bytes 2097152 | tf_op jit(solution)/shard_map/all_to_all | solution.py:400
  76.1 3.0 %collective-permute-start.4 = (f32[8,2,16,8,128]{4,3,2,1,0:T(8,128)}, f32[8,2,16,8,128]{4,3,2,1,0:T(8,128)}, u32[]{:S(2)}, u32[]{:S(2)}) collective-permute-start(f32[8,2,16,8,128]{4,3,2,1,0:T(8,128)} %join.3.own), channel_id=1, source_target_pairs={{0,1},{1,0},{2,3},{3,2},{4,5},{5,4},{6,7},{7,6},{8,9},{9,8},{10,11... | collective-permute-start | bytes 3145736 | tf_op jit(solution)/shard_map/ppermute | solution.py:20
  91.2 8.4 %collective-permute-start.5 = (f32[4,16,8,128]{3,2,1,0:T(8,128)S(1)}, f32[4,16,8,128]{3,2,1,0:T(8,128)S(1)}, u32[]{:S(2)}, u32[]{:S(2)}) collective-permute-start(f32[4,16,8,128]{3,2,1,0:T(8,128)S(1)} %get-tuple-element.22), channel_id=1, source_target_pairs={{0,2},{2,0},{4,6},{6,4},{8,10},{10,8},{12,14},{14,12},{16,18},{18,... | collective-permute-start | bytes 786440 | tf_op jit(solution)/shard_map/ppermute | solution.py:393
  92.0 9.2 %collective-permute-start.6 = (f32[4,16,8,128]{3,2,1,0:T(8,128)S(1)}, f32[4,16,8,128]{3,2,1,0:T(8,128)S(1)}, u32[]{:S(2)}, u32[]{:S(2)}) collective-permute-start(f32[4,16,8,128]{3,2,1,0:T(8,128)S(1)} %get-tuple-element.23), channel_id=1, source_target_pairs={{0,4},{2,6},{4,0},{6,2},{8,12},{10,14},{12,8},{14,10},{16,20},{18,... | collective-permute-start | bytes 786440 | tf_op jit(solution)/shard_map/ppermute | solution.py:393
  92.7 13.7 %collective-permute-start.7 = (f32[4,16,8,128]{3,2,1,0:T(8,128)S(1)}, f32[4,16,8,128]{3,2,1,0:T(8,128)S(1)}, u32[]{:S(2)}, u32[]{:S(2)}) collective-permute-start(f32[4,16,8,128]{3,2,1,0:T(8,128)S(1)} %get-tuple-element.24), channel_id=1, source_target_pairs={{0,6},{2,4},{4,2},{6,0},{8,14},{10,12},{12,10},{14,8},{16,22},{18,... | collective-permute-start | bytes 786440 | tf_op jit(solution)/shard_map/ppermute | solution.py:393
  107.5 29.9 %all-to-all-start.2 = ((f32[4,4,16,8,128]{4,3,2,1,0:T(8,128)}), f32[4,4,16,8,128]{4,3,2,1,0:T(8,128)S(1)}, u32[]{:S(2)}, u32[]{:S(2)}) async-start(f32[4,4,16,8,128]{4,3,2,1,0:T(8,128)} %regroup.4.refs_1_), calls=%async_computation.2 | async-start | bytes 2097152 | tf_op jit(solution)/shard_map/all_to_all | solution.py:400
  112.6 8.4 %collective-permute-start.8 = (f32[4,16,8,128]{3,2,1,0:T(8,128)S(1)}, f32[4,16,8,128]{3,2,1,0:T(8,128)S(1)}, u32[]{:S(2)}, u32[]{:S(2)}) collective-permute-start(f32[4,16,8,128]{3,2,1,0:T(8,128)S(1)} %get-tuple-element.26), channel_id=1, source_target_pairs={{0,2},{2,0},{4,6},{6,4},{8,10},{10,8},{12,14},{14,12},{16,18},{18,... | collective-permute-start | bytes 786440 | tf_op jit(solution)/shard_map/ppermute | solution.py:393
  113.5 9.2 %collective-permute-start.9 = (f32[4,16,8,128]{3,2,1,0:T(8,128)S(1)}, f32[4,16,8,128]{3,2,1,0:T(8,128)S(1)}, u32[]{:S(2)}, u32[]{:S(2)}) collective-permute-start(f32[4,16,8,128]{3,2,1,0:T(8,128)S(1)} %get-tuple-element.27), channel_id=1, source_target_pairs={{0,4},{2,6},{4,0},{6,2},{8,12},{10,14},{12,8},{14,10},{16,20},{18,... | collective-permute-start | bytes 786440 | tf_op jit(solution)/shard_map/ppermute | solution.py:393
  114.4 12.0 %collective-permute-start.10 = (f32[4,16,8,128]{3,2,1,0:T(8,128)S(1)}, f32[4,16,8,128]{3,2,1,0:T(8,128)S(1)}, u32[]{:S(2)}, u32[]{:S(2)}) collective-permute-start(f32[4,16,8,128]{3,2,1,0:T(8,128)S(1)} %get-tuple-element.28), channel_id=1, source_target_pairs={{0,6},{2,4},{4,2},{6,0},{8,14},{10,12},{12,10},{14,8},{16,22},{18,... | collective-permute-start | bytes 786440 | tf_op jit(solution)/shard_map/ppermute | solution.py:393

commit v7 on v5

--- a/solution.py
+++ b/solution.py
@@ -298,87 +298,40 @@
             tiles[j, t1] = tile
 
 
-def pack_kernel(in_ref, out_ref):
-    def step(group, carry):
-        lanes = pl.ds(pl.multiple_of(group * 128, 128), 128)
-        pack_rows(in_ref, lanes, out_ref.at[pl.ds(4 * group, 4)])
-        return carry
-
-    lax.fori_loop(0, 4, step, 0)
+def pack_kernel(chunk, in_ref, out_ref, held, arrived):
+    group = pl.program_id(0)
+
+    def fetch(place):
+        lanes = pl.ds((4 * chunk + place) * 128, 128)
+        return pltpu.make_async_copy(
+            in_ref.at[:, :, :, lanes], held.at[place], arrived.at[place]
+        )
+
+    @pl.when(group == 0)
+    def _():
+        for place in range(4):
+            fetch(place).start()
+
+    for place in range(4):
+
+        @pl.when(group == place)
+        def _(place=place):
+            fetch(place).wait()
+
+    pack_rows(held.at[group], slice(None), out_ref)
 
 
 def pack(weights, chunk):
     return pl.pallas_call(
-        pack_kernel,
-        grid=(1,),
-        in_specs=[pl.BlockSpec((2, 16, 16, 512), lambda i: (0, 0, 0, chunk))],
-        out_specs=pl.BlockSpec((PIECES, 16, 8, 128), lambda i: (0, 0, 0, 0)),
+        partial(pack_kernel, chunk),
+        grid=(4,),
+        in_specs=[pl.BlockSpec(memory_space=pl.ANY)],
+        out_specs=pl.BlockSpec((4, 16, 8, 128), lambda i: (i, 0, 0, 0)),
         out_shape=jax.ShapeDtypeStruct((PIECES, 16, 8, 128), jnp.float32),
-        compiler_params=pltpu.CompilerParams(vmem_limit_bytes=VMEM_LIMIT),
+        scratch_shapes=[pltpu.VMEM((4, 2, 16, 16, 128), jnp.float32), pltpu.SemaphoreType.DMA((4,))],
         cost_estimate=pl.CostEstimate(flops=10**6, bytes_accessed=2**21, transcendentals=0),
         name="pack",
     )(weights)
-
-
-def pack_masks_kernel(ids, in_ref, *refs):
-    outs, tiles = refs[:4], refs[4]
-    me = ids[0]
-
-    def step(mz, carry):
-        group = mz ^ (me // 4)
-        pack_rows(in_ref, pl.ds(pl.multiple_of(group * 128, 128), 128), tiles)
-        for mxy in range(4):
-            outs[mxy][mz] = tiles[mxy ^ (me % 4)]
-        return carry
-
-    lax.fori_loop(0, 4, step, 0)
-
-
-BUNDLE = (4, 16, 8, 128)
-
-
-def pack_masks(weights, ids, chunk):
-    return pl.pallas_call(
-        pack_masks_kernel,
-        grid=(1,),
-        in_specs=[
-            pl.BlockSpec(memory_space=pltpu.SMEM),
-            pl.BlockSpec((2, 16, 16, 512), lambda i: (0, 0, 0, chunk)),
-        ],
-        out_specs=[pl.BlockSpec(BUNDLE, lambda i: (0, 0, 0, 0))] * 4,
-        out_shape=[jax.ShapeDtypeStruct(BUNDLE, jnp.float32)] * 4,
-        scratch_shapes=[pltpu.VMEM(BUNDLE, jnp.float32)],
-        compiler_params=pltpu.CompilerParams(vmem_limit_bytes=VMEM_LIMIT),
-        cost_estimate=pl.CostEstimate(flops=10**6, bytes_accessed=2**21, transcendentals=0),
-        name="pack_masks",
-    )(ids, weights)
-
-
-def regroup_kernel(*refs):
-    for first in range(4):
-        for second in range(4):
-            refs[4 + second][first] = refs[first][second]
-
-
-def regroup(bundles):
-    in_vmem = pl.BlockSpec(memory_space=pltpu.VMEM)
-    return pl.pallas_call(
-        regroup_kernel,
-        in_specs=[in_vmem] * 4,
-        out_specs=[in_vmem] * 4,
-        out_shape=[jax.ShapeDtypeStruct(BUNDLE, jnp.float32)] * 4,
-        compiler_params=pltpu.CompilerParams(vmem_limit_bytes=VMEM_LIMIT),
-        cost_estimate=pl.CostEstimate(flops=10**5, bytes_accessed=2**21, transcendentals=0),
-        name="regroup",
-    )(*bundles)
-
-
-def exchange(bundles, unit):
-    moved = [bundles[0]]
-    for mask in range(1, 4):
-        pairs = [(source, source ^ (mask * unit)) for source in range(PIECES)]
-        moved.append(lax.ppermute(bundles[mask], ("bx", "by"), pairs))
-    return moved
 
 
 def merge_halves(out_ref, box, t1, low, high):
@@ -398,37 +351,17 @@
     lax.fori_loop(0, 8, step, 0)
 
 
-def join_masks_kernel(ids, *refs):
-    bundles, out_ref = refs[:4], refs[-1]
-    me = ids[0]
-    is_low = jnp.broadcast_to(me % 2, (8, 128)) == 0
-    for mz in range(4):
-        for mx in range(2):
-            box = (2 * mz + mx) ^ (me // 2)
-            for t1 in range(16):
-                mine = bundles[mz][2 * mx, t1]
-                partner = bundles[mz][2 * mx + 1, t1]
-                low = jnp.where(is_low, mine, partner)
-                high = jnp.where(is_low, partner, mine)
-                merge_halves(out_ref, box, t1, low, high)
-
-
-def join(received, ids=None, after=()):
+def join(received):
     in_vmem = pl.BlockSpec(memory_space=pltpu.VMEM)
-    if ids is None:
-        kernel, operands, in_specs = join_kernel, [received], [in_vmem]
-    else:
-        kernel, operands = join_masks_kernel, [ids, *received]
-        in_specs = [pl.BlockSpec(memory_space=pltpu.SMEM)] + [in_vmem] * 4
     return pl.pallas_call(
-        kernel,
-        in_specs=in_specs + [pl.BlockSpec(memory_space=pl.ANY)] * len(after),
+        join_kernel,
+        in_specs=[in_vmem],
         out_specs=in_vmem,
         out_shape=jax.ShapeDtypeStruct((8, 2, 16, 8, 128), jnp.float32),
         compiler_params=pltpu.CompilerParams(vmem_limit_bytes=VMEM_LIMIT),
-        cost_estimate=pl.CostEstimate(flops=1000, bytes_accessed=1000, transcendentals=0),
+        cost_estimate=pl.CostEstimate(flops=10**6, bytes_accessed=2**21, transcendentals=0),
         name="join",
-    )(*operands, *after)
+    )(received)
 
 
 def levels_kernel(
@@ -612,9 +545,7 @@
             pltpu.VMEM((2, 4, 8, 128), jnp.float32),
         ],
         compiler_params=pltpu.CompilerParams(vmem_limit_bytes=VMEM_LIMIT),
-        cost_estimate=pl.CostEstimate(
-            flops=1000, bytes_accessed=4 * 10**8 if chunk else 1000, transcendentals=0
-        ),
+        cost_estimate=pl.CostEstimate(flops=10**8, bytes_accessed=2**23, transcendentals=0),
         name="levels",
     )(ids, jnp.asarray(nodes), own, other, speeds, *[jnp.asarray(table) for table in tables])
 
@@ -652,7 +583,6 @@
         out_shape=jax.ShapeDtypeStruct((2, 16, 16, 1024), jnp.float32),
         scratch_shapes=[pltpu.VMEM((4, 128, 128), jnp.float32)],
         input_output_aliases=aliases,
-        compiler_params=pltpu.CompilerParams(vmem_limit_bytes=VMEM_LIMIT),
         cost_estimate=pl.CostEstimate(flops=10**6, bytes_accessed=2**21, transcendentals=0),
         name="unpack",
     )(*operands)
@@ -690,19 +620,15 @@
     ids = jnp.stack([me, core]).astype(jnp.int32)
     speeds = speed_tables(speed_modes, core)
 
-    first = deal(pack(local, 0))
-    near = exchange(pack_masks(local, ids, 1), 1)
-    second = exchange(regroup(near), 4)
-
-    own = join(first)
-    first = levels(0, ids, own, partner_2(own, "cores", 0), speeds[0])
-    back_first = deal(first)
-
-    own = join(second, ids, [first])
-    back_second = deal(levels(1, ids, own, partner_2(own, "cores", 0), speeds[1]))
-
-    out = unpack(back_first, 0, None)
-    out = unpack(back_second, 1, out)
+    received = [deal(pack(local, chunk)) for chunk in range(CHUNKS)]
+    results = []
+    for chunk in range(CHUNKS):
+        own = join(received[chunk])
+        other = partner_2(own, "cores", 0)
+        results.append(deal(levels(chunk, ids, own, other, speeds[chunk])))
+    out = None
+    for chunk in range(CHUNKS):
+        out = unpack(results[chunk], chunk, out)
     return out.reshape(weights.shape)
 
 

time: 165 us -> 128 us (0.78)
  waiting for transfers between devices: 94.9 us -> 62.1 us
  starting transfers between devices: 27.9 us -> 20.6 us
  Pallas kernels: 34.8 us -> 40.1 us
    ppermute x6 -> x0, waiting for transfers between devices: 40.9 us -> none  [exchange(): moved.append(lax.ppermute(bundles[mask], ('bx', 'by'), pairs))]
    ppermute x6 -> x0, starting transfers between devices: 9.83 us -> none  [exchange(): moved.append(lax.ppermute(bundles[mask], ('bx', 'by'), pairs))]
    all_to_all x3 -> x4, waiting for transfers between devices: 49.6 us -> 58.1 us  [deal(): return lax.all_to_all(pieces, ('bx', 'by'), 0, 0, tiled=True)]
    pallas_call x2, Pallas kernels: 4.51 us -> 7.75 us  [unpack(): pl.pallas_call(unpack_kernel, grid=(4,), in_specs=in_specs, out_specs=pl....]
    all_to_all x3 -> x4, starting transfers between devices: 18 us -> 20.4 us  [deal(): return lax.all_to_all(pieces, ('bx', 'by'), 0, 0, tiled=True)]
    pallas_call x5 -> x4, Pallas kernels: 5.58 us -> 7.84 us  [the longest x2 6.42 us: pack(): pl.pallas_call(partial(pack_kernel, chunk), grid=(4,), in_specs=[pl.Block...]
    unnamed x32 -> x28, local copies, waits for them, and re-layouts: 4.82 us -> 3.25 us
  transfers between devices with their start and end apart: 11 -> 6, of which waited for: 10 -> 6; matrix products, arithmetic and copies ran while one was open for 1% -> 1% of each run, Pallas kernels for 11% -> 26%
where the time goes in v7:
time: 128 us
  waiting for transfers between devices  62.1 us (49%)
  Pallas kernels  40.1 us (31%)
  starting transfers between devices  20.6 us (16%)
  local copies, waits for them, and re-layouts  3.89 us (3%)
    all_to_all x4, waiting for transfers between devices, deal(): return lax.all_to_all(pieces, ('bx', 'by'), 0, 0, tiled=True)  58.1 us
    pallas_call x2, Pallas kernels, levels(): pl.pallas_call(partial(levels_kernel, chunk), in_specs=[in_smem, in_smem]...  24.5 us
    all_to_all x4, starting transfers between devices, deal(): return lax.all_to_all(pieces, ('bx', 'by'), 0, 0, tiled=True)  20.4 us
    pallas_call x2, Pallas kernels, unpack(): pl.pallas_call(unpack_kernel, grid=(4,), in_specs=in_specs, out_specs=pl....  7.75 us
    pallas_call x2, Pallas kernels, pack(): pl.pallas_call(partial(pack_kernel, chunk), grid=(4,), in_specs=[pl.Block...  6.42 us
    ppermute x2, waiting for transfers between devices, partner_2(): return lax.ppermute(value, axis, pairs)  4.06 us
    unnamed x28, local copies, waits for them, and re-layouts  3.25 us
  transfers between devices with their start and end apart: 6, of which 6 were waited for; matrix products, arithmetic and copies ran while one was open for 1% of the time, Pallas kernels for 26%

profile of v7, /device:TPU:10, one launch (start us, length us, event | category | flops | bytes accessed | tf_op | source)
XLA Modules:
  0.0 127.8 jit_solution(3569069047502610133)
XLA Ops:
  0.0 3.2 %pack.3 = f32[16,16,8,128]{3,2,1,0:T(8,128)} custom-call(f32[2,16,16,1024]{3,2,1,0:T(8,128)} %bitcast.30), custom_call_target="tpu_custom_call" | custom-call | flops 1000000 | bytes 2097152 | tf_op jit(solution)/shard_map/pack/pallas_call | solution.py:325
  3.2 7.2 %all-to-all-start.2 = ((f32[16,16,8,128]{3,2,1,0:T(8,128)}), f32[16,16,8,128]{3,2,1,0:T(8,128)S(1)}, u32[]{:S(2)}, u32[]{:S(2)}) async-start(f32[16,16,8,128]{3,2,1,0:T(8,128)} %pack.3), calls=%async_computation.2 | async-start | bytes 2097152 | tf_op jit(solution)/shard_map/all_to_all | solution.py:636
  10.5 3.2 %pack.2 = f32[16,16,8,128]{3,2,1,0:T(8,128)} custom-call(f32[2,16,16,1024]{3,2,1,0:T(8,128)} %bitcast.31), custom_call_target="tpu_custom_call" | custom-call | flops 1000000 | bytes 2097152 | tf_op jit(solution)/shard_map/pack/pallas_call | solution.py:325
  13.8 22.6 %all-to-all-done.2.in_ref = f32[16,16,8,128]{3,2,1,0:T(8,128)S(1)} async-done(((f32[16,16,8,128]{3,2,1,0:T(8,128)}), f32[16,16,8,128]{3,2,1,0:T(8,128)S(1)}, u32[]{:S(2)}, u32[]{:S(2)}) %all-to-all-start.2) | async-done | bytes 1048608 | tf_op jit(solution)/shard_map/all_to_all | solution.py:636
  36.3 4.4 %all-to-all-start = ((f32[16,16,8,128]{3,2,1,0:T(8,128)}), f32[16,16,8,128]{3,2,1,0:T(8,128)}, u32[]{:S(2)}, u32[]{:S(2)}) async-start(f32[16,16,8,128]{3,2,1,0:T(8,128)} %pack.2), calls=%async_computation | async-start | bytes 2097152 | tf_op jit(solution)/shard_map/all_to_all | solution.py:636
  40.8 1.2 copy-done.4
  42.0 0.1 join.3.own
  42.1 0.1 collective-permute-start.1
  42.2 0.1 stack.94
  42.4 0.1 mul.130
  42.4 0.1 add_multiply_fusion
  42.5 0.1 broadcast_in_dim.8
  42.6 0.1 mul.141
  42.7 0.6 fusion.1
  43.3 0.1 add.152
  43.4 0.1 tile.26.speeds
  43.5 0.1 pad_add_fusion.ids
  43.6 1.4 %collective-permute-done.1.other = f32[8,2,16,8,128]{4,3,2,1,0:T(8,128)} collective-permute-done((f32[8,2,16,8,128]{4,3,2,1,0:T(8,128)S(1)}, f32[8,2,16,8,128]{4,3,2,1,0:T(8,128)}, u32[]{:S(2)}, u32[]{:S(2)}) %collective-permute-start.1) | collective-permute-done | bytes 1048608 | tf_op jit(solution)/shard_map/ppermute | solution.py:20
  45.0 11.7 %levels.3 = f32[16,16,8,128]{3,2,1,0:T(8,128)S(1)} custom-call(s32[2]{0:T(128)S(1)} %pad_add_fusion.ids, f32[496]{0:T(512)S(1)} %copy-done.10, f32[8,2,16,8,128]{4,3,2,1,0:T(8,128)S(1)} %join.3.own, f32[8,2,16,8,128]{4,3,2,1,0:T(8,128)} %collective-permute-done.1.other, f32[31,128]{1,0:T(8,128)S(1)} %tile.26.speeds, f32[8,128]{1,0:T(8,128)S(1)} %copy-done.9, ...), custom_call_target="tpu_custom_call" | custom-call | flops 100000000 | bytes 8388608 | tf_op jit(solution)/shard_map/levels/pallas_call | solution.py:534
  56.8 1.0 copy-done.2
  57.8 7.5 %all-to-all-done.in_ref = f32[16,16,8,128]{3,2,1,0:T(8,128)} async-done(((f32[16,16,8,128]{3,2,1,0:T(8,128)}), f32[16,16,8,128]{3,2,1,0:T(8,128)}, u32[]{:S(2)}, u32[]{:S(2)}) %all-to-all-start) | async-done | bytes 1048608 | tf_op jit(solution)/shard_map/all_to_all | solution.py:636
  65.2 4.4 %all-to-all-start.3 = ((f32[16,16,8,128]{3,2,1,0:T(8,128)}), f32[16,16,8,128]{3,2,1,0:T(8,128)}, u32[]{:S(2)}, u32[]{:S(2)}) async-start(f32[16,16,8,128]{3,2,1,0:T(8,128)} %copy-done.2), calls=%async_computation.3 | async-start | bytes 2097152 | tf_op jit(solution)/shard_map/all_to_all | solution.py:636
  69.7 1.3 %join.2.own = f32[8,2,16,8,128]{4,3,2,1,0:T(8,128)S(1)} custom-call(f32[16,16,8,128]{3,2,1,0:T(8,128)} %all-to-all-done.in_ref), custom_call_target="tpu_custom_call" | custom-call | flops 1000000 | bytes 2097152 | tf_op jit(solution)/shard_map/join/pallas_call | solution.py:356
  71.1 0.1 tile.24.speeds
  71.2 2.7 %collective-permute-done.other = f32[8,2,16,8,128]{4,3,2,1,0:T(8,128)} collective-permute-done((f32[8,2,16,8,128]{4,3,2,1,0:T(8,128)S(1)}, f32[8,2,16,8,128]{4,3,2,1,0:T(8,128)}, u32[]{:S(2)}, u32[]{:S(2)}) %collective-permute-start) | collective-permute-done | bytes 1048608 | tf_op jit(solution)/shard_map/ppermute | solution.py:20
  73.8 12.7 %levels.2 = f32[16,16,8,128]{3,2,1,0:T(8,128)} custom-call(s32[2]{0:T(128)S(1)} %pad_add_fusion.ids, f32[496]{0:T(512)S(1)} %copy-done.10, f32[8,2,16,8,128]{4,3,2,1,0:T(8,128)S(1)} %join.2.own, f32[8,2,16,8,128]{4,3,2,1,0:T(8,128)} %collective-permute-done.other, f32[31,128]{1,0:T(8,128)S(1)} %tile.24.speeds, f32[8,128]{1,0:T(8,128)S(1)} %copy-done.9, ...), custom_call_target="tpu_custom_call" | custom-call | flops 100000000 | bytes 8388608 | tf_op jit(solution)/shard_map/levels/pallas_call | solution.py:534
  86.6 7.6 %all-to-all-done.3.refs_0_ = f32[16,16,8,128]{3,2,1,0:T(8,128)} async-done(((f32[16,16,8,128]{3,2,1,0:T(8,128)}), f32[16,16,8,128]{3,2,1,0:T(8,128)}, u32[]{:S(2)}, u32[]{:S(2)}) %all-to-all-start.3) | async-done | bytes 1048608 | tf_op jit(solution)/shard_map/all_to_all | solution.py:636
  94.1 4.4 %all-to-all-start.1 = ((f32[16,16,8,128]{3,2,1,0:T(8,128)}), f32[16,16,8,128]{3,2,1,0:T(8,128)S(1)}, u32[]{:S(2)}, u32[]{:S(2)}) async-start(f32[16,16,8,128]{3,2,1,0:T(8,128)} %levels.2), calls=%async_computation.1 | async-start | bytes 2097152 | tf_op jit(solution)/shard_map/all_to_all | solution.py:636
  98.6 3.9 %unpack.2.refs_1_ = f32[2,16,16,1024]{3,2,1,0:T(8,128)} custom-call(f32[16,16,8,128]{3,2,1,0:T(8,128)} %all-to-all-done.3.refs_0_), custom_call_target="tpu_custom_call" | custom-call | flops 1000000 | bytes 2097152 | tf_op jit(solution)/shard_map/unpack/pallas_call | solution.py:578
  102.4 20.5 %all-to-all-done.1.refs_0_ = f32[16,16,8,128]{3,2,1,0:T(8,128)S(1)} async-done(((f32[16,16,8,128]{3,2,1,0:T(8,128)}), f32[16,16,8,128]{3,2,1,0:T(8,128)S(1)}, u32[]{:S(2)}, u32[]{:S(2)}) %all-to-all-start.1) | async-done | bytes 1048608 | tf_op jit(solution)/shard_map/all_to_all | solution.py:636
  122.9 1.0 copy-done.11
  123.9 3.9 %unpack.3 = f32[2,16,16,1024]{3,2,1,0:T(8,128)} custom-call(f32[16,16,8,128]{3,2,1,0:T(8,128)} %copy-done.11, f32[2,16,16,1024]{3,2,1,0:T(8,128)} %unpack.2.refs_1_), custom_call_target="tpu_custom_call", output_to_operand_aliasing={{}: (1, {})} | custom-call | flops 1000000 | bytes 2097152 | tf_op jit(solution)/shard_map/unpack/pallas_call | solution.py:578
  (40 shorter events, 0.2 us)
Async XLA Ops:
  0.0 42.7 %copy-start = (f32[4,4]{1,0:T(4,128)S(1)}, f32[4,4]{1,0:T(4,128)}, u32[]{:S(2)}) copy-start(f32[4,4]{1,0:T(4,128)} %param.20) | copy-start | bytes 196
  3.2 33.1 %all-to-all-start.2 = ((f32[16,16,8,128]{3,2,1,0:T(8,128)}), f32[16,16,8,128]{3,2,1,0:T(8,128)S(1)}, u32[]{:S(2)}, u32[]{:S(2)}) async-start(f32[16,16,8,128]{3,2,1,0:T(8,128)} %pack.3), calls=%async_computation.2 | async-start | bytes 2097152 | tf_op jit(solution)/shard_map/all_to_all | solution.py:636
  10.4 34.5 %copy-start.6 = (f32[2,4,8,128]{3,2,1,0:T(8,128)S(1)}, f32[2,4,8,128]{3,2,1,0:T(8,128)}, u32[]{:S(2)}) copy-start(f32[2,4,8,128]{3,2,1,0:T(8,128)} %constant.77.clone.last_lengths) | copy-start | bytes 98308
  10.4 34.5 %copy-start.7 = (f32[4,8,128]{2,1,0:T(8,128)S(1)}, f32[4,8,128]{2,1,0:T(8,128)}, u32[]{:S(2)}) copy-start(f32[4,8,128]{2,1,0:T(8,128)} %constant.76.clone.last_two) | copy-start | bytes 49156
  10.4 34.5 %copy-start.10 = (f32[496]{0:T(512)S(1)}, f32[496]{0:T(512)}, u32[]{:S(2)}) copy-start(f32[496]{0:T(512)} %constant.72.clone.nodes) | copy-start | bytes 5956
  13.7 28.7 %copy-start.12 = (f32[31]{0:T(128)S(1)}, f32[31]{0:T(128)}, u32[]{:S(2)}) copy-start(f32[31]{0:T(128)} %constant.82) | copy-start | bytes 376
  13.7 28.7 %copy-start.13 = (f32[31]{0:T(128)S(1)}, f32[31]{0:T(128)}, u32[]{:S(2)}) copy-start(f32[31]{0:T(128)} %constant.71.clone) | copy-start | bytes 376
  13.7 31.3 %copy-start.1 = (f32[496,8,128]{2,1,0:T(8,128)S(1)}, f32[496,8,128]{2,1,0:T(8,128)}, u32[]{:S(2)}) copy-start(f32[496,8,128]{2,1,0:T(8,128)} %constant.74.clone.lengths) | copy-start | bytes 6094852
  13.7 31.3 %copy-start.5 = (bf16[256,256]{1,0:T(8,128)(2,1)S(1)}, bf16[256,256]{1,0:T(8,128)(2,1)}, u32[]{:S(2)}) copy-start(bf16[256,256]{1,0:T(8,128)(2,1)} %constant.78.clone.first_table) | copy-start | bytes 393220
  13.7 31.3 %copy-start.8 = (f32[2,8,128]{2,1,0:T(8,128)S(1)}, f32[2,8,128]{2,1,0:T(8,128)}, u32[]{:S(2)}) copy-start(f32[2,8,128]{2,1,0:T(8,128)} %constant.75.clone.last_one) | copy-start | bytes 24580
  13.7 31.3 %copy-start.9 = (f32[8,128]{1,0:T(8,128)S(1)}, f32[8,128]{1,0:T(8,128)}, u32[]{:S(2)}) copy-start(f32[8,128]{1,0:T(8,128)} %constant.73.clone.waves) | copy-start | bytes 12292
  36.3 4.4 %copy-start.3 = (f32[16,16,8,128]{3,2,1,0:T(8,128)}, f32[16,16,8,128]{3,2,1,0:T(8,128)S(1)}, u32[]{:S(2)}) copy-start(f32[16,16,8,128]{3,2,1,0:T(8,128)S(1)} %all-to-all-done.2.in_ref) | copy-start | bytes 3145732
  36.3 28.9 %all-to-all-start = ((f32[16,16,8,128]{3,2,1,0:T(8,128)}), f32[16,16,8,128]{3,2,1,0:T(8,128)}, u32[]{:S(2)}, u32[]{:S(2)}) async-start(f32[16,16,8,128]{3,2,1,0:T(8,128)} %pack.2), calls=%async_computation | async-start | bytes 2097152 | tf_op jit(solution)/shard_map/all_to_all | solution.py:636
  40.8 1.2 copy-start.4
  42.1 2.9 %collective-permute-start.1 = (f32[8,2,16,8,128]{4,3,2,1,0:T(8,128)S(1)}, f32[8,2,16,8,128]{4,3,2,1,0:T(8,128)}, u32[]{:S(2)}, u32[]{:S(2)}) collective-permute-start(f32[8,2,16,8,128]{4,3,2,1,0:T(8,128)S(1)} %join.3.own), channel_id=1, source_target_pairs={{0,1},{1,0},{2,3},{3,2},{4,5},{5,4},{6,7},{7,6},{8,9},{9,8},{10,11... | collective-permute-start | bytes 3145736 | tf_op jit(solution)/shard_map/ppermute | solution.py:20
  56.8 1.0 copy-start.2
  65.2 28.9 %all-to-all-start.3 = ((f32[16,16,8,128]{3,2,1,0:T(8,128)}), f32[16,16,8,128]{3,2,1,0:T(8,128)}, u32[]{:S(2)}, u32[]{:S(2)}) async-start(f32[16,16,8,128]{3,2,1,0:T(8,128)} %copy-done.2), calls=%async_computation.3 | async-start | bytes 2097152 | tf_op jit(solution)/shard_map/all_to_all | solution.py:636
  71.0 2.9 %collective-permute-start = (f32[8,2,16,8,128]{4,3,2,1,0:T(8,128)S(1)}, f32[8,2,16,8,128]{4,3,2,1,0:T(8,128)}, u32[]{:S(2)}, u32[]{:S(2)}) collective-permute-start(f32[8,2,16,8,128]{4,3,2,1,0:T(8,128)S(1)} %join.2.own), channel_id=1, source_target_pairs={{0,1},{1,0},{2,3},{3,2},{4,5},{5,4},{6,7},{7,6},{8,9},{9,8},{10,11... | collective-permute-start | bytes 3145736 | tf_op jit(solution)/shard_map/ppermute | solution.py:20
  94.1 28.8 %all-to-all-start.1 = ((f32[16,16,8,128]{3,2,1,0:T(8,128)}), f32[16,16,8,128]{3,2,1,0:T(8,128)S(1)}, u32[]{:S(2)}, u32[]{:S(2)}) async-start(f32[16,16,8,128]{3,2,1,0:T(8,128)} %levels.2), calls=%async_computation.1 | async-start | bytes 2097152 | tf_op jit(solution)/shard_map/all_to_all | solution.py:636
  122.9 1.0 copy-start.11

commit v8 on v7

--- a/solution.py
+++ b/solution.py
@@ -287,15 +287,21 @@
 
 def pack_rows(in_ref, lanes, tiles):
     upper = lax.broadcasted_iota(jnp.int32, (8, 128), 0) < 4
-    for t1 in range(16):
-        groups = [None] * 4
-        for high in range(2):
-            real = in_ref[0, t1, 8 * high : 8 * high + 8, lanes]
-            imag = in_ref[1, t1, 8 * high : 8 * high + 8, lanes]
-            groups[2 * high] = jnp.where(upper, real, pltpu.roll(imag, 4, 0))
-            groups[2 * high + 1] = jnp.where(upper, pltpu.roll(real, 4, 0), imag)
-        for j, tile in enumerate(swap_lanes(groups)):
-            tiles[j, t1] = tile
+
+    def step(quarter, carry):
+        for place in range(4):
+            t1 = 4 * quarter + place
+            groups = [None] * 4
+            for high in range(2):
+                real = in_ref[0, t1, 8 * high : 8 * high + 8, lanes]
+                imag = in_ref[1, t1, 8 * high : 8 * high + 8, lanes]
+                groups[2 * high] = jnp.where(upper, real, pltpu.roll(imag, 4, 0))
+                groups[2 * high + 1] = jnp.where(upper, pltpu.roll(real, 4, 0), imag)
+            for j, tile in enumerate(swap_lanes(groups)):
+                tiles[j, t1] = tile
+        return carry
+
+    lax.fori_loop(0, 4, step, 0)
 
 
 def pack_kernel(chunk, in_ref, out_ref, held, arrived):
@@ -551,16 +557,17 @@
 
 
 def unpack_rows(tiles, rows, out_ref, lanes):
-    for part in range(2):
-        for high in range(2):
-            block = part * 2 + high
-            for a in range(4):
-                values = [tiles[j, part * 8 + high * 4 + a] for j in range(4)]
-                for b, tile in enumerate(swap_lanes(values)):
-                    t2 = 4 * b + a
-                    rows[block, 8 * t2 : 8 * t2 + 8, :] = tile
-            for t1 in range(8):
-                out_ref[part, high * 8 + t1, :, lanes] = rows[block, pl.ds(t1, 16, stride=8), :]
+    def step(block, carry):
+        for a in range(4):
+            values = [tiles[j, 4 * block + a] for j in range(4)]
+            for b, tile in enumerate(swap_lanes(values)):
+                t2 = 4 * b + a
+                rows[block, 8 * t2 : 8 * t2 + 8, :] = tile
+        for t1 in range(8):
+            out_ref[block // 2, block % 2 * 8 + t1, :, lanes] = rows[block, pl.ds(t1, 16, stride=8), :]
+        return carry
+
+    lax.fori_loop(0, 4, step, 0)
 
 
 def unpack_kernel(*refs):
@@ -583,6 +590,7 @@
         out_shape=jax.ShapeDtypeStruct((2, 16, 16, 1024), jnp.float32),
         scratch_shapes=[pltpu.VMEM((4, 128, 128), jnp.float32)],
         input_output_aliases=aliases,
+        compiler_params=pltpu.CompilerParams(vmem_limit_bytes=VMEM_LIMIT),
         cost_estimate=pl.CostEstimate(flops=10**6, bytes_accessed=2**21, transcendentals=0),
         name="unpack",
     )(*operands)

time: 128 us -> 128 us (level)
  waiting for transfers between devices: 62.1 us -> 60.2 us
  Pallas kernels: 40.1 us -> 41.7 us
    pallas_call x2, Pallas kernels: 6.42 us -> 8.62 us  [pack(): pl.pallas_call(partial(pack_kernel, chunk), grid=(4,), in_specs=[pl.Block...]
    all_to_all x4, waiting for transfers between devices: 58.1 us -> 55.9 us  [deal(): return lax.all_to_all(pieces, ('bx', 'by'), 0, 0, tiled=True)]
  transfers between devices with their start and end apart: 6 -> 6, of which waited for: 6 -> 6; matrix products, arithmetic and copies ran while one was open for 1% -> 1% of each run, Pallas kernels for 26% -> 27%
where the time goes in v8:
time: 128 us; the launch traced here: 127 us
  waiting for transfers between devices  60.2 us (47%)
  Pallas kernels  41.7 us (33%)
  starting transfers between devices  20.5 us (16%)
  local copies, waits for them, and re-layouts  3.86 us (3%)
    all_to_all x4, waiting for transfers between devices, deal(): return lax.all_to_all(pieces, ('bx', 'by'), 0, 0, tiled=True)  55.9 us
    pallas_call x2, Pallas kernels, levels(): pl.pallas_call(partial(levels_kernel, chunk), in_specs=[in_smem, in_smem]...  23.8 us
    all_to_all x4, starting transfers between devices, deal(): return lax.all_to_all(pieces, ('bx', 'by'), 0, 0, tiled=True)  20.4 us
    pallas_call x2, Pallas kernels, pack(): pl.pallas_call(partial(pack_kernel, chunk), grid=(4,), in_specs=[pl.Block...  8.62 us
    pallas_call x2, Pallas kernels, unpack(): pl.pallas_call(unpack_kernel, grid=(4,), in_specs=in_specs, out_specs=pl....  6.88 us
    ppermute x2, waiting for transfers between devices, partner_2(): return lax.ppermute(value, axis, pairs)  4.29 us
    unnamed x28, local copies, waits for them, and re-layouts  3.23 us
  transfers between devices with their start and end apart: 6, of which 6 were waited for; matrix products, arithmetic and copies ran while one was open for 1% of the time, Pallas kernels for 27%

profile of v8, /device:TPU:10, one launch (start us, length us, event | category | flops | bytes accessed | tf_op | source)
XLA Modules:
  0.0 127.3 jit_solution(8383216659178499070)
XLA Ops:
  0.0 4.3 %pack.3 = f32[16,16,8,128]{3,2,1,0:T(8,128)} custom-call(f32[2,16,16,1024]{3,2,1,0:T(8,128)} %bitcast.30), custom_call_target="tpu_custom_call" | custom-call | flops 1000000 | bytes 2097152 | tf_op jit(solution)/shard_map/pack/pallas_call | solution.py:331
  4.3 7.2 %all-to-all-start.2 = ((f32[16,16,8,128]{3,2,1,0:T(8,128)}), f32[16,16,8,128]{3,2,1,0:T(8,128)S(1)}, u32[]{:S(2)}, u32[]{:S(2)}) async-start(f32[16,16,8,128]{3,2,1,0:T(8,128)} %pack.3), calls=%async_computation.2 | async-start | bytes 2097152 | tf_op jit(solution)/shard_map/all_to_all | solution.py:644
  11.6 4.3 %pack.2 = f32[16,16,8,128]{3,2,1,0:T(8,128)} custom-call(f32[2,16,16,1024]{3,2,1,0:T(8,128)} %bitcast.31), custom_call_target="tpu_custom_call" | custom-call | flops 1000000 | bytes 2097152 | tf_op jit(solution)/shard_map/pack/pallas_call | solution.py:331
  16.0 21.5 %all-to-all-done.2.in_ref = f32[16,16,8,128]{3,2,1,0:T(8,128)S(1)} async-done(((f32[16,16,8,128]{3,2,1,0:T(8,128)}), f32[16,16,8,128]{3,2,1,0:T(8,128)S(1)}, u32[]{:S(2)}, u32[]{:S(2)}) %all-to-all-start.2) | async-done | bytes 1048608 | tf_op jit(solution)/shard_map/all_to_all | solution.py:644
  37.4 4.4 %all-to-all-start = ((f32[16,16,8,128]{3,2,1,0:T(8,128)}), f32[16,16,8,128]{3,2,1,0:T(8,128)}, u32[]{:S(2)}, u32[]{:S(2)}) async-start(f32[16,16,8,128]{3,2,1,0:T(8,128)} %pack.2), calls=%async_computation | async-start | bytes 2097152 | tf_op jit(solution)/shard_map/all_to_all | solution.py:644
  41.9 1.2 copy-done.5
  43.1 0.1 join.3.own
  43.2 0.1 collective-permute-start.1
  43.3 0.1 stack.94
  43.5 0.1 mul.130
  43.5 0.1 add_multiply_fusion
  43.6 0.1 broadcast_in_dim.8
  43.7 0.1 mul.141
  43.8 0.6 fusion.1
  44.4 0.1 add.152
  44.5 0.1 tile.26.speeds
  44.6 0.1 pad_add_fusion.ids
  44.7 1.4 %collective-permute-done.1.other = f32[8,2,16,8,128]{4,3,2,1,0:T(8,128)} collective-permute-done((f32[8,2,16,8,128]{4,3,2,1,0:T(8,128)S(1)}, f32[8,2,16,8,128]{4,3,2,1,0:T(8,128)}, u32[]{:S(2)}, u32[]{:S(2)}) %collective-permute-start.1) | collective-permute-done | bytes 1048608 | tf_op jit(solution)/shard_map/ppermute | solution.py:20
  46.1 11.7 %levels.3 = f32[16,16,8,128]{3,2,1,0:T(8,128)S(1)} custom-call(s32[2]{0:T(128)S(1)} %pad_add_fusion.ids, f32[496]{0:T(512)S(1)} %copy-done.11, f32[8,2,16,8,128]{4,3,2,1,0:T(8,128)S(1)} %join.3.own, f32[8,2,16,8,128]{4,3,2,1,0:T(8,128)} %collective-permute-done.1.other, f32[31,128]{1,0:T(8,128)S(1)} %tile.26.speeds, f32[8,128]{1,0:T(8,128)S(1)} %copy-done.10, ...), custom_call_target="tpu_custom_call" | custom-call | flops 100000000 | bytes 8388608 | tf_op jit(solution)/shard_map/levels/pallas_call | solution.py:540
  57.9 1.0 copy-done.2
  58.8 7.5 %all-to-all-done.in_ref = f32[16,16,8,128]{3,2,1,0:T(8,128)} async-done(((f32[16,16,8,128]{3,2,1,0:T(8,128)}), f32[16,16,8,128]{3,2,1,0:T(8,128)}, u32[]{:S(2)}, u32[]{:S(2)}) %all-to-all-start) | async-done | bytes 1048608 | tf_op jit(solution)/shard_map/all_to_all | solution.py:644
  66.4 4.4 %all-to-all-start.3 = ((f32[16,16,8,128]{3,2,1,0:T(8,128)}), f32[16,16,8,128]{3,2,1,0:T(8,128)S(1)}, u32[]{:S(2)}, u32[]{:S(2)}) async-start(f32[16,16,8,128]{3,2,1,0:T(8,128)} %copy-done.2), calls=%async_computation.3 | async-start | bytes 2097152 | tf_op jit(solution)/shard_map/all_to_all | solution.py:644
  70.8 2.3 %join.2.own = f32[8,2,16,8,128]{4,3,2,1,0:T(8,128)} custom-call(f32[16,16,8,128]{3,2,1,0:T(8,128)} %all-to-all-done.in_ref), custom_call_target="tpu_custom_call" | custom-call | flops 1000000 | bytes 2097152 | tf_op jit(solution)/shard_map/join/pallas_call | solution.py:362
  73.1 0.1 tile.24.speeds
  73.2 2.9 %collective-permute-done.other = f32[8,2,16,8,128]{4,3,2,1,0:T(8,128)} collective-permute-done((f32[8,2,16,8,128]{4,3,2,1,0:T(8,128)}, f32[8,2,16,8,128]{4,3,2,1,0:T(8,128)}, u32[]{:S(2)}, u32[]{:S(2)}) %collective-permute-start) | collective-permute-done | bytes 1048608 | tf_op jit(solution)/shard_map/ppermute | solution.py:20
  76.1 12.0 %levels.2 = f32[16,16,8,128]{3,2,1,0:T(8,128)S(1)} custom-call(s32[2]{0:T(128)S(1)} %pad_add_fusion.ids, f32[496]{0:T(512)S(1)} %copy-done.11, f32[8,2,16,8,128]{4,3,2,1,0:T(8,128)} %join.2.own, f32[8,2,16,8,128]{4,3,2,1,0:T(8,128)} %collective-permute-done.other, f32[31,128]{1,0:T(8,128)S(1)} %tile.24.speeds, f32[8,128]{1,0:T(8,128)S(1)} %copy-done.10, ...), custom_call_target="tpu_custom_call" | custom-call | flops 100000000 | bytes 8388608 | tf_op jit(solution)/shard_map/levels/pallas_call | solution.py:540
  88.1 1.0 copy-done.3
  89.1 6.0 %all-to-all-done.3.refs_0_ = f32[16,16,8,128]{3,2,1,0:T(8,128)S(1)} async-done(((f32[16,16,8,128]{3,2,1,0:T(8,128)}), f32[16,16,8,128]{3,2,1,0:T(8,128)S(1)}, u32[]{:S(2)}, u32[]{:S(2)}) %all-to-all-start.3) | async-done | bytes 1048608 | tf_op jit(solution)/shard_map/all_to_all | solution.py:644
  95.1 4.4 %all-to-all-start.1 = ((f32[16,16,8,128]{3,2,1,0:T(8,128)}), f32[16,16,8,128]{3,2,1,0:T(8,128)S(1)}, u32[]{:S(2)}, u32[]{:S(2)}) async-start(f32[16,16,8,128]{3,2,1,0:T(8,128)} %copy-done.3), calls=%async_computation.1 | async-start | bytes 2097152 | tf_op jit(solution)/shard_map/all_to_all | solution.py:644
  99.5 3.4 %unpack.2.refs_1_ = f32[2,16,16,1024]{3,2,1,0:T(8,128)} custom-call(f32[16,16,8,128]{3,2,1,0:T(8,128)S(1)} %all-to-all-done.3.refs_0_), custom_call_target="tpu_custom_call" | custom-call | flops 1000000 | bytes 2097152 | tf_op jit(solution)/shard_map/unpack/pallas_call | solution.py:585
  103.0 20.9 %all-to-all-done.1.refs_0_ = f32[16,16,8,128]{3,2,1,0:T(8,128)S(1)} async-done(((f32[16,16,8,128]{3,2,1,0:T(8,128)}), f32[16,16,8,128]{3,2,1,0:T(8,128)S(1)}, u32[]{:S(2)}, u32[]{:S(2)}) %all-to-all-start.1) | async-done | bytes 1048608 | tf_op jit(solution)/shard_map/all_to_all | solution.py:644
  123.9 3.4 %unpack.3 = f32[2,16,16,1024]{3,2,1,0:T(8,128)} custom-call(f32[16,16,8,128]{3,2,1,0:T(8,128)S(1)} %all-to-all-done.1.refs_0_, f32[2,16,16,1024]{3,2,1,0:T(8,128)} %unpack.2.refs_1_), custom_call_target="tpu_custom_call", output_to_operand_aliasing={{}: (1, {})} | custom-call | flops 1000000 | bytes 2097152 | tf_op jit(solution)/shard_map/unpack/pallas_call | solution.py:585
  (40 shorter events, 0.2 us)
Async XLA Ops:
  0.0 43.8 %copy-start = (f32[4,4]{1,0:T(4,128)S(1)}, f32[4,4]{1,0:T(4,128)}, u32[]{:S(2)}) copy-start(f32[4,4]{1,0:T(4,128)} %param.20) | copy-start | bytes 196
  4.3 33.1 %all-to-all-start.2 = ((f32[16,16,8,128]{3,2,1,0:T(8,128)}), f32[16,16,8,128]{3,2,1,0:T(8,128)S(1)}, u32[]{:S(2)}, u32[]{:S(2)}) async-start(f32[16,16,8,128]{3,2,1,0:T(8,128)} %pack.3), calls=%async_computation.2 | async-start | bytes 2097152 | tf_op jit(solution)/shard_map/all_to_all | solution.py:644
  11.5 34.5 %copy-start.7 = (f32[2,4,8,128]{3,2,1,0:T(8,128)S(1)}, f32[2,4,8,128]{3,2,1,0:T(8,128)}, u32[]{:S(2)}) copy-start(f32[2,4,8,128]{3,2,1,0:T(8,128)} %constant.77.clone.last_lengths) | copy-start | bytes 98308
  11.5 34.5 %copy-start.8 = (f32[4,8,128]{2,1,0:T(8,128)S(1)}, f32[4,8,128]{2,1,0:T(8,128)}, u32[]{:S(2)}) copy-start(f32[4,8,128]{2,1,0:T(8,128)} %constant.76.clone.last_two) | copy-start | bytes 49156
  11.5 34.5 %copy-start.11 = (f32[496]{0:T(512)S(1)}, f32[496]{0:T(512)}, u32[]{:S(2)}) copy-start(f32[496]{0:T(512)} %constant.72.clone.nodes) | copy-start | bytes 5956
  15.9 27.6 %copy-start.12 = (f32[31]{0:T(128)S(1)}, f32[31]{0:T(128)}, u32[]{:S(2)}) copy-start(f32[31]{0:T(128)} %constant.82) | copy-start | bytes 376
  15.9 27.6 %copy-start.13 = (f32[31]{0:T(128)S(1)}, f32[31]{0:T(128)}, u32[]{:S(2)}) copy-start(f32[31]{0:T(128)} %constant.71.clone) | copy-start | bytes 376
  15.9 30.2 %copy-start.1 = (f32[496,8,128]{2,1,0:T(8,128)S(1)}, f32[496,8,128]{2,1,0:T(8,128)}, u32[]{:S(2)}) copy-start(f32[496,8,128]{2,1,0:T(8,128)} %constant.74.clone.lengths) | copy-start | bytes 6094852
  15.9 30.2 %copy-start.6 = (bf16[256,256]{1,0:T(8,128)(2,1)S(1)}, bf16[256,256]{1,0:T(8,128)(2,1)}, u32[]{:S(2)}) copy-start(bf16[256,256]{1,0:T(8,128)(2,1)} %constant.78.clone.first_table) | copy-start | bytes 393220
  15.9 30.2 %copy-start.9 = (f32[2,8,128]{2,1,0:T(8,128)S(1)}, f32[2,8,128]{2,1,0:T(8,128)}, u32[]{:S(2)}) copy-start(f32[2,8,128]{2,1,0:T(8,128)} %constant.75.clone.last_one) | copy-start | bytes 24580
  15.9 30.2 %copy-start.10 = (f32[8,128]{1,0:T(8,128)S(1)}, f32[8,128]{1,0:T(8,128)}, u32[]{:S(2)}) copy-start(f32[8,128]{1,0:T(8,128)} %constant.73.clone.waves) | copy-start | bytes 12292
  37.4 4.4 %copy-start.4 = (f32[16,16,8,128]{3,2,1,0:T(8,128)}, f32[16,16,8,128]{3,2,1,0:T(8,128)S(1)}, u32[]{:S(2)}) copy-start(f32[16,16,8,128]{3,2,1,0:T(8,128)S(1)} %all-to-all-done.2.in_ref) | copy-start | bytes 3145732
  37.4 28.9 %all-to-all-start = ((f32[16,16,8,128]{3,2,1,0:T(8,128)}), f32[16,16,8,128]{3,2,1,0:T(8,128)}, u32[]{:S(2)}, u32[]{:S(2)}) async-start(f32[16,16,8,128]{3,2,1,0:T(8,128)} %pack.2), calls=%async_computation | async-start | bytes 2097152 | tf_op jit(solution)/shard_map/all_to_all | solution.py:644
  41.9 1.2 copy-start.5
  43.2 2.9 %collective-permute-start.1 = (f32[8,2,16,8,128]{4,3,2,1,0:T(8,128)S(1)}, f32[8,2,16,8,128]{4,3,2,1,0:T(8,128)}, u32[]{:S(2)}, u32[]{:S(2)}) collective-permute-start(f32[8,2,16,8,128]{4,3,2,1,0:T(8,128)S(1)} %join.3.own), channel_id=1, source_target_pairs={{0,1},{1,0},{2,3},{3,2},{4,5},{5,4},{6,7},{7,6},{8,9},{9,8},{10,11... | collective-permute-start | bytes 3145736 | tf_op jit(solution)/shard_map/ppermute | solution.py:20
  57.9 1.0 copy-start.2
  66.4 28.8 %all-to-all-start.3 = ((f32[16,16,8,128]{3,2,1,0:T(8,128)}), f32[16,16,8,128]{3,2,1,0:T(8,128)S(1)}, u32[]{:S(2)}, u32[]{:S(2)}) async-start(f32[16,16,8,128]{3,2,1,0:T(8,128)} %copy-done.2), calls=%async_computation.3 | async-start | bytes 2097152 | tf_op jit(solution)/shard_map/all_to_all | solution.py:644
  73.0 3.0 %collective-permute-start = (f32[8,2,16,8,128]{4,3,2,1,0:T(8,128)}, f32[8,2,16,8,128]{4,3,2,1,0:T(8,128)}, u32[]{:S(2)}, u32[]{:S(2)}) collective-permute-start(f32[8,2,16,8,128]{4,3,2,1,0:T(8,128)} %join.2.own), channel_id=1, source_target_pairs={{0,1},{1,0},{2,3},{3,2},{4,5},{5,4},{6,7},{7,6},{8,9},{9,8},{10,11... | collective-permute-start | bytes 3145736 | tf_op jit(solution)/shard_map/ppermute | solution.py:20
  88.1 1.0 copy-start.3
  95.1 28.8 %all-to-all-start.1 = ((f32[16,16,8,128]{3,2,1,0:T(8,128)}), f32[16,16,8,128]{3,2,1,0:T(8,128)S(1)}, u32[]{:S(2)}, u32[]{:S(2)}) async-start(f32[16,16,8,128]{3,2,1,0:T(8,128)} %copy-done.3), calls=%async_computation.1 | async-start | bytes 2097152 | tf_op jit(solution)/shard_map/all_to_all | solution.py:644

commit v9 on v7

--- a/solution.py
+++ b/solution.py
@@ -583,6 +583,7 @@
         out_shape=jax.ShapeDtypeStruct((2, 16, 16, 1024), jnp.float32),
         scratch_shapes=[pltpu.VMEM((4, 128, 128), jnp.float32)],
         input_output_aliases=aliases,
+        compiler_params=pltpu.CompilerParams(vmem_limit_bytes=VMEM_LIMIT),
         cost_estimate=pl.CostEstimate(flops=10**6, bytes_accessed=2**21, transcendentals=0),
         name="unpack",
     )(*operands)

time: 128 us -> 126 us (0.984)
  Pallas kernels: 40.1 us -> 37.1 us
    pallas_call x2, Pallas kernels: 7.75 us -> 4.51 us  [unpack(): pl.pallas_call(unpack_kernel, grid=(4,), in_specs=in_specs, out_specs=pl....]
  transfers between devices with their start and end apart: 6 -> 6, of which waited for: 6 -> 6; matrix products, arithmetic and copies ran while one was open for 1% -> 1% of each run, Pallas kernels for 26% -> 25%
where the time goes in v9:
time: 126 us; the launch traced here: 125 us
  waiting for transfers between devices  62.5 us (50%)
  Pallas kernels  37.1 us (29%)
  starting transfers between devices  20.5 us (16%)
  local copies, waits for them, and re-layouts  3.86 us (3%)
    all_to_all x4, waiting for transfers between devices, deal(): return lax.all_to_all(pieces, ('bx', 'by'), 0, 0, tiled=True)  58.2 us
    pallas_call x2, Pallas kernels, levels(): pl.pallas_call(partial(levels_kernel, chunk), in_specs=[in_smem, in_smem]...  23.8 us
    all_to_all x4, starting transfers between devices, deal(): return lax.all_to_all(pieces, ('bx', 'by'), 0, 0, tiled=True)  20.4 us
    pallas_call x2, Pallas kernels, pack(): pl.pallas_call(partial(pack_kernel, chunk), grid=(4,), in_specs=[pl.Block...  6.42 us
    pallas_call x2, Pallas kernels, unpack(): pl.pallas_call(unpack_kernel, grid=(4,), in_specs=in_specs, out_specs=pl....  4.51 us
    ppermute x2, waiting for transfers between devices, partner_2(): return lax.ppermute(value, axis, pairs)  4.29 us
    unnamed x28, local copies, waits for them, and re-layouts  3.23 us
  transfers between devices with their start and end apart: 6, of which 6 were waited for; matrix products, arithmetic and copies ran while one was open for 1% of the time, Pallas kernels for 25%

profile of v9, /device:TPU:10, one launch (start us, length us, event | category | flops | bytes accessed | tf_op | source)
XLA Modules:
  0.0 125.0 jit_solution(3762741799527172223)
XLA Ops:
  0.0 3.2 %pack.3 = f32[16,16,8,128]{3,2,1,0:T(8,128)} custom-call(f32[2,16,16,1024]{3,2,1,0:T(8,128)} %bitcast.30), custom_call_target="tpu_custom_call" | custom-call | flops 1000000 | bytes 2097152 | tf_op jit(solution)/shard_map/pack/pallas_call | solution.py:325
  3.2 7.2 %all-to-all-start.2 = ((f32[16,16,8,128]{3,2,1,0:T(8,128)}), f32[16,16,8,128]{3,2,1,0:T(8,128)S(1)}, u32[]{:S(2)}, u32[]{:S(2)}) async-start(f32[16,16,8,128]{3,2,1,0:T(8,128)} %pack.3), calls=%async_computation.2 | async-start | bytes 2097152 | tf_op jit(solution)/shard_map/all_to_all | solution.py:637
  10.5 3.2 %pack.2 = f32[16,16,8,128]{3,2,1,0:T(8,128)} custom-call(f32[2,16,16,1024]{3,2,1,0:T(8,128)} %bitcast.31), custom_call_target="tpu_custom_call" | custom-call | flops 1000000 | bytes 2097152 | tf_op jit(solution)/shard_map/pack/pallas_call | solution.py:325
  13.8 22.6 %all-to-all-done.2.in_ref = f32[16,16,8,128]{3,2,1,0:T(8,128)S(1)} async-done(((f32[16,16,8,128]{3,2,1,0:T(8,128)}), f32[16,16,8,128]{3,2,1,0:T(8,128)S(1)}, u32[]{:S(2)}, u32[]{:S(2)}) %all-to-all-start.2) | async-done | bytes 1048608 | tf_op jit(solution)/shard_map/all_to_all | solution.py:637
  36.3 4.4 %all-to-all-start = ((f32[16,16,8,128]{3,2,1,0:T(8,128)}), f32[16,16,8,128]{3,2,1,0:T(8,128)}, u32[]{:S(2)}, u32[]{:S(2)}) async-start(f32[16,16,8,128]{3,2,1,0:T(8,128)} %pack.2), calls=%async_computation | async-start | bytes 2097152 | tf_op jit(solution)/shard_map/all_to_all | solution.py:637
  40.8 1.2 copy-done.5
  42.0 0.1 join.3.own
  42.1 0.1 collective-permute-start.1
  42.2 0.1 stack.94
  42.4 0.1 mul.130
  42.4 0.1 add_multiply_fusion
  42.5 0.1 broadcast_in_dim.8
  42.6 0.1 mul.141
  42.7 0.6 fusion.1
  43.3 0.1 add.152
  43.4 0.1 tile.26.speeds
  43.5 0.1 pad_add_fusion.ids
  43.6 1.4 %collective-permute-done.1.other = f32[8,2,16,8,128]{4,3,2,1,0:T(8,128)} collective-permute-done((f32[8,2,16,8,128]{4,3,2,1,0:T(8,128)S(1)}, f32[8,2,16,8,128]{4,3,2,1,0:T(8,128)}, u32[]{:S(2)}, u32[]{:S(2)}) %collective-permute-start.1) | collective-permute-done | bytes 1048608 | tf_op jit(solution)/shard_map/ppermute | solution.py:20
  45.0 11.7 %levels.3 = f32[16,16,8,128]{3,2,1,0:T(8,128)S(1)} custom-call(s32[2]{0:T(128)S(1)} %pad_add_fusion.ids, f32[496]{0:T(512)S(1)} %copy-done.11, f32[8,2,16,8,128]{4,3,2,1,0:T(8,128)S(1)} %join.3.own, f32[8,2,16,8,128]{4,3,2,1,0:T(8,128)} %collective-permute-done.1.other, f32[31,128]{1,0:T(8,128)S(1)} %tile.26.speeds, f32[8,128]{1,0:T(8,128)S(1)} %copy-done.10, ...), custom_call_target="tpu_custom_call" | custom-call | flops 100000000 | bytes 8388608 | tf_op jit(solution)/shard_map/levels/pallas_call | solution.py:534
  56.8 1.0 copy-done.2
  57.7 7.5 %all-to-all-done.in_ref = f32[16,16,8,128]{3,2,1,0:T(8,128)} async-done(((f32[16,16,8,128]{3,2,1,0:T(8,128)}), f32[16,16,8,128]{3,2,1,0:T(8,128)}, u32[]{:S(2)}, u32[]{:S(2)}) %all-to-all-start) | async-done | bytes 1048608 | tf_op jit(solution)/shard_map/all_to_all | solution.py:637
  65.2 4.4 %all-to-all-start.3 = ((f32[16,16,8,128]{3,2,1,0:T(8,128)}), f32[16,16,8,128]{3,2,1,0:T(8,128)S(1)}, u32[]{:S(2)}, u32[]{:S(2)}) async-start(f32[16,16,8,128]{3,2,1,0:T(8,128)} %copy-done.2), calls=%async_computation.3 | async-start | bytes 2097152 | tf_op jit(solution)/shard_map/all_to_all | solution.py:637
  69.7 2.3 %join.2.own = f32[8,2,16,8,128]{4,3,2,1,0:T(8,128)} custom-call(f32[16,16,8,128]{3,2,1,0:T(8,128)} %all-to-all-done.in_ref), custom_call_target="tpu_custom_call" | custom-call | flops 1000000 | bytes 2097152 | tf_op jit(solution)/shard_map/join/pallas_call | solution.py:356
  72.0 0.1 tile.24.speeds
  72.1 2.9 %collective-permute-done.other = f32[8,2,16,8,128]{4,3,2,1,0:T(8,128)} collective-permute-done((f32[8,2,16,8,128]{4,3,2,1,0:T(8,128)}, f32[8,2,16,8,128]{4,3,2,1,0:T(8,128)}, u32[]{:S(2)}, u32[]{:S(2)}) %collective-permute-start) | collective-permute-done | bytes 1048608 | tf_op jit(solution)/shard_map/ppermute | solution.py:20
  75.0 12.0 %levels.2 = f32[16,16,8,128]{3,2,1,0:T(8,128)S(1)} custom-call(s32[2]{0:T(128)S(1)} %pad_add_fusion.ids, f32[496]{0:T(512)S(1)} %copy-done.11, f32[8,2,16,8,128]{4,3,2,1,0:T(8,128)} %join.2.own, f32[8,2,16,8,128]{4,3,2,1,0:T(8,128)} %collective-permute-done.other, f32[31,128]{1,0:T(8,128)S(1)} %tile.24.speeds, f32[8,128]{1,0:T(8,128)S(1)} %copy-done.10, ...), custom_call_target="tpu_custom_call" | custom-call | flops 100000000 | bytes 8388608 | tf_op jit(solution)/shard_map/levels/pallas_call | solution.py:534
  87.0 1.0 copy-done.3
  88.0 6.0 %all-to-all-done.3.refs_0_ = f32[16,16,8,128]{3,2,1,0:T(8,128)S(1)} async-done(((f32[16,16,8,128]{3,2,1,0:T(8,128)}), f32[16,16,8,128]{3,2,1,0:T(8,128)S(1)}, u32[]{:S(2)}, u32[]{:S(2)}) %all-to-all-start.3) | async-done | bytes 1048608 | tf_op jit(solution)/shard_map/all_to_all | solution.py:637
  94.0 4.4 %all-to-all-start.1 = ((f32[16,16,8,128]{3,2,1,0:T(8,128)}), f32[16,16,8,128]{3,2,1,0:T(8,128)S(1)}, u32[]{:S(2)}, u32[]{:S(2)}) async-start(f32[16,16,8,128]{3,2,1,0:T(8,128)} %copy-done.3), calls=%async_computation.1 | async-start | bytes 2097152 | tf_op jit(solution)/shard_map/all_to_all | solution.py:637
  98.4 2.3 %unpack.2.refs_1_ = f32[2,16,16,1024]{3,2,1,0:T(8,128)} custom-call(f32[16,16,8,128]{3,2,1,0:T(8,128)S(1)} %all-to-all-done.3.refs_0_), custom_call_target="tpu_custom_call" | custom-call | flops 1000000 | bytes 2097152 | tf_op jit(solution)/shard_map/unpack/pallas_call | solution.py:578
  100.7 22.1 %all-to-all-done.1.refs_0_ = f32[16,16,8,128]{3,2,1,0:T(8,128)S(1)} async-done(((f32[16,16,8,128]{3,2,1,0:T(8,128)}), f32[16,16,8,128]{3,2,1,0:T(8,128)S(1)}, u32[]{:S(2)}, u32[]{:S(2)}) %all-to-all-start.1) | async-done | bytes 1048608 | tf_op jit(solution)/shard_map/all_to_all | solution.py:637
  122.8 2.2 %unpack.3 = f32[2,16,16,1024]{3,2,1,0:T(8,128)} custom-call(f32[16,16,8,128]{3,2,1,0:T(8,128)S(1)} %all-to-all-done.1.refs_0_, f32[2,16,16,1024]{3,2,1,0:T(8,128)} %unpack.2.refs_1_), custom_call_target="tpu_custom_call", output_to_operand_aliasing={{}: (1, {})} | custom-call | flops 1000000 | bytes 2097152 | tf_op jit(solution)/shard_map/unpack/pallas_call | solution.py:578
  (40 shorter events, 0.2 us)
Async XLA Ops:
  0.0 42.7 %copy-start = (f32[4,4]{1,0:T(4,128)S(1)}, f32[4,4]{1,0:T(4,128)}, u32[]{:S(2)}) copy-start(f32[4,4]{1,0:T(4,128)} %param.20) | copy-start | bytes 196
  3.2 33.1 %all-to-all-start.2 = ((f32[16,16,8,128]{3,2,1,0:T(8,128)}), f32[16,16,8,128]{3,2,1,0:T(8,128)S(1)}, u32[]{:S(2)}, u32[]{:S(2)}) async-start(f32[16,16,8,128]{3,2,1,0:T(8,128)} %pack.3), calls=%async_computation.2 | async-start | bytes 2097152 | tf_op jit(solution)/shard_map/all_to_all | solution.py:637
  10.4 34.5 %copy-start.7 = (f32[2,4,8,128]{3,2,1,0:T(8,128)S(1)}, f32[2,4,8,128]{3,2,1,0:T(8,128)}, u32[]{:S(2)}) copy-start(f32[2,4,8,128]{3,2,1,0:T(8,128)} %constant.77.clone.last_lengths) | copy-start | bytes 98308
  10.4 34.5 %copy-start.8 = (f32[4,8,128]{2,1,0:T(8,128)S(1)}, f32[4,8,128]{2,1,0:T(8,128)}, u32[]{:S(2)}) copy-start(f32[4,8,128]{2,1,0:T(8,128)} %constant.76.clone.last_two) | copy-start | bytes 49156
  10.4 34.5 %copy-start.11 = (f32[496]{0:T(512)S(1)}, f32[496]{0:T(512)}, u32[]{:S(2)}) copy-start(f32[496]{0:T(512)} %constant.72.clone.nodes) | copy-start | bytes 5956
  13.7 28.7 %copy-start.12 = (f32[31]{0:T(128)S(1)}, f32[31]{0:T(128)}, u32[]{:S(2)}) copy-start(f32[31]{0:T(128)} %constant.82) | copy-start | bytes 376
  13.7 28.7 %copy-start.13 = (f32[31]{0:T(128)S(1)}, f32[31]{0:T(128)}, u32[]{:S(2)}) copy-start(f32[31]{0:T(128)} %constant.71.clone) | copy-start | bytes 376
  13.7 31.3 %copy-start.1 = (f32[496,8,128]{2,1,0:T(8,128)S(1)}, f32[496,8,128]{2,1,0:T(8,128)}, u32[]{:S(2)}) copy-start(f32[496,8,128]{2,1,0:T(8,128)} %constant.74.clone.lengths) | copy-start | bytes 6094852
  13.7 31.3 %copy-start.6 = (bf16[256,256]{1,0:T(8,128)(2,1)S(1)}, bf16[256,256]{1,0:T(8,128)(2,1)}, u32[]{:S(2)}) copy-start(bf16[256,256]{1,0:T(8,128)(2,1)} %constant.78.clone.first_table) | copy-start | bytes 393220
  13.7 31.3 %copy-start.9 = (f32[2,8,128]{2,1,0:T(8,128)S(1)}, f32[2,8,128]{2,1,0:T(8,128)}, u32[]{:S(2)}) copy-start(f32[2,8,128]{2,1,0:T(8,128)} %constant.75.clone.last_one) | copy-start | bytes 24580
  13.7 31.3 %copy-start.10 = (f32[8,128]{1,0:T(8,128)S(1)}, f32[8,128]{1,0:T(8,128)}, u32[]{:S(2)}) copy-start(f32[8,128]{1,0:T(8,128)} %constant.73.clone.waves) | copy-start | bytes 12292
  36.3 4.4 %copy-start.4 = (f32[16,16,8,128]{3,2,1,0:T(8,128)}, f32[16,16,8,128]{3,2,1,0:T(8,128)S(1)}, u32[]{:S(2)}) copy-start(f32[16,16,8,128]{3,2,1,0:T(8,128)S(1)} %all-to-all-done.2.in_ref) | copy-start | bytes 3145732
  36.3 28.9 %all-to-all-start = ((f32[16,16,8,128]{3,2,1,0:T(8,128)}), f32[16,16,8,128]{3,2,1,0:T(8,128)}, u32[]{:S(2)}, u32[]{:S(2)}) async-start(f32[16,16,8,128]{3,2,1,0:T(8,128)} %pack.2), calls=%async_computation | async-start | bytes 2097152 | tf_op jit(solution)/shard_map/all_to_all | solution.py:637
  40.8 1.2 copy-start.5
  42.1 2.9 %collective-permute-start.1 = (f32[8,2,16,8,128]{4,3,2,1,0:T(8,128)S(1)}, f32[8,2,16,8,128]{4,3,2,1,0:T(8,128)}, u32[]{:S(2)}, u32[]{:S(2)}) collective-permute-start(f32[8,2,16,8,128]{4,3,2,1,0:T(8,128)S(1)} %join.3.own), channel_id=1, source_target_pairs={{0,1},{1,0},{2,3},{3,2},{4,5},{5,4},{6,7},{7,6},{8,9},{9,8},{10,11... | collective-permute-start | bytes 3145736 | tf_op jit(solution)/shard_map/ppermute | solution.py:20
  56.8 1.0 copy-start.2
  65.2 28.8 %all-to-all-start.3 = ((f32[16,16,8,128]{3,2,1,0:T(8,128)}), f32[16,16,8,128]{3,2,1,0:T(8,128)S(1)}, u32[]{:S(2)}, u32[]{:S(2)}) async-start(f32[16,16,8,128]{3,2,1,0:T(8,128)} %copy-done.2), calls=%async_computation.3 | async-start | bytes 2097152 | tf_op jit(solution)/shard_map/all_to_all | solution.py:637
  71.9 3.0 %collective-permute-start = (f32[8,2,16,8,128]{4,3,2,1,0:T(8,128)}, f32[8,2,16,8,128]{4,3,2,1,0:T(8,128)}, u32[]{:S(2)}, u32[]{:S(2)}) collective-permute-start(f32[8,2,16,8,128]{4,3,2,1,0:T(8,128)} %join.2.own), channel_id=1, source_target_pairs={{0,1},{1,0},{2,3},{3,2},{4,5},{5,4},{6,7},{7,6},{8,9},{9,8},{10,11... | collective-permute-start | bytes 3145736 | tf_op jit(solution)/shard_map/ppermute | solution.py:20
  87.0 1.0 copy-start.3
  94.0 28.8 %all-to-all-start.1 = ((f32[16,16,8,128]{3,2,1,0:T(8,128)}), f32[16,16,8,128]{3,2,1,0:T(8,128)S(1)}, u32[]{:S(2)}, u32[]{:S(2)}) async-start(f32[16,16,8,128]{3,2,1,0:T(8,128)} %copy-done.3), calls=%async_computation.1 | async-start | bytes 2097152 | tf_op jit(solution)/shard_map/all_to_all | solution.py:637

commit v10 on v9

--- a/solution.py
+++ b/solution.py
@@ -298,37 +298,44 @@
             tiles[j, t1] = tile
 
 
-def pack_kernel(chunk, in_ref, out_ref, held, arrived):
-    group = pl.program_id(0)
-
-    def fetch(place):
-        lanes = pl.ds((4 * chunk + place) * 128, 128)
+def pack_kernel(chunk, in_ref, out_ref, held, packed, arrived, left):
+    def fetch(group):
+        lanes = pl.ds(pl.multiple_of((4 * chunk + group) * 128, 128), 128)
         return pltpu.make_async_copy(
-            in_ref.at[:, :, :, lanes], held.at[place], arrived.at[place]
+            in_ref.at[:, :, :, lanes], held.at[group], arrived.at[group]
         )
 
-    @pl.when(group == 0)
-    def _():
-        for place in range(4):
-            fetch(place).start()
-
-    for place in range(4):
-
-        @pl.when(group == place)
-        def _(place=place):
-            fetch(place).wait()
-
-    pack_rows(held.at[group], slice(None), out_ref)
+    def send(group):
+        return pltpu.make_async_copy(
+            packed.at[group], out_ref.at[pl.ds(4 * group, 4)], left.at[group]
+        )
+
+    for group in range(4):
+        fetch(group).start()
+
+    def step(group, carry):
+        fetch(group).wait()
+        pack_rows(held.at[group], slice(None), packed.at[group])
+        send(group).start()
+        return carry
+
+    lax.fori_loop(0, 4, step, 0)
+    for group in range(4):
+        send(group).wait()
 
 
 def pack(weights, chunk):
     return pl.pallas_call(
         partial(pack_kernel, chunk),
-        grid=(4,),
         in_specs=[pl.BlockSpec(memory_space=pl.ANY)],
-        out_specs=pl.BlockSpec((4, 16, 8, 128), lambda i: (i, 0, 0, 0)),
+        out_specs=pl.BlockSpec(memory_space=pl.ANY),
         out_shape=jax.ShapeDtypeStruct((PIECES, 16, 8, 128), jnp.float32),
-        scratch_shapes=[pltpu.VMEM((4, 2, 16, 16, 128), jnp.float32), pltpu.SemaphoreType.DMA((4,))],
+        scratch_shapes=[
+            pltpu.VMEM((4, 2, 16, 16, 128), jnp.float32),
+            pltpu.VMEM((4, 4, 16, 8, 128), jnp.float32),
+            pltpu.SemaphoreType.DMA((4,)),
+            pltpu.SemaphoreType.DMA((4,)),
+        ],
         cost_estimate=pl.CostEstimate(flops=10**6, bytes_accessed=2**21, transcendentals=0),
         name="pack",
     )(weights)

time: 126 us -> 125 us (level)
  no operation moved by 1% of the time
where the time goes in v10:
time: 125 us
  waiting for transfers between devices  62.9 us (50%)
  Pallas kernels  36.3 us (29%)
  starting transfers between devices  20.5 us (16%)
  local copies, waits for them, and re-layouts  3.86 us (3%)
    all_to_all x4, waiting for transfers between devices, deal(): return lax.all_to_all(pieces, ('bx', 'by'), 0, 0, tiled=True)  58.6 us
    pallas_call x2, Pallas kernels, levels(): pl.pallas_call(partial(levels_kernel, chunk), in_specs=[in_smem, in_smem]...  23.8 us
    all_to_all x4, starting transfers between devices, deal(): return lax.all_to_all(pieces, ('bx', 'by'), 0, 0, tiled=True)  20.4 us
    pallas_call x2, Pallas kernels, pack(): pl.pallas_call(partial(pack_kernel, chunk), in_specs=[pl.BlockSpec(memory...  5.59 us
    pallas_call x2, Pallas kernels, unpack(): pl.pallas_call(unpack_kernel, grid=(4,), in_specs=in_specs, out_specs=pl....  4.51 us
    ppermute x2, waiting for transfers between devices, partner_2(): return lax.ppermute(value, axis, pairs)  4.29 us
    unnamed x28, local copies, waits for them, and re-layouts  3.23 us
  transfers between devices with their start and end apart: 6, of which 6 were waited for; matrix products, arithmetic and copies ran while one was open for 1% of the time, Pallas kernels for 25%

profile of v10, /device:TPU:10, one launch (start us, length us, event | category | flops | bytes accessed | tf_op | source)
XLA Modules:
  0.0 124.6 jit_solution(13476601577705296829)
XLA Ops:
  0.0 2.8 %pack.3 = f32[16,16,8,128]{3,2,1,0:T(8,128)} custom-call(f32[2,16,16,1024]{3,2,1,0:T(8,128)} %bitcast.30), custom_call_target="tpu_custom_call" | custom-call | flops 1000000 | bytes 2097152 | tf_op jit(solution)/shard_map/pack/pallas_call | solution.py:328
  2.8 7.2 %all-to-all-start.2 = ((f32[16,16,8,128]{3,2,1,0:T(8,128)}), f32[16,16,8,128]{3,2,1,0:T(8,128)S(1)}, u32[]{:S(2)}, u32[]{:S(2)}) async-start(f32[16,16,8,128]{3,2,1,0:T(8,128)} %pack.3), calls=%async_computation.2 | async-start | bytes 2097152 | tf_op jit(solution)/shard_map/all_to_all | solution.py:644
  10.0 2.8 %pack.2 = f32[16,16,8,128]{3,2,1,0:T(8,128)} custom-call(f32[2,16,16,1024]{3,2,1,0:T(8,128)} %bitcast.31), custom_call_target="tpu_custom_call" | custom-call | flops 1000000 | bytes 2097152 | tf_op jit(solution)/shard_map/pack/pallas_call | solution.py:328
  12.9 23.0 %all-to-all-done.2.in_ref = f32[16,16,8,128]{3,2,1,0:T(8,128)S(1)} async-done(((f32[16,16,8,128]{3,2,1,0:T(8,128)}), f32[16,16,8,128]{3,2,1,0:T(8,128)S(1)}, u32[]{:S(2)}, u32[]{:S(2)}) %all-to-all-start.2) | async-done | bytes 1048608 | tf_op jit(solution)/shard_map/all_to_all | solution.py:644
  35.9 4.4 %all-to-all-start = ((f32[16,16,8,128]{3,2,1,0:T(8,128)}), f32[16,16,8,128]{3,2,1,0:T(8,128)}, u32[]{:S(2)}, u32[]{:S(2)}) async-start(f32[16,16,8,128]{3,2,1,0:T(8,128)} %pack.2), calls=%async_computation | async-start | bytes 2097152 | tf_op jit(solution)/shard_map/all_to_all | solution.py:644
  40.4 1.2 copy-done.5
  41.6 0.1 join.3.own
  41.7 0.1 collective-permute-start.1
  41.8 0.1 stack.94
  41.9 0.1 mul.130
  42.0 0.1 add_multiply_fusion
  42.1 0.1 broadcast_in_dim.8
  42.2 0.1 mul.141
  42.3 0.6 fusion.1
  42.9 0.1 add.152
  43.0 0.1 tile.26.speeds
  43.1 0.1 pad_add_fusion.ids
  43.2 1.4 %collective-permute-done.1.other = f32[8,2,16,8,128]{4,3,2,1,0:T(8,128)} collective-permute-done((f32[8,2,16,8,128]{4,3,2,1,0:T(8,128)S(1)}, f32[8,2,16,8,128]{4,3,2,1,0:T(8,128)}, u32[]{:S(2)}, u32[]{:S(2)}) %collective-permute-start.1) | collective-permute-done | bytes 1048608 | tf_op jit(solution)/shard_map/ppermute | solution.py:20
  44.6 11.7 %levels.3 = f32[16,16,8,128]{3,2,1,0:T(8,128)S(1)} custom-call(s32[2]{0:T(128)S(1)} %pad_add_fusion.ids, f32[496]{0:T(512)S(1)} %copy-done.11, f32[8,2,16,8,128]{4,3,2,1,0:T(8,128)S(1)} %join.3.own, f32[8,2,16,8,128]{4,3,2,1,0:T(8,128)} %collective-permute-done.1.other, f32[31,128]{1,0:T(8,128)S(1)} %tile.26.speeds, f32[8,128]{1,0:T(8,128)S(1)} %copy-done.10, ...), custom_call_target="tpu_custom_call" | custom-call | flops 100000000 | bytes 8388608 | tf_op jit(solution)/shard_map/levels/pallas_call | solution.py:541
  56.4 1.0 copy-done.2
  57.3 7.5 %all-to-all-done.in_ref = f32[16,16,8,128]{3,2,1,0:T(8,128)} async-done(((f32[16,16,8,128]{3,2,1,0:T(8,128)}), f32[16,16,8,128]{3,2,1,0:T(8,128)}, u32[]{:S(2)}, u32[]{:S(2)}) %all-to-all-start) | async-done | bytes 1048608 | tf_op jit(solution)/shard_map/all_to_all | solution.py:644
  64.8 4.4 %all-to-all-start.3 = ((f32[16,16,8,128]{3,2,1,0:T(8,128)}), f32[16,16,8,128]{3,2,1,0:T(8,128)S(1)}, u32[]{:S(2)}, u32[]{:S(2)}) async-start(f32[16,16,8,128]{3,2,1,0:T(8,128)} %copy-done.2), calls=%async_computation.3 | async-start | bytes 2097152 | tf_op jit(solution)/shard_map/all_to_all | solution.py:644
  69.2 2.3 %join.2.own = f32[8,2,16,8,128]{4,3,2,1,0:T(8,128)} custom-call(f32[16,16,8,128]{3,2,1,0:T(8,128)} %all-to-all-done.in_ref), custom_call_target="tpu_custom_call" | custom-call | flops 1000000 | bytes 2097152 | tf_op jit(solution)/shard_map/join/pallas_call | solution.py:363
  71.6 0.1 tile.24.speeds
  71.6 2.9 %collective-permute-done.other = f32[8,2,16,8,128]{4,3,2,1,0:T(8,128)} collective-permute-done((f32[8,2,16,8,128]{4,3,2,1,0:T(8,128)}, f32[8,2,16,8,128]{4,3,2,1,0:T(8,128)}, u32[]{:S(2)}, u32[]{:S(2)}) %collective-permute-start) | collective-permute-done | bytes 1048608 | tf_op jit(solution)/shard_map/ppermute | solution.py:20
  74.5 12.0 %levels.2 = f32[16,16,8,128]{3,2,1,0:T(8,128)S(1)} custom-call(s32[2]{0:T(128)S(1)} %pad_add_fusion.ids, f32[496]{0:T(512)S(1)} %copy-done.11, f32[8,2,16,8,128]{4,3,2,1,0:T(8,128)} %join.2.own, f32[8,2,16,8,128]{4,3,2,1,0:T(8,128)} %collective-permute-done.other, f32[31,128]{1,0:T(8,128)S(1)} %tile.24.speeds, f32[8,128]{1,0:T(8,128)S(1)} %copy-done.10, ...), custom_call_target="tpu_custom_call" | custom-call | flops 100000000 | bytes 8388608 | tf_op jit(solution)/shard_map/levels/pallas_call | solution.py:541
  86.6 1.0 copy-done.3
  87.6 6.0 %all-to-all-done.3.refs_0_ = f32[16,16,8,128]{3,2,1,0:T(8,128)S(1)} async-done(((f32[16,16,8,128]{3,2,1,0:T(8,128)}), f32[16,16,8,128]{3,2,1,0:T(8,128)S(1)}, u32[]{:S(2)}, u32[]{:S(2)}) %all-to-all-start.3) | async-done | bytes 1048608 | tf_op jit(solution)/shard_map/all_to_all | solution.py:644
  93.6 4.4 %all-to-all-start.1 = ((f32[16,16,8,128]{3,2,1,0:T(8,128)}), f32[16,16,8,128]{3,2,1,0:T(8,128)S(1)}, u32[]{:S(2)}, u32[]{:S(2)}) async-start(f32[16,16,8,128]{3,2,1,0:T(8,128)} %copy-done.3), calls=%async_computation.1 | async-start | bytes 2097152 | tf_op jit(solution)/shard_map/all_to_all | solution.py:644
  98.0 2.3 %unpack.2.refs_1_ = f32[2,16,16,1024]{3,2,1,0:T(8,128)} custom-call(f32[16,16,8,128]{3,2,1,0:T(8,128)S(1)} %all-to-all-done.3.refs_0_), custom_call_target="tpu_custom_call" | custom-call | flops 1000000 | bytes 2097152 | tf_op jit(solution)/shard_map/unpack/pallas_call | solution.py:585
  100.3 22.1 %all-to-all-done.1.refs_0_ = f32[16,16,8,128]{3,2,1,0:T(8,128)S(1)} async-done(((f32[16,16,8,128]{3,2,1,0:T(8,128)}), f32[16,16,8,128]{3,2,1,0:T(8,128)S(1)}, u32[]{:S(2)}, u32[]{:S(2)}) %all-to-all-start.1) | async-done | bytes 1048608 | tf_op jit(solution)/shard_map/all_to_all | solution.py:644
  122.4 2.2 %unpack.3 = f32[2,16,16,1024]{3,2,1,0:T(8,128)} custom-call(f32[16,16,8,128]{3,2,1,0:T(8,128)S(1)} %all-to-all-done.1.refs_0_, f32[2,16,16,1024]{3,2,1,0:T(8,128)} %unpack.2.refs_1_), custom_call_target="tpu_custom_call", output_to_operand_aliasing={{}: (1, {})} | custom-call | flops 1000000 | bytes 2097152 | tf_op jit(solution)/shard_map/unpack/pallas_call | solution.py:585
  (40 shorter events, 0.2 us)
Async XLA Ops:
  0.0 42.3 %copy-start = (f32[4,4]{1,0:T(4,128)S(1)}, f32[4,4]{1,0:T(4,128)}, u32[]{:S(2)}) copy-start(f32[4,4]{1,0:T(4,128)} %param.20) | copy-start | bytes 196
  2.8 33.1 %all-to-all-start.2 = ((f32[16,16,8,128]{3,2,1,0:T(8,128)}), f32[16,16,8,128]{3,2,1,0:T(8,128)S(1)}, u32[]{:S(2)}, u32[]{:S(2)}) async-start(f32[16,16,8,128]{3,2,1,0:T(8,128)} %pack.3), calls=%async_computation.2 | async-start | bytes 2097152 | tf_op jit(solution)/shard_map/all_to_all | solution.py:644
  10.0 34.5 %copy-start.7 = (f32[2,4,8,128]{3,2,1,0:T(8,128)S(1)}, f32[2,4,8,128]{3,2,1,0:T(8,128)}, u32[]{:S(2)}) copy-start(f32[2,4,8,128]{3,2,1,0:T(8,128)} %constant.77.clone.last_lengths) | copy-start | bytes 98308
  10.0 34.5 %copy-start.8 = (f32[4,8,128]{2,1,0:T(8,128)S(1)}, f32[4,8,128]{2,1,0:T(8,128)}, u32[]{:S(2)}) copy-start(f32[4,8,128]{2,1,0:T(8,128)} %constant.76.clone.last_two) | copy-start | bytes 49156
  10.0 34.5 %copy-start.11 = (f32[496]{0:T(512)S(1)}, f32[496]{0:T(512)}, u32[]{:S(2)}) copy-start(f32[496]{0:T(512)} %constant.72.clone.nodes) | copy-start | bytes 5956
  12.9 29.2 %copy-start.12 = (f32[31]{0:T(128)S(1)}, f32[31]{0:T(128)}, u32[]{:S(2)}) copy-start(f32[31]{0:T(128)} %constant.82) | copy-start | bytes 376
  12.9 29.2 %copy-start.13 = (f32[31]{0:T(128)S(1)}, f32[31]{0:T(128)}, u32[]{:S(2)}) copy-start(f32[31]{0:T(128)} %constant.71.clone) | copy-start | bytes 376
  12.9 31.7 %copy-start.1 = (f32[496,8,128]{2,1,0:T(8,128)S(1)}, f32[496,8,128]{2,1,0:T(8,128)}, u32[]{:S(2)}) copy-start(f32[496,8,128]{2,1,0:T(8,128)} %constant.74.clone.lengths) | copy-start | bytes 6094852
  12.9 31.7 %copy-start.6 = (bf16[256,256]{1,0:T(8,128)(2,1)S(1)}, bf16[256,256]{1,0:T(8,128)(2,1)}, u32[]{:S(2)}) copy-start(bf16[256,256]{1,0:T(8,128)(2,1)} %constant.78.clone.first_table) | copy-start | bytes 393220
  12.9 31.7 %copy-start.9 = (f32[2,8,128]{2,1,0:T(8,128)S(1)}, f32[2,8,128]{2,1,0:T(8,128)}, u32[]{:S(2)}) copy-start(f32[2,8,128]{2,1,0:T(8,128)} %constant.75.clone.last_one) | copy-start | bytes 24580
  12.9 31.7 %copy-start.10 = (f32[8,128]{1,0:T(8,128)S(1)}, f32[8,128]{1,0:T(8,128)}, u32[]{:S(2)}) copy-start(f32[8,128]{1,0:T(8,128)} %constant.73.clone.waves) | copy-start | bytes 12292
  35.9 4.4 %copy-start.4 = (f32[16,16,8,128]{3,2,1,0:T(8,128)}, f32[16,16,8,128]{3,2,1,0:T(8,128)S(1)}, u32[]{:S(2)}) copy-start(f32[16,16,8,128]{3,2,1,0:T(8,128)S(1)} %all-to-all-done.2.in_ref) | copy-start | bytes 3145732
  35.9 28.9 %all-to-all-start = ((f32[16,16,8,128]{3,2,1,0:T(8,128)}), f32[16,16,8,128]{3,2,1,0:T(8,128)}, u32[]{:S(2)}, u32[]{:S(2)}) async-start(f32[16,16,8,128]{3,2,1,0:T(8,128)} %pack.2), calls=%async_computation | async-start | bytes 2097152 | tf_op jit(solution)/shard_map/all_to_all | solution.py:644
  40.4 1.2 copy-start.5
  41.7 2.9 %collective-permute-start.1 = (f32[8,2,16,8,128]{4,3,2,1,0:T(8,128)S(1)}, f32[8,2,16,8,128]{4,3,2,1,0:T(8,128)}, u32[]{:S(2)}, u32[]{:S(2)}) collective-permute-start(f32[8,2,16,8,128]{4,3,2,1,0:T(8,128)S(1)} %join.3.own), channel_id=1, source_target_pairs={{0,1},{1,0},{2,3},{3,2},{4,5},{5,4},{6,7},{7,6},{8,9},{9,8},{10,11... | collective-permute-start | bytes 3145736 | tf_op jit(solution)/shard_map/ppermute | solution.py:20
  56.4 1.0 copy-start.2
  64.8 28.8 %all-to-all-start.3 = ((f32[16,16,8,128]{3,2,1,0:T(8,128)}), f32[16,16,8,128]{3,2,1,0:T(8,128)S(1)}, u32[]{:S(2)}, u32[]{:S(2)}) async-start(f32[16,16,8,128]{3,2,1,0:T(8,128)} %copy-done.2), calls=%async_computation.3 | async-start | bytes 2097152 | tf_op jit(solution)/shard_map/all_to_all | solution.py:644
  71.5 3.0 %collective-permute-start = (f32[8,2,16,8,128]{4,3,2,1,0:T(8,128)}, f32[8,2,16,8,128]{4,3,2,1,0:T(8,128)}, u32[]{:S(2)}, u32[]{:S(2)}) collective-permute-start(f32[8,2,16,8,128]{4,3,2,1,0:T(8,128)} %join.2.own), channel_id=1, source_target_pairs={{0,1},{1,0},{2,3},{3,2},{4,5},{5,4},{6,7},{7,6},{8,9},{9,8},{10,11... | collective-permute-start | bytes 3145736 | tf_op jit(solution)/shard_map/ppermute | solution.py:20
  86.6 1.0 copy-start.3
  93.6 28.8 %all-to-all-start.1 = ((f32[16,16,8,128]{3,2,1,0:T(8,128)}), f32[16,16,8,128]{3,2,1,0:T(8,128)S(1)}, u32[]{:S(2)}, u32[]{:S(2)}) async-start(f32[16,16,8,128]{3,2,1,0:T(8,128)} %copy-done.3), calls=%async_computation.1 | async-start | bytes 2097152 | tf_op jit(solution)/shard_map/all_to_all | solution.py:644
